TPU v7x, 256 devices: a whole 4x4x8 slice. The times are simulated.
256 devices in a mesh: flow: 16 (over x_lo, z), trans: 16 (over y, x_hi, core).
Axes of the slice: x: 4 (x_hi: 2, x_lo: 2; x = x_hi * 2 + x_lo), y: 4, z: 8, core: 2. Of those that a mesh axis runs over, the one named last changes fastest.
Arguments:
- populations: float32 [19, 384, 256, 256], P(None, 'flow', 'trans'), may hold values from 0.016666667 to 0.46666667, as said below
- magnetization: float32 [2, 2, 384, 256, 256], P(None, None, 'flow', 'trans'), may hold values from -6 to 6
- pore: int32 [384, 256, 256], P('flow', 'trans'), may hold values 0 or 1
- wall: int32 [384, 256, 256], P('flow', 'trans'), may hold values 0 or 1
Outputs:
- velocity: float32 [3, 384, 256, 256], P(None, 'flow', 'trans')
- new_magnetization: float32 [2, 2, 384, 256, 256], P(None, None, 'flow', 'trans')
- signal: float32 [2, 2], replicated
Inputs may be any that keep to these rules, and one draw needn't show every extreme that they name: `populations`: population i is its lattice weight times a factor between 0.6 and 1.4.
All inputs are finite; a program needn't handle non-finite values. No bound on the sum of `pore` or of `wall` on one device may be relied on, other than what follows from the above.
Results may differ from a plain program's by a relative error of at most 0.000025.
Values sent between devices are 32-bit elements; how exact they have to be, the bound alone decides.
No kernel may reach another device: no remote copies, remote signals or barrier semaphores. Data moves between devices by JAX's collectives and lax.ppermute only.
A program may use at most 128 MiB of HBM per device.

v0:
```python
import math

import jax
import jax.numpy as jnp
from jax import lax
from jax.sharding import PartitionSpec as P

Q_LOW = 2
Q_HIGH = 5


VELOCITIES = (
    (0, 0, 0),
    (1, 0, 0),
    (-1, 0, 0),
    (0, 1, 0),
    (0, -1, 0),
    (0, 0, 1),
    (0, 0, -1),
    (1, 1, 0),
    (-1, -1, 0),
    (1, -1, 0),
    (-1, 1, 0),
    (1, 0, 1),
    (-1, 0, -1),
    (1, 0, -1),
    (-1, 0, 1),
    (0, 1, 1),
    (0, -1, -1),
    (0, 1, -1),
    (0, -1, 1),
)
WEIGHTS = (1.0 / 3.0,) + (1.0 / 18.0,) * 6 + (1.0 / 36.0,) * 12
OPPOSITE = (0, 2, 1, 4, 3, 6, 5, 8, 7, 10, 9, 12, 11, 14, 13, 16, 15, 18, 17)
relax_time = 1.25
body_force = 0.002
diffusion_step = 0.1
surface_relax = 0.4


def padded_2(cells, sides, width):
    for axis, dim in sides:
        count = lax.axis_size(axis)
        head = lax.slice_in_dim(cells, 0, width, axis=dim)
        tail = lax.slice_in_dim(cells, cells.shape[dim] - width, cells.shape[dim], axis=dim)
        cells = jnp.concatenate(
            [
                lax.ppermute(tail, axis, [(i, (i + 1) % count) for i in range(count)]),
                cells,
                lax.ppermute(head, axis, [((i + 1) % count, i) for i in range(count)]),
            ],
            axis=dim,
        )
    return cells


def add_moments(totals, shifted, pop_index):
    step_z, step_y, step_x = VELOCITIES[pop_index]
    density, mom_z, mom_y, mom_x = totals
    return (
        density + shifted,
        mom_z + step_z * shifted,
        mom_y + step_y * shifted,
        mom_x + step_x * shifted,
    )


def moments(pops_in):
    zeros_grid = jnp.zeros_like(pops_in[0])
    totals = (zeros_grid, zeros_grid, zeros_grid, zeros_grid)
    for pop_index in range(19):
        totals = add_moments(totals, pops_in[pop_index], pop_index)
    return totals


def collide_one(pops_in, pop_index, density, vel_z, vel_y, vel_x, speed_sq, pore_f):
    step_z, step_y, step_x = VELOCITIES[pop_index]
    dotted = step_z * vel_z + step_y * vel_y + step_x * vel_x
    equilibrium = (
        WEIGHTS[pop_index] * density * (1.0 + 3.0 * dotted + 4.5 * dotted * dotted - 1.5 * speed_sq)
    )
    relaxed = pops_in[pop_index] - (pops_in[pop_index] - equilibrium) / relax_time
    return jnp.where(pore_f > 0.5, relaxed, pops_in[OPPOSITE[pop_index]])


def collide(pops_in, pore_f):
    density, mom_z, mom_y, mom_x = moments(pops_in)
    vel_z = mom_z / density + relax_time * body_force
    vel_y = mom_y / density
    vel_x = mom_x / density
    speed_sq = vel_z * vel_z + vel_y * vel_y + vel_x * vel_x
    return jnp.stack(
        [
            collide_one(pops_in, pop_index, density, vel_z, vel_y, vel_x, speed_sq, pore_f)
            for pop_index in range(19)
        ]
    )


def stream_moments(padded, pore_f, depth, width):
    zeros_grid = jnp.zeros_like(pore_f)
    totals = (zeros_grid, zeros_grid, zeros_grid, zeros_grid)
    for pop_index in range(19):
        step_z, step_y, step_x = VELOCITIES[pop_index]
        shifted = padded[
            pop_index, 1 - step_z : 1 - step_z + depth, 1 - step_y : 1 - step_y + width
        ]
        if step_x != 0:
            shifted = jnp.roll(shifted, step_x, axis=2)
        totals = add_moments(totals, shifted, pop_index)
    new_density, mom_z, mom_y, mom_x = totals
    return pore_f * jnp.stack([mom_z, mom_y, mom_x]) / new_density


def phase_tables(coords_int, extent):
    coords = coords_int.astype(jnp.float32)
    wave_numbers = jnp.array([Q_LOW, Q_HIGH], jnp.float32)
    angles = 2.0 * math.pi * wave_numbers[:, None] * coords[None, :] / extent
    return (jnp.cos(angles)[:, :, None, None], jnp.sin(angles)[:, :, None, None])


def torrey_step(extended, vel, pore_f, wall_f, cos_z, sin_z):
    center = extended[:, :, 1:-1, 1:-1]
    plus_z = extended[:, :, 2:, 1:-1]
    minus_z = extended[:, :, :-2, 1:-1]
    plus_y = extended[:, :, 1:-1, 2:]
    minus_y = extended[:, :, 1:-1, :-2]
    plus_x = jnp.roll(center, -1, axis=4)
    minus_x = jnp.roll(center, 1, axis=4)
    laplace = plus_z + minus_z + plus_y + minus_y + plus_x + minus_x - 6.0 * center
    advect = 0.5 * (
        vel[0] * (plus_z - minus_z) + vel[1] * (plus_y - minus_y) + vel[2] * (plus_x - minus_x)
    )
    updated = center + diffusion_step * laplace - advect - surface_relax * wall_f * center
    real_part = updated[:, 0]
    imag_part = updated[:, 1]
    rot_real = real_part * cos_z + imag_part * sin_z
    rot_imag = imag_part * cos_z - real_part * sin_z
    return jnp.stack([rot_real, rot_imag], axis=1) * pore_f


def local(populations, magnetization, pore, wall):
    pore_f = pore.astype(jnp.float32)
    wall_f = wall.astype(jnp.float32)
    depth_z = populations.shape[1]
    width_y = populations.shape[2]
    width_x = populations.shape[3]
    relaxed_pops = collide(populations, pore_f)
    padded = padded_2(relaxed_pops, (("flow", 1), ("trans", 2)), 1)
    velocity = stream_moments(padded, pore_f, depth_z, width_y)
    flow_count = lax.axis_size("flow")
    trans_count = lax.axis_size("trans")
    extent = depth_z * flow_count
    start_z = lax.axis_index("flow") * depth_z
    cos_z, sin_z = phase_tables(start_z + jnp.arange(depth_z, dtype=jnp.int32), extent)
    magnet = magnetization
    for sweep in range(2):
        extended = padded_2(magnet, (("flow", 2), ("trans", 3)), 1)
        magnet = torrey_step(extended, velocity, pore_f, wall_f, cos_z, sin_z)
    local_sums = jnp.sum(magnet, axis=(2, 3, 4))
    totals = lax.psum(local_sums, ("flow", "trans"))
    signal = totals / math.sqrt(extent * width_y * trans_count * width_x)
    return (velocity, magnet, signal)


def solution(mesh):
    placed = (
        P(None, "flow", "trans", None),
        P(None, None, "flow", "trans", None),
        P("flow", "trans", None),
        P("flow", "trans", None),
    )
    return jax.shard_map(
        local,
        mesh=mesh,
        in_specs=placed,
        out_specs=(P(None, "flow", "trans", None), P(None, None, "flow", "trans", None), P()),
        check_vma=False,
    )
```

profile of v0, /device:TPU:1, one launch (start us, length us, event | category | flops | bytes accessed | tf_op | source)
XLA Modules:
  0.0 159.6 jit_solution(12641586650482388543)
XLA Ops:
  0.6 4.4 %bitcast_dynamic-update-slice_fusion.2 = (f32[19,24,16,256]{3,2,1,0:T(8,128)S(1)}, f32[24,16,256]{2,1,0:T(8,128)S(1)}, f32[24,16,256]{2,1,0:T(8,128)S(1)}, f32[2...) fusion(f32[19,24,16,256]{3,2,1,0:T(8,128)} %param.5, ...), kind=kLoop, calls=%fused_computation.255 | loop fusion | flops 12779519 | bytes 10715136
  5.0 1.2 copy-done.1
  6.2 0.3 fusion.14
  6.5 0.3 fusion.23
  6.9 0.3 fusion.32
  7.2 0.3 fusion.41
  7.6 0.3 bitcast_dynamic-update-slice_fusion.1
  7.9 0.3 bitcast_dynamic-update-slice_fusion
  8.6 0.3 fusion.73
  8.9 0.3 fusion.82
  9.3 0.3 fusion.91
  10.0 0.3 fusion.109
  10.3 0.3 fusion.118
  10.7 0.3 fusion.127
  11.4 0.3 fusion.145
  11.7 0.3 fusion.154
  12.1 0.3 fusion.163
  12.4 0.9 fusion.215
  13.3 2.5 %collective-permute-start = (f32[19,1,16,256]{3,2,1,0:T(8,128)}, f32[19,1,16,256]{3,2,1,0:T(8,128)S(1)}, u32[]{:S(2)}, u32[]{:S(2)}) collective-permute-start(f32[19,1,16,256]{3,2,1,0:T(8,128)} %get-tuple-element.43), channel_id=1, source_target_pairs={{0,16},{16,32},{32,48},{48,64},{64,80},{80,96},{96,112},{112,128},... | collective-permute-start | bytes 933896 | tf_op jit(solution)/shard_map/ppermute | solution.py:48
  15.7 4.9 %collective-permute-start.1 = (f32[19,1,16,256]{3,2,1,0:T(8,128)}, f32[19,1,16,256]{3,2,1,0:T(8,128)S(1)}, u32[]{:S(2)}, u32[]{:S(2)}) collective-permute-start(f32[19,1,16,256]{3,2,1,0:T(8,128)} %get-tuple-element.44), channel_id=1, source_target_pairs={{16,0},{32,16},{48,32},{64,48},{80,64},{96,80},{112,96},{128,112},... | collective-permute-start | bytes 933896 | tf_op jit(solution)/shard_map/ppermute | solution.py:50
  20.6 0.7 copy.8
  21.3 1.6 %collective-permute-start.4 = (f32[2,2,1,16,256]{4,2,3,1,0:T(1,128)}, f32[2,2,1,16,256]{4,2,3,1,0:T(1,128)S(1)}, u32[]{:S(2)}, u32[]{:S(2)}) collective-permute-start(f32[2,2,1,16,256]{4,2,3,1,0:T(1,128)} %copy.8), channel_id=1, source_target_pairs={{16,0},{32,16},{48,32},{64,48},{80,64},{96,80},{112,96},{128,112},... | collective-permute-start | bytes 196616 | tf_op jit(solution)/shard_map/ppermute | solution.py:50
  22.9 0.7 copy.10
  23.6 0.9 copy.18
  24.5 2.3 %fusion.220 = (f32[2,2,24,16,255]{4,2,3,1,0:T(8,128)}, f32[2,2,24,16,255]{4,2,3,1,0:T(8,128)}) fusion(f32[2,2,24,16,256]{4,2,3,1,0:T(8,128)S(1)} %copy.18), kind=kLoop, calls=%fused_computation.390 | loop fusion | bytes 6266880 | tf_op jit(solution)/shard_map/jit(_roll_static)/slice | solution.py:128
  26.8 0.8 convert_multiply_fusion
  27.9 3.8 %pad_maximum_fusion.22 = (f32[19,26,1,256]{3,2,1,0:T(1,128)S(1)}, f32[19,26,1,256]{3,2,1,0:T(1,128)S(1)}) fusion(f32[19,1,16,256]{3,2,1,0:T(8,128)S(1)} %collective-permute-done.1, f32[19,24,16,256]{3,2,1,0:T(8,128)} %copy-done, f32[19,1,16,256]{3,2,1,0:T(8,128)S(1)} %collective-permute-done), kind=kLoop, calls=%fused_computation.52 | loop fusion | flops 505856 | bytes 9105408 | tf_op jit(solution)/shard_map/slice | solution.py:45
  31.8 3.8 %collective-permute-start.2 = (f32[19,26,1,256]{3,2,1,0:T(1,128)S(1)}, f32[19,26,1,256]{3,2,1,0:T(1,128)S(1)}, u32[]{:S(2)}, u32[]{:S(2)}) collective-permute-start(f32[19,26,1,256]{3,2,1,0:T(1,128)S(1)} %get-tuple-element.35), channel_id=1, source_target_pairs={{0,1},{1,2},{2,3},{3,4},{4,5},{5,6},{6,7},{7,8},{8,9},{9,10},{10,1... | collective-permute-start | bytes 1517576 | tf_op jit(solution)/shard_map/ppermute | solution.py:48
  36.6 3.1 %collective-permute-start.6 = (f32[2,2,26,1,256]{4,2,3,1,0:T(8,128)S(1)}, f32[2,2,26,1,256]{4,2,3,1,0:T(8,128)S(1)}, u32[]{:S(2)}, u32[]{:S(2)}) collective-permute-start(f32[2,2,26,1,256]{4,2,3,1,0:T(8,128)S(1)} %get-tuple-element.47), channel_id=1, source_target_pairs={{1,0},{2,1},{3,2},{4,3},{5,4},{6,5},{7,6},{8,7},{9,8},{10,9},{11,1... | collective-permute-start | bytes 319496 | tf_op jit(solution)/shard_map/ppermute | solution.py:50
  40.8 2.9 %collective-permute-done.2 = f32[19,26,1,256]{3,2,1,0:T(1,128)S(1)} collective-permute-done((f32[19,26,1,256]{3,2,1,0:T(1,128)S(1)}, f32[19,26,1,256]{3,2,1,0:T(1,128)S(1)}, u32[]{:S(2)}, u32[]{:S(2)}) %collective-permute-start.2) | collective-permute-done | bytes 505888 | tf_op jit(solution)/shard_map/ppermute | solution.py:48
  43.7 6.7 %collective-permute-done.3 = f32[19,26,1,256]{3,2,1,0:T(1,128)S(1)} collective-permute-done((f32[19,26,1,256]{3,2,1,0:T(1,128)S(1)}, f32[19,26,1,256]{3,2,1,0:T(1,128)S(1)}, u32[]{:S(2)}, u32[]{:S(2)}) %collective-permute-start.3) | collective-permute-done | bytes 505888 | tf_op jit(solution)/shard_map/ppermute | solution.py:50
  51.2 1.2 add_add_fusion
  52.4 1.1 add_bitcast_fusion.2
  53.5 1.1 add_bitcast_fusion.1
  54.6 1.1 add_bitcast_fusion
  56.3 0.7 copy-done.4
  57.8 0.5 copy-done.2
  58.3 2.8 %multiply_subtract_fusion.1 = f32[2,2,24,16,256]{4,2,3,1,0:T(8,128)S(1)} fusion(f32[2,2,24,16,256]{4,2,3,1,0:T(8,128)S(1)} %copy.18, f32[2,2,24,16,255]{4,2,3,1,0:T(8,128)S(1)} %copy-done.3, f32[2,2,24,16,1]{4,2,3,1,0:T(8,128)S(1)} %get-tuple-element.64, f32[2,2,24,16,1]{4,2,3,1,0:T(8,128)S(1)} %get-tuple-element.63, ...), kind=kLoop, calls=%fused_computation.23 | loop fusion | flops 12189696 | bytes 8208384 | tf_op jit(solution)/shard_map/sub | solution.py:134
  61.6 4.3 %collective-permute-start.8 = (f32[2,2,1,16,256]{4,2,3,1,0:T(1,128)S(1)}, f32[2,2,1,16,256]{4,2,3,1,0:T(1,128)S(1)}, u32[]{:S(2)}, u32[]{:S(2)}) collective-permute-start(f32[2,2,1,16,256]{4,2,3,1,0:T(1,128)S(1)} %get-tuple-element.54), channel_id=1, source_target_pairs={{16,0},{32,16},{48,32},{64,48},{80,64},{96,80},{112,96},{128,112},... | collective-permute-start | bytes 196616 | tf_op jit(solution)/shard_map/ppermute | solution.py:50
  65.8 0.5 fusion.217
  66.4 0.8 collective-permute-done.8
  67.2 3.9 %collective-permute-done.9 = f32[2,2,1,16,256]{4,2,3,1,0:T(1,128)S(1)} collective-permute-done((f32[2,2,1,16,256]{4,2,3,1,0:T(1,128)S(1)}, f32[2,2,1,16,256]{4,2,3,1,0:T(1,128)S(1)}, u32[]{:S(2)}, u32[]{:S(2)}) %collective-permute-start.9) | collective-permute-done | bytes 65568 | tf_op jit(solution)/shard_map/ppermute | solution.py:48
  71.2 3.2 %collective-permute-start.11 = (f32[2,2,26,1,256]{4,2,3,1,0:T(8,128)S(1)}, f32[2,2,26,1,256]{4,2,3,1,0:T(8,128)S(1)}, u32[]{:S(2)}, u32[]{:S(2)}) collective-permute-start(f32[2,2,26,1,256]{4,2,3,1,0:T(8,128)S(1)} %get-tuple-element.46), channel_id=1, source_target_pairs={{0,1},{1,2},{2,3},{3,4},{4,5},{5,6},{6,7},{7,8},{8,9},{9,10},{10,1... | collective-permute-start | bytes 319496 | tf_op jit(solution)/shard_map/ppermute | solution.py:48
  74.7 2.4 %collective-permute-done.10 = f32[2,2,26,1,256]{4,2,3,1,0:T(8,128)S(1)} collective-permute-done((f32[2,2,26,1,256]{4,2,3,1,0:T(8,128)S(1)}, f32[2,2,26,1,256]{4,2,3,1,0:T(8,128)S(1)}, u32[]{:S(2)}, u32[]{:S(2)}) %collective-permute-start.10) | collective-permute-done | bytes 106528 | tf_op jit(solution)/shard_map/ppermute | solution.py:50
  77.1 2.8 %multiply_subtract_fusion = f32[2,2,24,16,256]{4,2,3,1,0:T(8,128)S(1)} fusion(f32[2,2,24,16,256]{4,2,3,1,0:T(8,128)S(1)} %maximum_multiply_fusion, f32[2,2,24,16,255]{4,2,3,1,0:T(8,128)S(1)} %get-tuple-element.56, f32[2,2,24,16,1]{4,2,3,1,0:T(8,128)S(1)} %get-tuple-element.58, f32[2,2,24,16,1]{4,2,3,1,0:T(8,128)S(1)} %get-tuple-element.57, ...), kind=kLoop, calls=%fused_computation.22 | loop fusion | flops 12189696 | bytes 8208384 | tf_op jit(solution)/shard_map/sub | solution.py:134
  80.5 1.6 %copy.25 = f32[2,2,24,16,256]{4,3,2,1,0:T(8,128)} copy(f32[2,2,24,16,256]{4,2,3,1,0:T(8,128)S(1)} %get-tuple-element.7) | data formatting | bytes 3145728
  82.1 76.9 %psum.7 = f32[2,2]{1,0:T(2,128)S(1)} all-reduce(f32[2,2]{1,0:T(2,128)S(1)} %get-tuple-element.6), channel_id=1, replica_groups=mesh['flow'=16,'trans'=16] {'flow','trans'}, use_global_device_ids=true, to_apply=%region_1.2 | all-reduce | flops 4 | bytes 32 | tf_op jit(solution)/shard_map/psum | solution.py:161
  159.0 0.6 broadcast_multiply_fusion.1
  (74 shorter events, 7.0 us)
Async XLA Ops:
  0.6 5.5 %copy-start.1 = (f32[19,24,16,256]{3,2,1,0:T(8,128)S(1)}, f32[19,24,16,256]{3,2,1,0:T(8,128)}, u32[]{:S(2)}) copy-start(f32[19,24,16,256]{3,2,1,0:T(8,128)} %param.5) | copy-start | bytes 22413316
  12.0 8.6 %copy-start.5 = (f32[2,2,24,16,256]{4,3,2,1,0:T(8,128)S(1)}, f32[2,2,24,16,256]{4,3,2,1,0:T(8,128)}, u32[]{:S(2)}) copy-start(f32[2,2,24,16,256]{4,3,2,1,0:T(8,128)} %param.6) | copy-start | bytes 4718596
  12.4 14.4 %copy-start = (f32[19,24,16,256]{3,2,1,0:T(8,128)}, f32[19,24,16,256]{3,2,1,0:T(8,128)S(1)}, u32[]{:S(2)}) copy-start(f32[19,24,16,256]{3,2,1,0:T(8,128)S(1)} %fusion.163) | copy-start | bytes 22413316
  13.3 14.6 %collective-permute-start = (f32[19,1,16,256]{3,2,1,0:T(8,128)}, f32[19,1,16,256]{3,2,1,0:T(8,128)S(1)}, u32[]{:S(2)}, u32[]{:S(2)}) collective-permute-start(f32[19,1,16,256]{3,2,1,0:T(8,128)} %get-tuple-element.43), channel_id=1, source_target_pairs={{0,16},{16,32},{32,48},{48,64},{64,80},{80,96},{96,112},{112,128},... | collective-permute-start | bytes 933896 | tf_op jit(solution)/shard_map/ppermute | solution.py:48
  15.7 12.2 %collective-permute-start.1 = (f32[19,1,16,256]{3,2,1,0:T(8,128)}, f32[19,1,16,256]{3,2,1,0:T(8,128)S(1)}, u32[]{:S(2)}, u32[]{:S(2)}) collective-permute-start(f32[19,1,16,256]{3,2,1,0:T(8,128)} %get-tuple-element.44), channel_id=1, source_target_pairs={{16,0},{32,16},{48,32},{64,48},{80,64},{96,80},{112,96},{128,112},... | collective-permute-start | bytes 933896 | tf_op jit(solution)/shard_map/ppermute | solution.py:50
  21.3 15.2 %collective-permute-start.4 = (f32[2,2,1,16,256]{4,2,3,1,0:T(1,128)}, f32[2,2,1,16,256]{4,2,3,1,0:T(1,128)S(1)}, u32[]{:S(2)}, u32[]{:S(2)}) collective-permute-start(f32[2,2,1,16,256]{4,2,3,1,0:T(1,128)} %copy.8), channel_id=1, source_target_pairs={{16,0},{32,16},{48,32},{64,48},{80,64},{96,80},{112,96},{128,112},... | collective-permute-start | bytes 196616 | tf_op jit(solution)/shard_map/ppermute | solution.py:50
  23.6 13.0 %collective-permute-start.5 = (f32[2,2,1,16,256]{4,2,3,1,0:T(1,128)}, f32[2,2,1,16,256]{4,2,3,1,0:T(1,128)S(1)}, u32[]{:S(2)}, u32[]{:S(2)}) collective-permute-start(f32[2,2,1,16,256]{4,2,3,1,0:T(1,128)} %copy.10), channel_id=1, source_target_pairs={{0,16},{16,32},{32,48},{48,64},{64,80},{80,96},{96,112},{112,128},... | collective-permute-start | bytes 196616 | tf_op jit(solution)/shard_map/ppermute | solution.py:48
  24.5 2.3 %copy-start.8 = (s32[24,16,256]{2,1,0:T(8,128)S(1)}, s32[24,16,256]{2,1,0:T(8,128)}, u32[]{:S(2)}) copy-start(s32[24,16,256]{2,1,0:T(8,128)} %param.8) | copy-start | bytes 1179652
  27.6 12.4 %slice-start = ((s8[7471104]{0:T(1024)(128)(4,1)}), s8[4194304]{0:T(1024)(128)(4,1)S(1)}, s32[]{:S(2)}) async-start(s8[7471104]{0:T(1024)(128)(4,1)} %bitcast.553), calls=%async_computation | async-start | bytes 8388608
  27.9 7.7 %copy-start.9 = (f32[2]{0:T(128)S(1)}, f32[2]{0:T(128)}, u32[]{:S(2)}) copy-start(f32[2]{0:T(128)} %constant.73) | copy-start | bytes 28
  27.9 8.0 %copy-start.7 = (s32[24,16,256]{2,1,0:T(8,128)S(1)}, s32[24,16,256]{2,1,0:T(8,128)}, u32[]{:S(2)}) copy-start(s32[24,16,256]{2,1,0:T(8,128)} %param.7) | copy-start | bytes 1179652
  27.9 12.1 %slice-start.1 = ((s8[7471104]{0:T(1024)(128)(4,1)}), s8[3276800]{0:T(1024)(128)(4,1)S(1)}, s32[]{:S(2)}) async-start(s8[7471104]{0:T(1024)(128)(4,1)} %bitcast.553), calls=%async_computation.1 | async-start | bytes 6553600
  31.8 4.3 %copy-start.6 = (f32[24,16,256]{2,1,0:T(8,128)S(1)}, f32[24,16,256]{2,1,0:T(8,128)}, u32[]{:S(2)}) copy-start(f32[24,16,256]{2,1,0:T(8,128)} %convert_multiply_fusion) | copy-start | bytes 1179652
  31.8 11.9 %collective-permute-start.2 = (f32[19,26,1,256]{3,2,1,0:T(1,128)S(1)}, f32[19,26,1,256]{3,2,1,0:T(1,128)S(1)}, u32[]{:S(2)}, u32[]{:S(2)}) collective-permute-start(f32[19,26,1,256]{3,2,1,0:T(1,128)S(1)} %get-tuple-element.35), channel_id=1, source_target_pairs={{0,1},{1,2},{2,3},{3,4},{4,5},{5,6},{6,7},{7,8},{8,9},{9,10},{10,1... | collective-permute-start | bytes 1517576 | tf_op jit(solution)/shard_map/ppermute | solution.py:48
  35.6 14.7 %collective-permute-start.3 = (f32[19,26,1,256]{3,2,1,0:T(1,128)S(1)}, f32[19,26,1,256]{3,2,1,0:T(1,128)S(1)}, u32[]{:S(2)}, u32[]{:S(2)}) collective-permute-start(f32[19,26,1,256]{3,2,1,0:T(1,128)S(1)} %get-tuple-element.36), channel_id=1, source_target_pairs={{1,0},{2,1},{3,2},{4,3},{5,4},{6,5},{7,6},{8,7},{9,8},{10,9},{11,1... | collective-permute-start | bytes 1517576 | tf_op jit(solution)/shard_map/ppermute | solution.py:50
  36.6 20.8 %collective-permute-start.6 = (f32[2,2,26,1,256]{4,2,3,1,0:T(8,128)S(1)}, f32[2,2,26,1,256]{4,2,3,1,0:T(8,128)S(1)}, u32[]{:S(2)}, u32[]{:S(2)}) collective-permute-start(f32[2,2,26,1,256]{4,2,3,1,0:T(8,128)S(1)} %get-tuple-element.47), channel_id=1, source_target_pairs={{1,0},{2,1},{3,2},{4,3},{5,4},{6,5},{7,6},{8,7},{9,8},{10,9},{11,1... | collective-permute-start | bytes 319496 | tf_op jit(solution)/shard_map/ppermute | solution.py:50
  39.7 17.7 %collective-permute-start.7 = (f32[2,2,26,1,256]{4,2,3,1,0:T(8,128)S(1)}, f32[2,2,26,1,256]{4,2,3,1,0:T(8,128)S(1)}, u32[]{:S(2)}, u32[]{:S(2)}) collective-permute-start(f32[2,2,26,1,256]{4,2,3,1,0:T(8,128)S(1)} %get-tuple-element.48), channel_id=1, source_target_pairs={{0,1},{1,2},{2,3},{3,4},{4,5},{5,6},{6,7},{7,8},{8,9},{9,10},{10,1... | collective-permute-start | bytes 319496 | tf_op jit(solution)/shard_map/ppermute | solution.py:48
  56.0 1.0 copy-start.4
  56.0 1.8 %copy-start.3 = (f32[2,2,24,16,255]{4,2,3,1,0:T(8,128)S(1)}, f32[2,2,24,16,255]{4,2,3,1,0:T(8,128)}, u32[]{:S(2)}) copy-start(f32[2,2,24,16,255]{4,2,3,1,0:T(8,128)} %get-tuple-element.62) | copy-start | bytes 4700164
  56.1 2.2 %copy-start.2 = (f32[2,2,24,16,255]{4,2,3,1,0:T(8,128)S(1)}, f32[2,2,24,16,255]{4,2,3,1,0:T(8,128)}, u32[]{:S(2)}) copy-start(f32[2,2,24,16,255]{4,2,3,1,0:T(8,128)} %get-tuple-element.61) | copy-start | bytes 4700164
  61.6 5.6 %collective-permute-start.8 = (f32[2,2,1,16,256]{4,2,3,1,0:T(1,128)S(1)}, f32[2,2,1,16,256]{4,2,3,1,0:T(1,128)S(1)}, u32[]{:S(2)}, u32[]{:S(2)}) collective-permute-start(f32[2,2,1,16,256]{4,2,3,1,0:T(1,128)S(1)} %get-tuple-element.54), channel_id=1, source_target_pairs={{16,0},{32,16},{48,32},{64,48},{80,64},{96,80},{112,96},{128,112},... | collective-permute-start | bytes 196616 | tf_op jit(solution)/shard_map/ppermute | solution.py:50
  65.8 5.2 %collective-permute-start.9 = (f32[2,2,1,16,256]{4,2,3,1,0:T(1,128)S(1)}, f32[2,2,1,16,256]{4,2,3,1,0:T(1,128)S(1)}, u32[]{:S(2)}, u32[]{:S(2)}) collective-permute-start(f32[2,2,1,16,256]{4,2,3,1,0:T(1,128)S(1)} %get-tuple-element.53), channel_id=1, source_target_pairs={{0,16},{16,32},{32,48},{48,64},{64,80},{80,96},{96,112},{112,128},... | collective-permute-start | bytes 196616 | tf_op jit(solution)/shard_map/ppermute | solution.py:48
  71.1 6.0 %collective-permute-start.10 = (f32[2,2,26,1,256]{4,2,3,1,0:T(8,128)S(1)}, f32[2,2,26,1,256]{4,2,3,1,0:T(8,128)S(1)}, u32[]{:S(2)}, u32[]{:S(2)}) collective-permute-start(f32[2,2,26,1,256]{4,2,3,1,0:T(8,128)S(1)} %get-tuple-element.45), channel_id=1, source_target_pairs={{1,0},{2,1},{3,2},{4,3},{5,4},{6,5},{7,6},{8,7},{9,8},{10,9},{11,1... | collective-permute-start | bytes 319496 | tf_op jit(solution)/shard_map/ppermute | solution.py:50
  71.2 5.9 %collective-permute-start.11 = (f32[2,2,26,1,256]{4,2,3,1,0:T(8,128)S(1)}, f32[2,2,26,1,256]{4,2,3,1,0:T(8,128)S(1)}, u32[]{:S(2)}, u32[]{:S(2)}) collective-permute-start(f32[2,2,26,1,256]{4,2,3,1,0:T(8,128)S(1)} %get-tuple-element.46), channel_id=1, source_target_pairs={{0,1},{1,2},{2,3},{3,4},{4,5},{5,6},{6,7},{7,8},{8,9},{9,10},{10,1... | collective-permute-start | bytes 319496 | tf_op jit(solution)/shard_map/ppermute | solution.py:48
where the time goes:
time: 160 us
  blocking collectives  76.9 us (48%)
  other arithmetic  27.5 us (17%)
  starting transfers between devices  23.7 us (15%)
  waiting for transfers between devices  16.6 us (10%)
  local copies, waits for them, and re-layouts  13.6 us (8%)
    psum x1, blocking collectives, local(): totals = lax.psum(local_sums, ('flow', 'trans'))  76.9 us
    ppermute x6, starting transfers between devices, padded_2(): lax.ppermute(head, axis, [((i + 1) % count, i) for i in range(count)])  13.9 us
    unnamed x19, other arithmetic  10.1 us
    ppermute x6, waiting for transfers between devices, padded_2(): lax.ppermute(head, axis, [((i + 1) % count, i) for i in range(count)])  9.83 us
    ppermute x6, starting transfers between devices, padded_2(): lax.ppermute(tail, axis, [(i, (i + 1) % count) for i in range(count)])  9.82 us
    ppermute x6, waiting for transfers between devices, padded_2(): lax.ppermute(tail, axis, [(i, (i + 1) % count) for i in range(count)])  6.77 us
    sub x2, other arithmetic, torrey_step(): center + diffusion_step * laplace - advect - surface_relax * wall_f * center  5.56 us
    unnamed x26, local copies, waits for them, and re-layouts  5.22 us
  transfers between devices with their start and end apart: 12, of which 5 were waited for; matrix products, arithmetic and copies ran while one was open for 11% of the time, Pallas kernels for 0%

commit v1 on v0

v1 whole, which is shorter than its diff:
```python
import functools
import math

import jax
import jax.numpy as jnp
from jax import lax
from jax.experimental import pallas as pl
from jax.experimental.pallas import tpu as pltpu
from jax.sharding import PartitionSpec as P

Q_LOW = 2
Q_HIGH = 5
RELAX_TIME = 1.25
BODY_FORCE = 0.002
DIFFUSION = 0.1
SURFACE = 0.4
BLOCK = 4
PLANES = 18


VMEM_LIMIT = 48 * 1024 * 1024


def row_mask(shape, row):
    return lax.broadcasted_iota(jnp.int32, shape, 0) == row


def collide_layer(pop, pore):
    p0 = pop(0)
    sums = []
    diffs = []
    for pair in range(9):
        fwd = pop(2 * pair + 1)
        bwd = pop(2 * pair + 2)
        sums.append(fwd + bwd)
        diffs.append(fwd - bwd)
    density = p0
    for s in sums:
        density = density + s
    mom_z = diffs[0] + diffs[3] + diffs[4] + diffs[5] + diffs[6]
    mom_y = diffs[1] + diffs[3] - diffs[4] + diffs[7] + diffs[8]
    mom_x = diffs[2] + diffs[5] - diffs[6] + diffs[7] - diffs[8]
    inv = 1.0 / density
    u_z = mom_z * inv + RELAX_TIME * BODY_FORCE
    u_y = mom_y * inv
    u_x = mom_x * inv
    is_pore = pore > 0
    rate = 1.0 / RELAX_TIME
    keep_s = jnp.where(is_pore, 0.5 * (1.0 - rate), 0.5)
    keep_d = jnp.where(is_pore, 0.5 * (1.0 - rate), -0.5)
    scaled = jnp.where(is_pore, density * (rate / 36.0), 0.0)
    h_z, h_y, h_x = scaled * u_z, scaled * u_y, scaled * u_x
    q_zz, q_yy, q_xx = 4.5 * h_z * u_z, 4.5 * h_y * u_y, 4.5 * h_x * u_x
    base = scaled - (q_zz + q_yy + q_xx) * (1.0 / 3.0)
    m_z, m_y, m_x = 3.0 * h_z, 3.0 * h_y, 3.0 * h_x
    q_zy, q_zx, q_yx = 3.0 * m_z * u_y, 3.0 * m_z * u_x, 3.0 * m_y * u_x
    out = [(keep_s + keep_s) * p0 + 12.0 * base]
    evens = [
        2.0 * (base + q_zz),
        2.0 * (base + q_yy),
        2.0 * (base + q_xx),
    ]
    zy = base + q_zz + q_yy
    zx = base + q_zz + q_xx
    yx = base + q_yy + q_xx
    evens += [zy + q_zy, zy - q_zy, zx + q_zx, zx - q_zx, yx + q_yx, yx - q_yx]
    odds = [2.0 * m_z, 2.0 * m_y, 2.0 * m_x, m_z + m_y, m_z - m_y, m_z + m_x, m_z - m_x, m_y + m_x, m_y - m_x]
    for pair in range(9):
        even = keep_s * sums[pair] + evens[pair]
        odd = keep_d * diffs[pair] + odds[pair]
        out.append(even + odd)
        out.append(even - odd)
    return out


def collide_kernel(pops, pore, m_low, m_high, pore_low, pore_high, wall_low, wall_high, acc, rows, up, down):
    step = pl.program_id(0)
    layers = pops.shape[1]
    width = pops.shape[2]
    total = acc.shape[1]
    shape = pops.shape[2:]

    @pl.when(step == 0)
    def _():
        acc[:, 0:2] = jnp.zeros((4, 2) + shape, jnp.float32)

    top = row_mask(shape, 0)
    bottom = row_mask(shape, width - 1)

    def layer(index, carry):
        z = step * layers + index
        r = collide_layer(lambda i: pops[i, index], pore[index])
        for i, sign in ((5, 1), (11, 1), (14, 1), (15, 1), (18, 1), (6, -1), (12, -1), (13, -1), (16, -1), (17, -1)):
            r[i] = pltpu.roll(r[i], sign % shape[1], 1)

        def shift_y(value, side):
            turned = pltpu.roll(value, 1 if side == 0 else width - 1, 0)
            return jnp.where(top if side == 0 else bottom, 0.0, turned)

        moved = []
        for side, (plain, x_up, x_down, z_up, z_down) in enumerate(((3, 15, 17, 7, 10), (4, 18, 16, 9, 8))):
            edge = width - 1 if side == 0 else 0
            both = r[plain] + r[x_up] + r[x_down]
            diff = r[x_up] - r[x_down]
            for slot, value in enumerate((both, diff, r[z_up], r[z_down])):
                rows[side, slot, pl.ds(z, 1), :] = value[edge : edge + 1]
            moved.append([shift_y(value, side) for value in (both, diff, r[z_up], r[z_down])])
        (up_d, up_x, up_zu, up_zd), (dn_d, dn_x, dn_zu, dn_zd) = moved
        acc[0, z + 2] = r[1] + r[11] + r[13] + up_zu + dn_zu
        acc[1, z + 2] = acc[0, z + 2]
        acc[2, z + 2] = up_zu - dn_zu
        acc[3, z + 2] = r[11] - r[13]
        acc[0, z + 1] = acc[0, z + 1] + (r[0] + r[5] + r[6] + up_d + dn_d)
        acc[2, z + 1] = acc[2, z + 1] + (up_d - dn_d)
        acc[3, z + 1] = acc[3, z + 1] + (r[5] - r[6] + up_x + dn_x)
        below = r[2] + r[12] + r[14] + up_zd + dn_zd
        acc[0, z] = acc[0, z] + below
        acc[1, z] = acc[1, z] - below
        acc[2, z] = acc[2, z] + (up_zd - dn_zd)
        acc[3, z] = acc[3, z] + (r[14] - r[12])
        return carry

    lax.fori_loop(0, layers, layer, 0)

    @pl.when(step == pl.num_programs(0) - 1)
    def _():
        last = total - 2
        for face, cross, own, near, far, pore_at, wall_at, z_row, diag in (
            (up, total - 1, last, m_high[:, 1], m_high[:, 0], pore_high, wall_high, last - 1, 2),
            (down, 0, 1, m_low[:, 0], m_low[:, 1], pore_low, wall_low, 0, 3),
        ):
            face[0] = acc[0, cross]
            face[1] = acc[2, cross]
            face[2] = acc[3, cross]
            face[3:7] = acc[:, own]
            face[7:11] = near
            face[11:15] = far
            face[15] = pore_at[0].astype(jnp.float32)
            face[16] = wall_at[0].astype(jnp.float32)
            inner = z_row - 1 if face is up else z_row + 1
            for side in range(2):
                at = 4 * side
                both = rows[side, 0, z_row : z_row + 1, :]
                diff = rows[side, 1, z_row : z_row + 1, :]
                along = rows[side, diag, inner : inner + 1, :]
                face[17, at : at + 1, :] = rows[side, diag, z_row : z_row + 1, :]
                face[17, at + 1 : at + 2, :] = both + along
                face[17, at + 2 : at + 3, :] = along if face is up else -along
                face[17, at + 3 : at + 4, :] = diff


def pack_kernel(acc, rows, magnet, pore, wall, up, down):
    depth = rows.shape[2]
    width = magnet.shape[2]
    first = row_mask((depth, rows.shape[3]), 0)
    final = row_mask((depth, rows.shape[3]), depth - 1)
    for side, face in ((0, up), (1, down)):
        from_below = jnp.where(first, 0.0, pltpu.roll(rows[side, 2], 1, 0))
        from_above = jnp.where(final, 0.0, pltpu.roll(rows[side, 3], depth - 1, 0))
        face[0] = rows[side, 0] + from_below + from_above
        face[1] = from_below - from_above
        face[2] = rows[side, 1]
        face[17] = jnp.zeros_like(face[17])

    def layer(z, carry):
        for face, near, far in ((up, width - 1, width - 2), (down, 0, 1)):
            at = pl.ds(z, 1)
            for k in range(4):
                face[3 + k, at, :] = acc[k, z + 1, near : near + 1, :]
                face[7 + k, at, :] = magnet[k, z, near : near + 1, :]
                face[11 + k, at, :] = magnet[k, z, far : far + 1, :]
            face[15, at, :] = pore[z, near : near + 1, :].astype(jnp.float32)
            face[16, at, :] = wall[z, near : near + 1, :].astype(jnp.float32)
        return carry

    lax.fori_loop(0, depth, layer, 0)


def merge_kernel(low, high, acc, rows, up_in, down_in, up, down):
    up[...] = up_in[...]
    down[...] = down_in[...]
    depth = rows.shape[2]
    width = low.shape[1]
    for side, face, edge in ((0, up, width - 1), (1, down, 0)):
        at = 4 * side
        for halo, z, sign in ((low, 0, 1.0), (high, depth - 1, -1.0)):
            here = pl.ds(z, 1)
            diag = halo[17, at : at + 1, :]
            face[0, here, :] = face[0, here, :] + diag
            face[1, here, :] = face[1, here, :] + sign * diag
            cross = halo[0, edge : edge + 1, :]
            face[3, here, :] = face[3, here, :] + cross
            face[4, here, :] = face[4, here, :] + sign * cross
            face[5, here, :] = face[5, here, :] + halo[1, edge : edge + 1, :]
            face[6, here, :] = face[6, here, :] + halo[2, edge : edge + 1, :]
            slot = 3 if sign > 0 else 2
            mine = rows[side, slot, here, :]
            base = 0 if sign > 0 else 3
            face[17, base : base + 1, :] = halo[17, at + 1 : at + 2, :] + mine
            face[17, base + 1 : base + 2, :] = halo[17, at + 2 : at + 3, :] - sign * mine
            face[17, base + 2 : base + 3, :] = halo[17, at + 3 : at + 4, :]
            base = 6 if sign > 0 else 10
            for k in range(4):
                face[17, base + k : base + k + 1, :] = halo[7 + k, edge : edge + 1, :]


def coefficients(vel, pore, wall):
    half = [0.5 * v for v in vel]
    plain = DIFFUSION * pore
    center = (1.0 - 6.0 * DIFFUSION) * pore - SURFACE * (pore * wall)
    return center, [(plain - h, plain + h) for h in half]


def stencil(coef, center, z_pair, y_pair, x_width):
    mid, ((z_p, z_m), (y_p, y_m), (x_p, x_m)) = coef
    plus_x = pltpu.roll(center, x_width - 1, 1)
    minus_x = pltpu.roll(center, 1, 1)
    return (
        mid * center
        + (z_p * z_pair[0] + z_m * z_pair[1])
        + (y_p * y_pair[0] + y_m * y_pair[1])
        + (x_p * plus_x + x_m * minus_x)
    )


def rotate(values, cos, sin):
    out = []
    for k in range(2):
        re, im = values[2 * k], values[2 * k + 1]
        out.append(re * cos[k] + im * sin[k])
        out.append(im * cos[k] - re * sin[k])
    return out


def final_kernel(
    table, wide, acc, magnet, pore, wall, low, high, left, right, up, down, vel_out, mag_out, sums, mid, thin
):
    depth, width, x_width = pore.shape
    shape = (width, x_width)
    top = row_mask(shape, 0)
    bottom = row_mask(shape, width - 1)
    first = row_mask((depth, x_width), 0)
    final = row_mask((depth, x_width), depth - 1)

    for side, face, own, sign in ((0, left, down, -1.0), (1, right, up, 1.0)):
        density = face[3] + own[0]
        inv = 1.0 / density
        pore_f = face[15]
        scale = pore_f * inv
        vel = [
            (face[4] + own[1]) * scale,
            (face[5] + sign * own[0]) * scale,
            (face[6] + own[2]) * scale,
        ]
        coef = coefficients(vel, pore_f, face[16])
        cos = [jnp.concatenate([wide[k], wide[k]], axis=1) for k in range(2)]
        sin = [jnp.concatenate([wide[2 + k], wide[2 + k]], axis=1) for k in range(2)]
        values = []
        for k in range(4):
            center = face[7 + k]
            plus = jnp.where(final, face[17, 10 + k : 11 + k, :], pltpu.roll(center, depth - 1, 0))
            minus = jnp.where(first, face[17, 6 + k : 7 + k, :], pltpu.roll(center, 1, 0))
            far, near = face[11 + k], own[7 + k]
            y_pair = (near, far) if side == 0 else (far, near)
            values.append(stencil(coef, center, (plus, minus), y_pair, x_width))
        for k, value in enumerate(rotate(values, cos, sin)):
            thin[side, k] = value

    def phases(z):
        return [table[0, z + 1], table[1, z + 1]], [table[2, z + 1], table[3, z + 1]]

    def velocity(moments, cross_left, cross_right, pore_f):
        density, m_z, m_y, m_x = moments
        d_l, z_l, x_l = cross_left
        d_r, z_r, x_r = cross_right
        density = density + jnp.where(top, d_l, jnp.where(bottom, d_r, 0.0))
        m_z = m_z + jnp.where(top, z_l, jnp.where(bottom, z_r, 0.0))
        m_y = m_y + jnp.where(top, d_l, jnp.where(bottom, -d_r, 0.0))
        m_x = m_x + jnp.where(top, x_l, jnp.where(bottom, x_r, 0.0))
        scale = pore_f / density
        return [m_z * scale, m_y * scale, m_x * scale]

    def beside(center, row_low, row_high):
        plus = jnp.where(bottom, row_high, pltpu.roll(center, width - 1, 0))
        minus = jnp.where(top, row_low, pltpu.roll(center, 1, 0))
        return plus, minus

    def first_step(z, vel, pore_f, wall_f, center, plus, minus, row_low, row_high):
        coef = coefficients(vel, pore_f, wall_f)
        cos, sin = phases(z)
        values = [
            stencil(coef, center(k), (plus(k), minus(k)), beside(center(k), row_low(k), row_high(k)), x_width)
            for k in range(4)
        ]
        for k, value in enumerate(rotate(values, cos, sin)):
            mid[k, z + 1] = value

    def halo_layer(halo, z, sign):
        cross = 0 if z < 0 else depth + 1
        moments = [
            halo[3] + acc[0, cross],
            halo[4] + acc[1, cross],
            halo[5] + acc[2, cross],
            halo[6] + acc[3, cross],
        ]
        base = 0 if z < 0 else 3
        vel = velocity(
            moments,
            [left[17, base + j : base + j + 1, :] for j in range(3)],
            [right[17, base + j : base + j + 1, :] for j in range(3)],
            halo[15],
        )
        corner = 6 if z < 0 else 10
        inside = 0 if z < 0 else depth - 1
        near, far = (lambda k: magnet[k, inside]), (lambda k: halo[11 + k])
        first_step(
            z,
            vel,
            halo[15],
            halo[16],
            lambda k: halo[7 + k],
            near if z < 0 else far,
            far if z < 0 else near,
            lambda k: left[17, corner + k : corner + k + 1, :],
            lambda k: right[17, corner + k : corner + k + 1, :],
        )

    def own_layer(z, extra, plus, minus):
        at = pl.ds(z, 1)
        moments = [acc[k, z + 1] for k in range(4)]
        if extra is not None:
            halo, sign = extra
            moments = [
                moments[0] + halo[0],
                moments[1] + sign * halo[0],
                moments[2] + halo[1],
                moments[3] + halo[2],
            ]
        pore_f = pore[z].astype(jnp.float32)
        wall_f = wall[z].astype(jnp.float32)
        vel = velocity(moments, [left[j, at, :] for j in range(3)], [right[j, at, :] for j in range(3)], pore_f)
        for j in range(3):
            vel_out[j, z] = vel[j]
        first_step(
            z,
            vel,
            pore_f,
            wall_f,
            lambda k: magnet[k, z],
            plus,
            minus,
            lambda k: left[7 + k, at, :],
            lambda k: right[7 + k, at, :],
        )

    halo_layer(low, -1, 1.0)
    own_layer(0, (low, 1.0), lambda k: magnet[k, 1], lambda k: low[7 + k])

    def inner(z, carry):
        own_layer(z, None, lambda k: magnet[k, z + 1], lambda k: magnet[k, z - 1])
        return carry

    lax.fori_loop(1, depth - 1, inner, 0)
    own_layer(depth - 1, (high, -1.0), lambda k: high[7 + k], lambda k: magnet[k, depth - 2])
    halo_layer(high, depth, -1.0)

    def second(z, totals):
        at = pl.ds(z, 1)
        pore_f = pore[z].astype(jnp.float32)
        wall_f = wall[z].astype(jnp.float32)
        coef = coefficients([vel_out[j, z] for j in range(3)], pore_f, wall_f)
        cos, sin = phases(z)
        values = []
        for k in range(4):
            center = mid[k, z + 1]
            y_pair = beside(center, thin[0, k, at, :], thin[1, k, at, :])
            values.append(stencil(coef, center, (mid[k, z + 2], mid[k, z]), y_pair, x_width))
        values = rotate(values, cos, sin)
        for k in range(4):
            mag_out[k, z] = values[k]
        return tuple(t + v for t, v in zip(totals, values))

    zero = jnp.zeros(shape, jnp.float32)
    totals = lax.fori_loop(0, depth, second, (zero, zero, zero, zero))
    sums[...] = jnp.zeros_like(sums)
    for k in range(4):
        line = jnp.sum(totals[k], axis=0, keepdims=True)
        sums[k : k + 1, :] = line[:, :128] + line[:, 128:]


def vmem(count):
    return [pl.BlockSpec(memory_space=pltpu.VMEM)] * count


def struct(*shape):
    return jax.ShapeDtypeStruct(shape, jnp.float32)


def collide(pops, magnet, pore, wall):
    _, depth, width, x_width = pops.shape
    last = depth // 2 - 1
    resident = lambda *shape: pl.BlockSpec(shape, lambda g: (0,) * len(shape))
    return pl.pallas_call(
        collide_kernel,
        grid=(depth // BLOCK,),
        in_specs=[
            pl.BlockSpec((19, BLOCK, width, x_width), lambda g: (0, g, 0, 0)),
            pl.BlockSpec((BLOCK, width, x_width), lambda g: (g, 0, 0)),
            pl.BlockSpec((4, 2, width, x_width), lambda g: (0, 0, 0, 0)),
            pl.BlockSpec((4, 2, width, x_width), lambda g: (0, last, 0, 0)),
            pl.BlockSpec((1, width, x_width), lambda g: (0, 0, 0)),
            pl.BlockSpec((1, width, x_width), lambda g: (depth - 1, 0, 0)),
            pl.BlockSpec((1, width, x_width), lambda g: (0, 0, 0)),
            pl.BlockSpec((1, width, x_width), lambda g: (depth - 1, 0, 0)),
        ],
        out_specs=[
            resident(4, depth + 2, width, x_width),
            resident(2, 4, depth, x_width),
            resident(PLANES, width, x_width),
            resident(PLANES, width, x_width),
        ],
        out_shape=[
            struct(4, depth + 2, width, x_width),
            struct(2, 4, depth, x_width),
            struct(PLANES, width, x_width),
            struct(PLANES, width, x_width),
        ],
        compiler_params=pltpu.CompilerParams(vmem_limit_bytes=VMEM_LIMIT),
        name="collide",
    )(pops, pore, magnet, magnet, pore, pore, wall, wall)


def pack(acc, rows, magnet, pore, wall):
    depth, x_width = rows.shape[2:]
    return pl.pallas_call(
        pack_kernel,
        in_specs=vmem(5),
        out_specs=vmem(2),
        out_shape=[struct(PLANES, depth, x_width)] * 2,
        compiler_params=pltpu.CompilerParams(vmem_limit_bytes=VMEM_LIMIT),
        cost_estimate=pl.CostEstimate(flops=2_000_000, bytes_accessed=6_000_000, transcendentals=0),
        name="pack",
    )(acc, rows, magnet, pore, wall)


def merge(low, high, acc, rows, up, down):
    return pl.pallas_call(
        merge_kernel,
        in_specs=vmem(6),
        out_specs=vmem(2),
        out_shape=[struct(*up.shape)] * 2,
        input_output_aliases={4: 0, 5: 1},
        compiler_params=pltpu.CompilerParams(vmem_limit_bytes=VMEM_LIMIT),
        name="merge",
    )(low, high, acc, rows, up, down)


def finish(table, wide, acc, magnet, pore, wall, low, high, left, right, up, down):
    depth, width, x_width = pore.shape
    return pl.pallas_call(
        final_kernel,
        in_specs=[pl.BlockSpec(memory_space=pltpu.SMEM)] + vmem(11),
        out_specs=vmem(3),
        out_shape=[struct(3, depth, width, x_width), struct(4, depth, width, x_width), struct(8, 128)],
        scratch_shapes=[
            pltpu.VMEM((4, depth + 2, width, x_width), jnp.float32),
            pltpu.VMEM((2, 4, depth, x_width), jnp.float32),
        ],
        compiler_params=pltpu.CompilerParams(vmem_limit_bytes=VMEM_LIMIT),
        name="finish",
    )(table, wide, acc, magnet, pore, wall, low, high, left, right, up, down)


def ring(value, axis, step):
    count = lax.axis_size(axis)
    return lax.ppermute(value, axis, [(i, (i + step) % count) for i in range(count)])


def phase_tables(start, depth, extent):
    layers = jnp.remainder(start + jnp.arange(-1, depth + 1, dtype=jnp.int32), extent)
    coords = layers.astype(jnp.float32)
    wave_numbers = jnp.array([Q_LOW, Q_HIGH], jnp.float32)
    angles = 2.0 * math.pi * wave_numbers[:, None] * coords[None, :] / extent
    return jnp.concatenate([jnp.cos(angles), jnp.sin(angles)], axis=0)


def sum_over(value, axis):
    count = lax.axis_size(axis)
    copies = jnp.broadcast_to(value[None], (count,) + value.shape)
    return jnp.sum(lax.all_to_all(copies, axis, 0, 0), axis=0)


def local(populations, magnetization, pore, wall):
    _, depth, width, x_width = populations.shape
    flow_count = lax.axis_size("flow")
    trans_count = lax.axis_size("trans")
    extent = depth * flow_count
    magnet = magnetization.reshape(4, depth, width, x_width)

    acc, rows, face_up, face_down = collide(populations, magnet, pore, wall)
    low = ring(face_up, "flow", 1)
    high = ring(face_down, "flow", -1)
    up, down = pack(acc, rows, magnet, pore, wall)
    up, down = merge(low, high, acc, rows, up, down)
    left = ring(up, "trans", 1)
    right = ring(down, "trans", -1)

    table = phase_tables(lax.axis_index("flow") * depth, depth, extent)
    wide = jnp.broadcast_to(table[:, 1:-1, None], (4, depth, 128))
    velocity, magnet, sums = finish(table, wide, acc, magnet, pore, wall, low, high, left, right, up, down)

    sums = sum_over(sum_over(sums, "flow"), "trans")
    signal = jnp.sum(sums[:4], axis=1).reshape(2, 2) / math.sqrt(extent * width * trans_count * x_width)
    return (velocity, magnet.reshape(magnetization.shape), signal)


def solution(mesh):
    placed = (
        P(None, "flow", "trans", None),
        P(None, None, "flow", "trans", None),
        P("flow", "trans", None),
        P("flow", "trans", None),
    )
    return jax.shard_map(
        local,
        mesh=mesh,
        in_specs=placed,
        out_specs=(P(None, "flow", "trans", None), P(None, None, "flow", "trans", None), P()),
        check_vma=False,
    )
```

time: 160 us -> 79.7 us (0.50)
  blocking collectives: 76.9 us -> 26.4 us
  other arithmetic: 27.5 us -> 0.3 us
  Pallas kernels: 0 us -> 18.4 us
  starting transfers between devices: 23.7 us -> 11 us
  local copies, waits for them, and re-layouts: 13.6 us -> 6.21 us
    psum x1 -> x0, blocking collectives: 76.9 us -> none  [local(): totals = lax.psum(local_sums, ('flow', 'trans'))]
    all_to_all x0 -> x2, blocking collectives: none -> 26.4 us  [sum_over(): return jnp.sum(lax.all_to_all(copies, axis, 0, 0), axis=0)]
    pallas_call x0 -> x4, Pallas kernels: none -> 18.4 us  [the longest x1 8.63 us: finish(): pl.pallas_call(final_kernel, in_specs=[pl.BlockSpec(memory_space=pltpu.SM...]
    ppermute x12 -> x4, starting transfers between devices: 23.7 us -> 11 us  [ring(): lax.ppermute(value, axis, [(i, (i + step) % count) for i in range(count)])]
    unnamed x19 -> x0, other arithmetic: 10.1 us -> none
    slice x24 -> x1, local copies, waits for them, and re-layouts: 7.1 us -> 0.07 us  [local(): wide = jnp.broadcast_to(table[:, 1:-1, None], (4, depth, 128))]
    sub x2 -> x0, other arithmetic: 5.56 us -> none  [torrey_step(): center + diffusion_step * laplace - advect - surface_relax * wall_f * center]
    slice x3 -> x0, other arithmetic: 3.91 us -> none  [the longest x1 3.84 us: padded_2(): lax.slice_in_dim(cells, cells.shape[dim] - width, cells.shape[dim], axis=...]
  transfers between devices with their start and end apart: 12 -> 4, of which waited for: 5 -> 3; matrix products, arithmetic and copies ran while one was open for 11% -> 0% of each run, Pallas kernels for 0% -> 1%
where the time goes in v1:
time: 79.7 us; the launch traced here: 79.2 us
  blocking collectives  26.4 us (33%)
  Pallas kernels  18.4 us (23%)
  waiting for transfers between devices  16.3 us (20%)
  starting transfers between devices  11 us (14%)
  local copies, waits for them, and re-layouts  6.21 us (8%)
    all_to_all x2, blocking collectives, sum_over(): return jnp.sum(lax.all_to_all(copies, axis, 0, 0), axis=0)  26.4 us
    ppermute x4, waiting for transfers between devices, ring(): lax.ppermute(value, axis, [(i, (i + step) % count) for i in range(count)])  16.3 us
    ppermute x4, starting transfers between devices, ring(): lax.ppermute(value, axis, [(i, (i + step) % count) for i in range(count)])  11 us
    pallas_call x1, Pallas kernels, finish(): pl.pallas_call(final_kernel, in_specs=[pl.BlockSpec(memory_space=pltpu.SM...  8.63 us
    pallas_call x1, Pallas kernels, collide(): pl.pallas_call(collide_kernel, grid=(depth // BLOCK,), in_specs=[pl.Block...  7.96 us
    unnamed x20, local copies, waits for them, and re-layouts  5.41 us
  transfers between devices with their start and end apart: 4, of which 3 were waited for; matrix products, arithmetic and copies ran while one was open for 0% of the time, Pallas kernels for 1%

profile of v1, /device:TPU:1, one launch (start us, length us, event | category | flops | bytes accessed | tf_op | source)
XLA Modules:
  0.0 79.2 jit_solution(8573848127695670763)
XLA Ops:
  0.6 0.0 copy-start
  0.6 1.4 %copy-done = f32[2,2,24,16,256]{4,3,2,1,0:T(8,128)S(1)} copy-done((f32[2,2,24,16,256]{4,3,2,1,0:T(8,128)S(1)}, f32[2,2,24,16,256]{4,3,2,1,0:T(8,128)}, u32[]{:S(2)}) %copy-start) | copy-done | bytes 1572888
  2.0 0.0 copy-start.3
  2.0 1.0 %copy-done.3 = s32[24,16,256]{2,1,0:T(8,128)S(1)} copy-done((s32[24,16,256]{2,1,0:T(8,128)S(1)}, s32[24,16,256]{2,1,0:T(8,128)}, u32[]{:S(2)}) %copy-start.3) | copy-done | bytes 393240
  3.0 0.0 copy-start.6
  3.0 1.0 %copy-done.6 = s32[24,16,256]{2,1,0:T(8,128)S(1)} copy-done((s32[24,16,256]{2,1,0:T(8,128)S(1)}, s32[24,16,256]{2,1,0:T(8,128)}, u32[]{:S(2)}) %copy-start.6) | copy-done | bytes 393240
  4.0 0.0 copy-start.1
  4.0 8.0 %collide.1 = (f32[4,26,16,256]{3,2,1,0:T(8,128)S(1)}, f32[2,4,24,256]{3,2,1,0:T(8,128)S(1)}, f32[18,16,256]{2,1,0:T(8,128)}, f32[18,16,256]{2,1,0:T(8,128)}) custom-call(f32[19,24,16,256]{3,2,1,0:T(8,128)} %pops.1, s32[24,16,256]{2,1,0:T(8,128)S(1)} %copy-done.3, f32[4,24,16,256]{3,2,1,0:T(8,128)S(1)} %bitcast.2, f32[4,24,16,256]{3,2,1,0:T(8,128)S(1)} %bitcast.3, ...), custom_call_target="tpu_custom_call" | custom-call | tf_op jit(solution)/shard_map/collide/pallas_call | solution.py:403
  12.0 0.0 copy-start.2
  12.0 2.5 %collective-permute-start = (f32[18,16,256]{2,1,0:T(8,128)}, f32[18,16,256]{2,1,0:T(8,128)}, u32[]{:S(2)}, u32[]{:S(2)}) collective-permute-start(f32[18,16,256]{2,1,0:T(8,128)} %get-tuple-element.15), channel_id=1, source_target_pairs={{0,16},{16,32},{32,48},{48,64},{64,80},{80,96},{96,112},{112,128},... | collective-permute-start | bytes 884744 | tf_op jit(solution)/shard_map/ppermute | solution.py:476
  14.5 4.9 %collective-permute-start.1 = (f32[18,16,256]{2,1,0:T(8,128)}, f32[18,16,256]{2,1,0:T(8,128)}, u32[]{:S(2)}, u32[]{:S(2)}) collective-permute-start(f32[18,16,256]{2,1,0:T(8,128)} %get-tuple-element.16), channel_id=1, source_target_pairs={{0,240},{16,0},{32,16},{48,32},{64,48},{80,64},{96,80},{112,96},{1... | collective-permute-start | bytes 884744 | tf_op jit(solution)/shard_map/ppermute | solution.py:476
  19.4 0.0 copy-done.1
  19.4 0.0 copy-start.4
  19.4 1.0 %copy-done.4 = s32[24,16,256]{2,1,0:T(8,128)S(1)} copy-done((s32[24,16,256]{2,1,0:T(8,128)S(1)}, s32[24,16,256]{2,1,0:T(8,128)}, u32[]{:S(2)}) %copy-start.4) | copy-done | bytes 393240
  20.4 0.0 copy-start.7
  20.4 1.0 %copy-done.7 = s32[24,16,256]{2,1,0:T(8,128)S(1)} copy-done((s32[24,16,256]{2,1,0:T(8,128)S(1)}, s32[24,16,256]{2,1,0:T(8,128)}, u32[]{:S(2)}) %copy-start.7) | copy-done | bytes 393240
  21.4 0.5 pack.1
  21.9 4.5 %collective-permute-done.low = f32[18,16,256]{2,1,0:T(8,128)} collective-permute-done((f32[18,16,256]{2,1,0:T(8,128)}, f32[18,16,256]{2,1,0:T(8,128)}, u32[]{:S(2)}, u32[]{:S(2)}) %collective-permute-start) | collective-permute-done | bytes 294944 | tf_op jit(solution)/shard_map/ppermute | solution.py:476
  26.4 0.0 collective-permute-done.1.high
  26.4 0.0 copy-done.2
  26.4 0.0 copy-start.9
  26.4 0.0 copy-start.5
  26.4 0.0 copy-start.8
  26.4 1.3 %merge.1 = (f32[18,24,256]{2,1,0:T(8,128)S(1)}, f32[18,24,256]{2,1,0:T(8,128)S(1)}) custom-call(f32[18,16,256]{2,1,0:T(8,128)} %collective-permute-done.low, f32[18,16,256]{2,1,0:T(8,128)} %collective-permute-done.1.high, f32[4,26,16,256]{3,2,1,0:T(8,128)S(1)} %get-tuple-element.14.acc, ...), custom_call_target="tpu_custom_call", output_to_operand_aliasing={{0}: (4, {}), {1}: (5, {})} | custom-call | tf_op jit(solution)/shard_map/merge/pallas_call | solution.py:447
  27.7 3.6 %collective-permute-start.2 = (f32[18,24,256]{2,1,0:T(8,128)S(1)}, f32[18,24,256]{2,1,0:T(8,128)S(1)}, u32[]{:S(2)}, u32[]{:S(2)}) collective-permute-start(f32[18,24,256]{2,1,0:T(8,128)S(1)} %get-tuple-element.20.up), channel_id=1, source_target_pairs={{0,1},{1,2},{2,3},{3,4},{4,5},{5,6},{6,7},{7,8},{8,9},{9,10},{10,1... | collective-permute-start | bytes 1327112 | tf_op jit(solution)/shard_map/ppermute | solution.py:476
  31.3 0.0 collective-permute-start.3
  31.3 0.0 copy-done.9
  31.3 0.1 fusion.1
  31.5 0.1 slice.6
  31.5 6.5 %collective-permute-done.2.left = f32[18,24,256]{2,1,0:T(8,128)S(1)} collective-permute-done((f32[18,24,256]{2,1,0:T(8,128)S(1)}, f32[18,24,256]{2,1,0:T(8,128)S(1)}, u32[]{:S(2)}, u32[]{:S(2)}) %collective-permute-start.2) | collective-permute-done | bytes 442400 | tf_op jit(solution)/shard_map/ppermute | solution.py:476
  38.0 5.2 %collective-permute-done.3.right = f32[18,24,256]{2,1,0:T(8,128)S(1)} collective-permute-done((f32[18,24,256]{2,1,0:T(8,128)S(1)}, f32[18,24,256]{2,1,0:T(8,128)S(1)}, u32[]{:S(2)}, u32[]{:S(2)}) %collective-permute-start.3) | collective-permute-done | bytes 442400 | tf_op jit(solution)/shard_map/ppermute | solution.py:476
  43.3 0.1 broadcast_in_dim.6.wide
  43.3 0.0 copy-done.5
  43.4 0.0 copy-done.8
  43.4 8.6 %finish.1 = (f32[3,24,16,256]{3,2,1,0:T(8,128)}, f32[4,24,16,256]{3,2,1,0:T(8,128)}, f32[8,128]{1,0:T(8,128)S(1)}) custom-call(f32[4,26]{1,0:T(4,128)S(1)} %pad_maximum_fusion.table, f32[4,24,128]{2,1,0:T(8,128)S(1)} %broadcast_in_dim.6.wide, f32[4,26,16,256]{3,2,1,0:T(8,128)} %copy-done.2, f32[4,24,16,256]{3,2,1,0:T(8,128)S(1)} %bitcast.5, ...), custom_call_target="tpu_custom_call" | custom-call | tf_op jit(solution)/shard_map/finish/pallas_call | solution.py:460
  52.0 13.0 %all_to_all.10 = f32[16,8,128]{2,1,0:T(8,128)S(1)} all-to-all(f32[16,8,128]{2,1,0:T(8,128)S(1)} %broadcast_in_dim.7), channel_id=1, replica_groups=mesh['flow'=16,'trans'=16] {'flow'}, dimensions={0} | all-to-all | bytes 131072 | tf_op jit(solution)/shard_map/all_to_all | solution.py:490
  65.0 13.5 %all_to_all.11 = f32[16,8,128]{2,1,0:T(8,128)S(1)} all-to-all(f32[16,8,128]{2,1,0:T(8,128)S(1)} %broadcast_in_dim.8), channel_id=1, replica_groups=mesh['flow'=16,'trans'=16] {'trans'}, dimensions={0} | all-to-all | bytes 131072 | tf_op jit(solution)/shard_map/all_to_all | solution.py:490
  78.5 0.1 slice_reduce_fusion
  78.6 0.6 div.14
  (7 shorter events, 0.1 us)
Async XLA Ops:
  0.6 1.4 %copy-start = (f32[2,2,24,16,256]{4,3,2,1,0:T(8,128)S(1)}, f32[2,2,24,16,256]{4,3,2,1,0:T(8,128)}, u32[]{:S(2)}) copy-start(f32[2,2,24,16,256]{4,3,2,1,0:T(8,128)} %param.6) | copy-start | bytes 4718596
  2.0 1.0 %copy-start.3 = (s32[24,16,256]{2,1,0:T(8,128)S(1)}, s32[24,16,256]{2,1,0:T(8,128)}, u32[]{:S(2)}) copy-start(s32[24,16,256]{2,1,0:T(8,128)} %pore.5) | copy-start | bytes 1179652
  3.0 1.0 %copy-start.6 = (s32[24,16,256]{2,1,0:T(8,128)S(1)}, s32[24,16,256]{2,1,0:T(8,128)}, u32[]{:S(2)}) copy-start(s32[24,16,256]{2,1,0:T(8,128)} %wall.3) | copy-start | bytes 1179652
  4.0 15.3 %copy-start.1 = (f32[2,2,24,16,256]{4,3,2,1,0:T(8,128)S(1)}, f32[2,2,24,16,256]{4,3,2,1,0:T(8,128)}, u32[]{:S(2)}) copy-start(f32[2,2,24,16,256]{4,3,2,1,0:T(8,128)} %param.6) | copy-start | bytes 4718596
  12.0 14.4 %copy-start.2 = (f32[4,26,16,256]{3,2,1,0:T(8,128)}, f32[4,26,16,256]{3,2,1,0:T(8,128)S(1)}, u32[]{:S(2)}) copy-start(f32[4,26,16,256]{3,2,1,0:T(8,128)S(1)} %get-tuple-element.14.acc) | copy-start | bytes 5111812
  12.0 14.4 %collective-permute-start = (f32[18,16,256]{2,1,0:T(8,128)}, f32[18,16,256]{2,1,0:T(8,128)}, u32[]{:S(2)}, u32[]{:S(2)}) collective-permute-start(f32[18,16,256]{2,1,0:T(8,128)} %get-tuple-element.15), channel_id=1, source_target_pairs={{0,16},{16,32},{32,48},{48,64},{64,80},{80,96},{96,112},{112,128},... | collective-permute-start | bytes 884744 | tf_op jit(solution)/shard_map/ppermute | solution.py:476
  14.5 11.9 %collective-permute-start.1 = (f32[18,16,256]{2,1,0:T(8,128)}, f32[18,16,256]{2,1,0:T(8,128)}, u32[]{:S(2)}, u32[]{:S(2)}) collective-permute-start(f32[18,16,256]{2,1,0:T(8,128)} %get-tuple-element.16), channel_id=1, source_target_pairs={{0,240},{16,0},{32,16},{48,32},{64,48},{80,64},{96,80},{112,96},{1... | collective-permute-start | bytes 884744 | tf_op jit(solution)/shard_map/ppermute | solution.py:476
  19.4 1.0 %copy-start.4 = (s32[24,16,256]{2,1,0:T(8,128)S(1)}, s32[24,16,256]{2,1,0:T(8,128)}, u32[]{:S(2)}) copy-start(s32[24,16,256]{2,1,0:T(8,128)} %pore.5) | copy-start | bytes 1179652
  20.4 1.0 %copy-start.7 = (s32[24,16,256]{2,1,0:T(8,128)S(1)}, s32[24,16,256]{2,1,0:T(8,128)}, u32[]{:S(2)}) copy-start(s32[24,16,256]{2,1,0:T(8,128)} %wall.3) | copy-start | bytes 1179652
  26.4 5.0 %copy-start.9 = (f32[2]{0:T(128)S(1)}, f32[2]{0:T(128)}, u32[]{:S(2)}) copy-start(f32[2]{0:T(128)} %constant.38) | copy-start | bytes 28
  26.4 17.0 %copy-start.5 = (s32[24,16,256]{2,1,0:T(8,128)S(1)}, s32[24,16,256]{2,1,0:T(8,128)}, u32[]{:S(2)}) copy-start(s32[24,16,256]{2,1,0:T(8,128)} %pore.5) | copy-start | bytes 1179652
  26.4 17.0 %copy-start.8 = (s32[24,16,256]{2,1,0:T(8,128)S(1)}, s32[24,16,256]{2,1,0:T(8,128)}, u32[]{:S(2)}) copy-start(s32[24,16,256]{2,1,0:T(8,128)} %wall.3) | copy-start | bytes 1179652
  27.7 10.4 %collective-permute-start.2 = (f32[18,24,256]{2,1,0:T(8,128)S(1)}, f32[18,24,256]{2,1,0:T(8,128)S(1)}, u32[]{:S(2)}, u32[]{:S(2)}) collective-permute-start(f32[18,24,256]{2,1,0:T(8,128)S(1)} %get-tuple-element.20.up), channel_id=1, source_target_pairs={{0,1},{1,2},{2,3},{3,4},{4,5},{5,6},{6,7},{7,8},{8,9},{9,10},{10,1... | collective-permute-start | bytes 1327112 | tf_op jit(solution)/shard_map/ppermute | solution.py:476
  31.3 12.0 %collective-permute-start.3 = (f32[18,24,256]{2,1,0:T(8,128)S(1)}, f32[18,24,256]{2,1,0:T(8,128)S(1)}, u32[]{:S(2)}, u32[]{:S(2)}) collective-permute-start(f32[18,24,256]{2,1,0:T(8,128)S(1)} %get-tuple-element.21.down), channel_id=1, source_target_pairs={{0,15},{1,0},{2,1},{3,2},{4,3},{5,4},{6,5},{7,6},{8,7},{9,8},{10,9... | collective-permute-start | bytes 1327112 | tf_op jit(solution)/shard_map/ppermute | solution.py:476

commit v2 on v0

v2 whole, which is shorter than its diff:
```python
import functools
import math

import jax
import jax.numpy as jnp
from jax import lax
from jax.experimental import pallas as pl
from jax.experimental.pallas import tpu as pltpu
from jax.sharding import PartitionSpec as P

Q_LOW = 2
Q_HIGH = 5
RELAX_TIME = 1.25
BODY_FORCE = 0.002
DIFFUSION = 0.1
SURFACE = 0.4


MIB = 1024 * 1024


def row_mask(shape, row):
    return lax.broadcasted_iota(jnp.int32, shape, 0) == row


def is_even():
    return lax.rem(lax.axis_index("trans"), 2) == 0


def collide_layer(pop, pore):
    p0 = pop(0)
    sums = []
    diffs = []
    for pair in range(9):
        fwd = pop(2 * pair + 1)
        bwd = pop(2 * pair + 2)
        sums.append(fwd + bwd)
        diffs.append(fwd - bwd)
    density = p0
    for s in sums:
        density = density + s
    mom_z = diffs[0] + diffs[3] + diffs[4] + diffs[5] + diffs[6]
    mom_y = diffs[1] + diffs[3] - diffs[4] + diffs[7] + diffs[8]
    mom_x = diffs[2] + diffs[5] - diffs[6] + diffs[7] - diffs[8]
    inv = 1.0 / density
    u_z = mom_z * inv + RELAX_TIME * BODY_FORCE
    u_y = mom_y * inv
    u_x = mom_x * inv
    is_pore = pore > 0
    rate = 1.0 / RELAX_TIME
    keep_s = jnp.where(is_pore, 0.5 * (1.0 - rate), 0.5)
    keep_d = jnp.where(is_pore, 0.5 * (1.0 - rate), -0.5)
    scaled = jnp.where(is_pore, density * (rate / 36.0), 0.0)
    h_z, h_y, h_x = scaled * u_z, scaled * u_y, scaled * u_x
    q_zz, q_yy, q_xx = 4.5 * h_z * u_z, 4.5 * h_y * u_y, 4.5 * h_x * u_x
    base = scaled - (q_zz + q_yy + q_xx) * (1.0 / 3.0)
    m_z, m_y, m_x = 3.0 * h_z, 3.0 * h_y, 3.0 * h_x
    q_zy, q_zx, q_yx = 3.0 * m_z * u_y, 3.0 * m_z * u_x, 3.0 * m_y * u_x
    out = [(keep_s + keep_s) * p0 + 12.0 * base]
    evens = [
        2.0 * (base + q_zz),
        2.0 * (base + q_yy),
        2.0 * (base + q_xx),
    ]
    zy = base + q_zz + q_yy
    zx = base + q_zz + q_xx
    yx = base + q_yy + q_xx
    evens += [zy + q_zy, zy - q_zy, zx + q_zx, zx - q_zx, yx + q_yx, yx - q_yx]
    odds = [2.0 * m_z, 2.0 * m_y, 2.0 * m_x, m_z + m_y, m_z - m_y, m_z + m_x, m_z - m_x, m_y + m_x, m_y - m_x]
    for pair in range(9):
        even = keep_s * sums[pair] + evens[pair]
        odd = keep_d * diffs[pair] + odds[pair]
        out.append(even + odd)
        out.append(even - odd)
    return out


def stream_layer(r):
    width, x_width = r[0].shape
    shape = (width, x_width)
    r = list(r)
    for i, sign in ((5, 1), (11, 1), (14, 1), (15, 1), (18, 1), (6, -1), (12, -1), (13, -1), (16, -1), (17, -1)):
        r[i] = pltpu.roll(r[i], sign % x_width, 1)
    top = row_mask(shape, 0)
    bottom = row_mask(shape, width - 1)
    moved, edges = [], []
    for side, (plain, x_up, x_down, z_up, z_down) in enumerate(((3, 15, 17, 7, 10), (4, 18, 16, 9, 8))):
        both = r[plain] + r[x_up] + r[x_down]
        diff = r[x_up] - r[x_down]
        values = (both, diff, r[z_up], r[z_down])
        edge = width - 1 if side == 0 else 0
        edges.append([v[edge : edge + 1] for v in values])
        turn = 1 if side == 0 else width - 1
        moved.append([jnp.where(top if side == 0 else bottom, 0.0, pltpu.roll(v, turn, 0)) for v in values])
    (up_d, up_x, up_zu, up_zd), (dn_d, dn_x, dn_zu, dn_zd) = moved
    above = (r[1] + r[11] + r[13] + up_zu + dn_zu, up_zu - dn_zu, r[11] - r[13])
    here = (r[0] + r[5] + r[6] + up_d + dn_d, up_d - dn_d, r[5] - r[6] + up_x + dn_x)
    below = (r[2] + r[12] + r[14] + up_zd + dn_zd, up_zd - dn_zd, r[14] - r[12])
    return above, here, below, edges


def edge_kernel(pops, magnet, pore, wall, up, down, near, far, low_p, high_p, mag, por, wal, sems):
    depth, width = por.shape[:2]
    copies = [
        pltpu.make_async_copy(pops.at[:, pl.ds(depth - 2, 2)], high_p, sems.at[0]),
        pltpu.make_async_copy(pops.at[:, pl.ds(0, 2)], low_p, sems.at[1]),
        pltpu.make_async_copy(pore, por, sems.at[2]),
        pltpu.make_async_copy(wall, wal, sems.at[3]),
        pltpu.make_async_copy(magnet, mag, sems.at[4]),
    ]
    for copy in copies:
        copy.start()
    copies[2].wait()
    for face, held, copy, border, behind in ((up, high_p, 0, 1, 0), (down, low_p, 1, 0, 1)):
        copies[copy].wait()
        first = depth - 2 if face is up else 0

        def layer(at):
            return stream_layer(collide_layer(lambda i: held[i, at], por[first + at]))

        above, here, below, edges = layer(border)
        above_in, _, below_in, edges_in = layer(behind)
        cross, along = (above, above_in) if face is up else (below, below_in)
        sign = 1.0 if face is up else -1.0
        for j in range(3):
            face[j] = cross[j]
        face[3] = here[0] + along[0]
        face[4] = sign * along[0]
        face[5] = here[1] + along[1]
        face[6] = here[2] + along[2]
        diag = 2 if face is up else 3
        face[17] = jnp.zeros_like(face[17])
        for side in range(2):
            at = 4 * side
            face[17, at : at + 1, :] = edges[side][diag]
            face[17, at + 1 : at + 2, :] = edges[side][0] + edges_in[side][diag]
            face[17, at + 2 : at + 3, :] = sign * edges_in[side][diag]
            face[17, at + 3 : at + 4, :] = edges[side][1]
    copies[3].wait()
    copies[4].wait()
    for face, border, behind in ((up, depth - 1, depth - 2), (down, 0, 1)):
        face[7:11] = mag[:, border]
        face[11:15] = mag[:, behind]
        face[15] = por[border].astype(jnp.float32)
        face[16] = wal[border].astype(jnp.float32)

    def rows(face, border, behind):
        def layer(z, carry):
            at = pl.ds(z, 1)
            for k in range(4):
                face[k, at, :] = mag[k, z, border : border + 1, :]
                face[4 + k, at, :] = mag[k, z, behind : behind + 1, :]
            face[8, at, :] = por[z, border : border + 1, :].astype(jnp.float32)
            face[9, at, :] = wal[z, border : border + 1, :].astype(jnp.float32)
            return carry

        lax.fori_loop(0, depth, layer, 0, unroll=2)

    even = is_even()

    @pl.when(even)
    def _():
        rows(near, width - 1, width - 2)
        rows(far, 0, 1)

    @pl.when(jnp.logical_not(even))
    def _():
        rows(near, 0, 1)
        rows(far, width - 1, width - 2)


def collide_kernel(pops, pore, acc, up, down, held, por, rows, sems):
    depth, width, x_width = por.shape
    shape = (width, x_width)
    chunks = sems.shape[0] - 1
    size = depth // chunks
    copies = [
        pltpu.make_async_copy(pops.at[:, pl.ds(c * size, size)], held.at[:, pl.ds(c * size, size)], sems.at[c])
        for c in range(chunks)
    ]
    pore_copy = pltpu.make_async_copy(pore, por, sems.at[chunks])
    pore_copy.start()
    for copy in copies:
        copy.start()
    acc[:, 0:2] = jnp.zeros((4, 2) + shape, jnp.float32)

    def layer(z, carry):
        above, here, below, edges = stream_layer(collide_layer(lambda i: held[i, z], por[z]))
        for side in range(2):
            for slot in range(4):
                rows[side, slot, pl.ds(z, 1), :] = edges[side][slot]
        acc[0, z + 2] = above[0]
        acc[1, z + 2] = above[0]
        acc[2, z + 2] = above[1]
        acc[3, z + 2] = above[2]
        acc[0, z + 1] = acc[0, z + 1] + here[0]
        acc[2, z + 1] = acc[2, z + 1] + here[1]
        acc[3, z + 1] = acc[3, z + 1] + here[2]
        acc[0, z] = acc[0, z] + below[0]
        acc[1, z] = acc[1, z] - below[0]
        acc[2, z] = acc[2, z] + below[1]
        acc[3, z] = acc[3, z] + below[2]
        return carry

    pore_copy.wait()
    for c in range(chunks):
        copies[c].wait()
        lax.fori_loop(c * size, (c + 1) * size, layer, 0, unroll=2)

    first = row_mask((depth, x_width), 0)
    final = row_mask((depth, x_width), depth - 1)
    for side, face in ((0, up), (1, down)):
        from_below = jnp.where(first, 0.0, pltpu.roll(rows[side, 2], 1, 0))
        from_above = jnp.where(final, 0.0, pltpu.roll(rows[side, 3], depth - 1, 0))
        face[0] = rows[side, 0] + from_below + from_above
        face[1] = from_below - from_above
        face[2] = rows[side, 1]
        face[7] = jnp.zeros_like(face[7])
        face[7, 0:1, :] = rows[side, 3, 0:1, :]
        face[7, 3:4, :] = rows[side, 2, depth - 1 : depth, :]

    def border(z, carry):
        for face, edge in ((up, width - 1), (down, 0)):
            for k in range(4):
                face[3 + k, pl.ds(z, 1), :] = acc[k, z + 1, edge : edge + 1, :]
        return carry

    lax.fori_loop(0, depth, border, 0, unroll=2)


def merge_kernel(low, high, up, down, near, far):
    depth = up.shape[1]
    width = low.shape[1]

    def put(face, own, side, edge):
        face[...] = own[...]
        at = 4 * side
        for halo, z, sign, base, corner in ((low, 0, 1.0, 0, 6), (high, depth - 1, -1.0, 3, 10)):
            here = slice(z, z + 1)
            diag = halo[17, at : at + 1, :]
            face[0, here, :] = own[0, here, :] + diag
            face[1, here, :] = own[1, here, :] + sign * diag
            cross = halo[0, edge : edge + 1, :]
            face[3, here, :] = own[3, here, :] + cross
            face[4, here, :] = own[4, here, :] + sign * cross
            face[5, here, :] = own[5, here, :] + halo[1, edge : edge + 1, :]
            face[6, here, :] = own[6, here, :] + halo[2, edge : edge + 1, :]
            mine = own[7, base : base + 1, :]
            face[7, base : base + 1, :] = halo[17, at + 1 : at + 2, :] + mine
            face[7, base + 1 : base + 2, :] = halo[17, at + 2 : at + 3, :] - sign * mine
            face[7, base + 2 : base + 3, :] = halo[17, at + 3 : at + 4, :]
            for k in range(4):
                face[7, corner + k : corner + k + 1, :] = halo[7 + k, edge : edge + 1, :]

    even = is_even()

    @pl.when(even)
    def _():
        put(near, up, 0, width - 1)
        put(far, down, 1, 0)

    @pl.when(jnp.logical_not(even))
    def _():
        put(near, down, 1, 0)
        put(far, up, 0, width - 1)


def coefficients(vel, pore, wall):
    half = [0.5 * v for v in vel]
    plain = DIFFUSION * pore
    center = (1.0 - 6.0 * DIFFUSION) * pore - SURFACE * (pore * wall)
    return center, [(plain - h, plain + h) for h in half]


def stencil(coef, center, z_pair, y_pair, x_width):
    mid, ((z_p, z_m), (y_p, y_m), (x_p, x_m)) = coef
    plus_x = pltpu.roll(center, x_width - 1, 1)
    minus_x = pltpu.roll(center, 1, 1)
    return (
        mid * center
        + (z_p * z_pair[0] + z_m * z_pair[1])
        + (y_p * y_pair[0] + y_m * y_pair[1])
        + (x_p * plus_x + x_m * minus_x)
    )


def rotate(values, cos, sin):
    out = []
    for k in range(2):
        re, im = values[2 * k], values[2 * k + 1]
        out.append(re * cos[k] + im * sin[k])
        out.append(im * cos[k] - re * sin[k])
    return out


def beside(center, row_low, row_high):
    width = center.shape[0]
    plus = jnp.where(row_mask(center.shape, width - 1), row_high, pltpu.roll(center, width - 1, 0))
    minus = jnp.where(row_mask(center.shape, 0), row_low, pltpu.roll(center, 1, 0))
    return plus, minus


def phases(table, z):
    return [table[0, z + 1], table[1, z + 1]], [table[2, z + 1], table[3, z + 1]]


def first_kernel(table, magnet, pore, wall, acc, low, high, got_near, got_far, mid, vel, por, wal, mag, sems):
    depth, width, x_width = por.shape
    copies = [
        pltpu.make_async_copy(src, dst, sems.at[i])
        for i, (src, dst) in enumerate(((pore, por), (wall, wal), (magnet, mag)))
    ]
    for copy in copies:
        copy.start()
    for copy in copies:
        copy.wait()
    even = is_even()

    def layer(z, extra, plus, minus):
        moments = [acc[k, z + 1] for k in range(4)]
        if extra is not None:
            halo, sign = extra
            moments = [
                moments[0] + halo[0],
                moments[1] + sign * halo[0],
                moments[2] + halo[1],
                moments[3] + halo[2],
            ]
        pore_f = por[z].astype(jnp.float32)
        scale = pore_f / moments[0]
        speed = [m * scale for m in moments[1:]]
        for j in range(3):
            vel[j, z] = speed[j]
        coef = coefficients(speed, pore_f, wal[z].astype(jnp.float32))
        cos, sin = phases(table, z)
        values = []
        for k in range(4):
            center = mag[k, z]
            row_near = got_near[k, pl.ds(z, 1), :]
            row_far = got_far[k, pl.ds(z, 1), :]
            y_pair = beside(center, jnp.where(even, row_far, row_near), jnp.where(even, row_near, row_far))
            values.append(stencil(coef, center, (plus(k), minus(k)), y_pair, x_width))
        for k, value in enumerate(rotate(values, cos, sin)):
            mid[k, z] = value

    layer(0, (low, 1.0), lambda k: mag[k, 1], lambda k: low[7 + k])

    def inner(z, carry):
        layer(z, None, lambda k: mag[k, z + 1], lambda k: mag[k, z - 1])
        return carry

    lax.fori_loop(1, depth - 1, inner, 0, unroll=2)
    layer(depth - 1, (high, -1.0), lambda k: high[7 + k], lambda k: mag[k, depth - 2])


def second_kernel(
    table, wide, magnet, pore, wall, acc, low, high,
    near_m, far_m, near_w, far_w, got_near_m, got_far_m, got_near_w, got_far_w, mid_in, vel_in,
    vel_out, mag_out, sums, por, wal, inside, mid, vel, new, rows, sides, own, sems,
):
    depth, width, x_width = por.shape
    shape = (width, x_width)
    chunks = 3
    size = depth // chunks
    loads = [
        pltpu.make_async_copy(pore, por, sems.at[0]),
        pltpu.make_async_copy(wall, wal, sems.at[1]),
        pltpu.make_async_copy(magnet.at[:, pl.ds(0, 1)], inside.at[:, pl.ds(0, 1)], sems.at[2]),
        pltpu.make_async_copy(magnet.at[:, pl.ds(depth - 1, 1)], inside.at[:, pl.ds(1, 1)], sems.at[3]),
    ]
    for copy in loads:
        copy.start()
    even = is_even()
    for planes, mine_near, mine_far, near, far in (
        (slice(0, 10), near_m, far_m, got_near_m, got_far_m),
        (slice(10, 18), near_w, far_w, got_near_w, got_far_w),
    ):
        sides[0, planes] = jnp.where(even, far[...], near[...])
        sides[1, planes] = jnp.where(even, near[...], far[...])
        own[0, planes] = jnp.where(even, mine_far[...], mine_near[...])
        own[1, planes] = jnp.where(even, mine_near[...], mine_far[...])

    first = row_mask((depth, x_width), 0)
    final = row_mask((depth, x_width), depth - 1)
    cos = [jnp.concatenate([wide[k], wide[k]], axis=1) for k in range(2)]
    sin = [jnp.concatenate([wide[2 + k], wide[2 + k]], axis=1) for k in range(2)]

    def column(moments, cross, sign, pore_f, wall_f, center, ends, y_pair):
        density = moments(0) + cross(0)
        scale = pore_f / density
        speed = [
            (moments(1) + cross(1)) * scale,
            (moments(2) + sign * cross(0)) * scale,
            (moments(3) + cross(2)) * scale,
        ]
        coef = coefficients(speed, pore_f, wall_f)
        values = []
        for k in range(4):
            low_end, high_end = ends(k)
            mid_k = center(k)
            plus = jnp.where(final, high_end, pltpu.roll(mid_k, depth - 1, 0))
            minus = jnp.where(first, low_end, pltpu.roll(mid_k, 1, 0))
            values.append(stencil(coef, mid_k, (plus, minus), y_pair(k), x_width))
        return speed, rotate(values, cos, sin)

    for side, edge in ((0, 0), (1, width - 1)):
        face, mine = sides.at[side], own.at[side]
        sign = -1.0 if side == 0 else 1.0
        order = (lambda a, b: (a, b)) if side == 0 else (lambda a, b: (b, a))
        _, outer = column(
            lambda j: face[13 + j],
            lambda j: mine[10 + j],
            sign,
            face[8],
            face[9],
            lambda k: face[k],
            lambda k: (face[17, 6 + k : 7 + k, :], face[17, 10 + k : 11 + k, :]),
            lambda k: order(mine[k], face[4 + k]),
        )
        speed, border = column(
            lambda j: mine[13 + j],
            lambda j: face[10 + j],
            -sign,
            mine[8],
            mine[9],
            lambda k: mine[k],
            lambda k: (low[7 + k, edge : edge + 1, :], high[7 + k, edge : edge + 1, :]),
            lambda k: order(mine[4 + k], face[k]),
        )
        for k in range(4):
            rows[side, k] = outer[k]
        for k in range(4):
            rows[side, 4 + k] = border[k]
        for j in range(3):
            rows[side, 8 + j] = speed[j]

    for copy in loads:
        copy.wait()
    top = row_mask(shape, 0)
    bottom = row_mask(shape, width - 1)
    for halo, z, cross, base, corner, inner in ((low, -1, 0, 0, 6, 0), (high, depth, depth + 1, 3, 10, 1)):
        d_l, z_l, x_l = [sides[0, 17, base + j : base + j + 1, :] for j in range(3)]
        d_r, z_r, x_r = [sides[1, 17, base + j : base + j + 1, :] for j in range(3)]
        density = halo[3] + acc[0, cross] + jnp.where(top, d_l, jnp.where(bottom, d_r, 0.0))
        m_z = halo[4] + acc[1, cross] + jnp.where(top, z_l, jnp.where(bottom, z_r, 0.0))
        m_y = halo[5] + acc[2, cross] + jnp.where(top, d_l, jnp.where(bottom, -d_r, 0.0))
        m_x = halo[6] + acc[3, cross] + jnp.where(top, x_l, jnp.where(bottom, x_r, 0.0))
        scale = halo[15] / density
        coef = coefficients([m_z * scale, m_y * scale, m_x * scale], halo[15], halo[16])
        values = []
        for k in range(4):
            center = halo[7 + k]
            z_pair = (inside[k, inner], halo[11 + k])
            z_pair = z_pair if z < 0 else z_pair[::-1]
            at = slice(corner + k, corner + k + 1)
            y_pair = beside(center, sides[0, 17, at, :], sides[1, 17, at, :])
            values.append(stencil(coef, center, z_pair, y_pair, x_width))
        for k, value in enumerate(rotate(values, *phases(table, z))):
            mid[k, z + 1] = value

    def patched(layer, slot, at):
        return jnp.where(top, rows[0, slot, at, :], jnp.where(bottom, rows[1, slot, at, :], layer))

    def second(z, totals, final_layer=False):
        at = pl.ds(z, 1)
        speed = [patched(vel_in[j, z], 8 + j, at) for j in range(3)]
        for j in range(3):
            vel[j, z] = speed[j]
        coef = coefficients(speed, por[z].astype(jnp.float32), wal[z].astype(jnp.float32))
        values = []
        for k in range(4):
            center = mid[k, z + 1]
            if final_layer:
                plus = mid[k, z + 2]
            else:
                plus = patched(mid_in[k, z + 1], 4 + k, pl.ds(z + 1, 1))
                mid[k, z + 2] = plus
            y_pair = beside(center, rows[0, k, at, :], rows[1, k, at, :])
            values.append(stencil(coef, center, (plus, mid[k, z]), y_pair, x_width))
        values = rotate(values, *phases(table, z))
        for k in range(4):
            new[k, z] = values[k]
        return tuple(t + v for t, v in zip(totals, values))

    for k in range(4):
        mid[k, 1] = patched(mid_in[k, 0], 4 + k, pl.ds(0, 1))
    totals = (jnp.zeros(shape, jnp.float32),) * 4
    stores = []
    for c in range(chunks):
        ending = c == chunks - 1
        totals = lax.fori_loop(c * size, (c + 1) * size - (1 if ending else 0), second, totals, unroll=2)
        if ending:
            totals = second(depth - 1, totals, True)
        part = pl.ds(c * size, size)
        stores.append(pltpu.make_async_copy(new.at[:, part], mag_out.at[:, part], sems.at[4 + 2 * c]))
        stores.append(pltpu.make_async_copy(vel.at[:, part], vel_out.at[:, part], sems.at[5 + 2 * c]))
        stores[-2].start()
        stores[-1].start()
    sums[...] = jnp.zeros_like(sums)
    for k in range(4):
        line = jnp.sum(totals[k], axis=0, keepdims=True)
        sums[k : k + 1, :] = line[:, :128] + line[:, 128:]
    for copy in stores:
        copy.wait()


VMEM = pl.BlockSpec(memory_space=pltpu.VMEM)
SMEM = pl.BlockSpec(memory_space=pltpu.SMEM)
HBM = pl.BlockSpec(memory_space=pltpu.HBM)


def struct(*shape):
    return jax.ShapeDtypeStruct(shape, jnp.float32)


def floats(*shape):
    return pltpu.VMEM(shape, jnp.float32)


def ints(*shape):
    return pltpu.VMEM(shape, jnp.int32)


def params(mib):
    return pltpu.CompilerParams(vmem_limit_bytes=mib * MIB)


def edge_faces(pops, magnet, pore, wall):
    depth, width, x_width = pore.shape
    return pl.pallas_call(
        edge_kernel,
        in_specs=[HBM] * 4,
        out_specs=[VMEM] * 4,
        out_shape=[struct(18, width, x_width)] * 2 + [struct(10, depth, x_width)] * 2,
        scratch_shapes=[
            floats(19, 2, width, x_width),
            floats(19, 2, width, x_width),
            floats(4, depth, width, x_width),
            ints(depth, width, x_width),
            ints(depth, width, x_width),
            pltpu.SemaphoreType.DMA((5,)),
        ],
        compiler_params=params(60),
        name="edge_faces",
    )(pops, magnet, pore, wall)


def collide(pops, pore):
    depth, width, x_width = pore.shape
    chunks = 6 if depth % 12 == 0 else 1
    return pl.pallas_call(
        collide_kernel,
        in_specs=[HBM] * 2,
        out_specs=[VMEM] * 3,
        out_shape=[struct(4, depth + 2, width, x_width)] + [struct(8, depth, x_width)] * 2,
        scratch_shapes=[
            floats(19, depth, width, x_width),
            ints(depth, width, x_width),
            floats(2, 4, depth, x_width),
            pltpu.SemaphoreType.DMA((chunks + 1,)),
        ],
        compiler_params=params(48),
        cost_estimate=pl.CostEstimate(flops=20_000_000, bytes_accessed=12_000_000, transcendentals=0),
        name="collide",
    )(pops, pore)


def merge(low, high, up, down):
    return pl.pallas_call(
        merge_kernel,
        in_specs=[VMEM] * 4,
        out_specs=[VMEM] * 2,
        out_shape=[struct(*up.shape)] * 2,
        compiler_params=params(8),
        name="merge",
    )(low, high, up, down)


def first_step(table, magnet, pore, wall, acc, low, high, got_near, got_far):
    depth, width, x_width = pore.shape
    return pl.pallas_call(
        first_kernel,
        in_specs=[SMEM] + [HBM] * 3 + [VMEM] * 5,
        out_specs=[VMEM] * 2,
        out_shape=[struct(4, depth, width, x_width), struct(3, depth, width, x_width)],
        scratch_shapes=[
            ints(depth, width, x_width),
            ints(depth, width, x_width),
            floats(4, depth, width, x_width),
            pltpu.SemaphoreType.DMA((3,)),
        ],
        compiler_params=params(16),
        cost_estimate=pl.CostEstimate(flops=20_000_000, bytes_accessed=6_000_000, transcendentals=0),
        name="first_step",
    )(table, magnet, pore, wall, acc, low, high, got_near, got_far)


def second_step(table, wide, magnet, pore, wall, *rest):
    depth, width, x_width = pore.shape
    return pl.pallas_call(
        second_kernel,
        in_specs=[SMEM, VMEM] + [HBM] * 3 + [VMEM] * len(rest),
        out_specs=[HBM, HBM, VMEM],
        out_shape=[struct(3, depth, width, x_width), struct(4, depth, width, x_width), struct(8, 128)],
        scratch_shapes=[
            ints(depth, width, x_width),
            ints(depth, width, x_width),
            floats(4, 2, width, x_width),
            floats(4, depth + 2, width, x_width),
            floats(3, depth, width, x_width),
            floats(4, depth, width, x_width),
            floats(2, 11, depth, x_width),
            floats(2, 18, depth, x_width),
            floats(2, 18, depth, x_width),
            pltpu.SemaphoreType.DMA((10,)),
        ],
        compiler_params=params(24),
        name="second_step",
    )(table, wide, magnet, pore, wall, *rest)


def ring(value, axis, step):
    count = lax.axis_size(axis)
    return lax.ppermute(value, axis, [(i, (i + step) % count) for i in range(count)])


def swap(value, axis, near):
    count = lax.axis_size(axis)
    step = 1 if near else -1
    return lax.ppermute(value, axis, [(i, (i + (step if i % 2 == 0 else -step)) % count) for i in range(count)])


def phase_tables(start, depth, extent):
    layers = jnp.remainder(start + jnp.arange(-1, depth + 1, dtype=jnp.int32), extent)
    coords = layers.astype(jnp.float32)
    wave_numbers = jnp.array([Q_LOW, Q_HIGH], jnp.float32)
    angles = 2.0 * math.pi * wave_numbers[:, None] * coords[None, :] / extent
    return jnp.concatenate([jnp.cos(angles), jnp.sin(angles)], axis=0)


def sum_over(value, axis):
    count = lax.axis_size(axis)
    copies = jnp.broadcast_to(value[None], (count,) + value.shape)
    return jnp.sum(lax.all_to_all(copies, axis, 0, 0), axis=0)


def local(populations, magnetization, pore, wall):
    _, depth, width, x_width = populations.shape
    flow_count = lax.axis_size("flow")
    trans_count = lax.axis_size("trans")
    extent = depth * flow_count
    magnet = magnetization.reshape(4, depth, width, x_width)
    table = phase_tables(lax.axis_index("flow") * depth, depth, extent)
    wide = jnp.broadcast_to(table[:, 1:-1, None], (4, depth, 128))

    face_up, face_down, near_m, far_m = edge_faces(populations, magnet, pore, wall)
    low = ring(face_up, "flow", 1)
    high = ring(face_down, "flow", -1)
    got_near_m = swap(near_m, "trans", True)
    got_far_m = swap(far_m, "trans", False)
    acc, up, down = collide(populations, pore)
    near_w, far_w = merge(low, high, up, down)
    got_near_w = swap(near_w, "trans", True)
    got_far_w = swap(far_w, "trans", False)
    mid, vel = first_step(table, magnet, pore, wall, acc, low, high, got_near_m, got_far_m)
    velocity, magnet, sums = second_step(
        table, wide, magnet, pore, wall, acc, low, high,
        near_m, far_m, near_w, far_w, got_near_m, got_far_m, got_near_w, got_far_w, mid, vel,
    )
    sums = sum_over(sum_over(sums, "flow"), "trans")
    signal = jnp.sum(sums[:4], axis=1).reshape(2, 2) / math.sqrt(extent * width * trans_count * x_width)
    return (velocity, magnet.reshape(magnetization.shape), signal)


def solution(mesh):
    placed = (
        P(None, "flow", "trans", None),
        P(None, None, "flow", "trans", None),
        P("flow", "trans", None),
        P("flow", "trans", None),
    )
    return jax.shard_map(
        local,
        mesh=mesh,
        in_specs=placed,
        out_specs=(P(None, "flow", "trans", None), P(None, None, "flow", "trans", None), P()),
        check_vma=False,
    )
```

time: 160 us -> 62.5 us (0.39)
  blocking collectives: 76.9 us -> 26.2 us
  other arithmetic: 27.5 us -> 0.29 us
  Pallas kernels: 0 us -> 16.6 us
  local copies, waits for them, and re-layouts: 13.6 us -> 0.83 us
  waiting for transfers between devices: 16.6 us -> 3.84 us
  starting transfers between devices: 23.7 us -> 13.8 us
    psum x1 -> x0, blocking collectives: 76.9 us -> none  [local(): totals = lax.psum(local_sums, ('flow', 'trans'))]
    all_to_all x0 -> x2, blocking collectives: none -> 26.2 us  [sum_over(): return jnp.sum(lax.all_to_all(copies, axis, 0, 0), axis=0)]
    pallas_call x0 -> x5, Pallas kernels: none -> 16.6 us  [the longest x1 5.1 us: collide(): pl.pallas_call(collide_kernel, in_specs=[HBM] * 2, out_specs=[VMEM] * 3,...]
    ppermute x12 -> x6, waiting for transfers between devices: 16.6 us -> 3.84 us  [the longest x4 3.83 us: swap(): lax.ppermute(value, axis, [(i, (i + (step if i % 2 == 0 else -step)) % co...]
    unnamed x19 -> x0, other arithmetic: 10.1 us -> none
    ppermute x12 -> x6, starting transfers between devices: 23.7 us -> 13.8 us  [the longest x2 7.5 us: ring(): lax.ppermute(value, axis, [(i, (i + step) % count) for i in range(count)])]
    slice x24 -> x1, local copies, waits for them, and re-layouts: 7.1 us -> 0.07 us  [local(): wide = jnp.broadcast_to(table[:, 1:-1, None], (4, depth, 128))]
    sub x2 -> x0, other arithmetic: 5.56 us -> none  [torrey_step(): center + diffusion_step * laplace - advect - surface_relax * wall_f * center]
  transfers between devices with their start and end apart: 12 -> 6, of which waited for: 5 -> 2; matrix products, arithmetic and copies ran while one was open for 11% -> 0% of each run, Pallas kernels for 0% -> 13%
where the time goes in v2:
time: 62.5 us; the launch traced here: 62.3 us
  blocking collectives  26.2 us (42%)
  Pallas kernels  16.6 us (27%)
  starting transfers between devices  13.8 us (22%)
  waiting for transfers between devices  3.84 us (6%)
  local copies, waits for them, and re-layouts  0.83 us (1%)
  between operations  0.74 us (1%)
    all_to_all x2, blocking collectives, sum_over(): return jnp.sum(lax.all_to_all(copies, axis, 0, 0), axis=0)  26.2 us
    ppermute x2, starting transfers between devices, ring(): lax.ppermute(value, axis, [(i, (i + step) % count) for i in range(count)])  7.5 us
    ppermute x4, starting transfers between devices, swap(): lax.ppermute(value, axis, [(i, (i + (step if i % 2 == 0 else -step)) % co...  6.34 us
    pallas_call x1, Pallas kernels, collide(): pl.pallas_call(collide_kernel, in_specs=[HBM] * 2, out_specs=[VMEM] * 3,...  5.1 us
    pallas_call x1, Pallas kernels, second_step(): pl.pallas_call(second_kernel, in_specs=[SMEM, VMEM] + [HBM] * 3 + [VMEM]...  4.8 us
    ppermute x4, waiting for transfers between devices, swap(): lax.ppermute(value, axis, [(i, (i + (step if i % 2 == 0 else -step)) % co...  3.83 us
    pallas_call x1, Pallas kernels, edge_faces(): pl.pallas_call(edge_kernel, in_specs=[HBM] * 4, out_specs=[VMEM] * 4, out...  3.57 us
    pallas_call x1, Pallas kernels, first_step(): pl.pallas_call(first_kernel, in_specs=[SMEM] + [HBM] * 3 + [VMEM] * 5, ou...  3.06 us
  transfers between devices with their start and end apart: 6, of which 2 were waited for; matrix products, arithmetic and copies ran while one was open for 0% of the time, Pallas kernels for 13%

profile of v2, /device:TPU:1, one launch (start us, length us, event | category | flops | bytes accessed | tf_op | source)
XLA Modules:
  0.0 62.3 jit_solution(11522597167869237721)
XLA Ops:
  0.6 0.0 copy-start.1
  0.6 3.6 %edge_faces.1 = (f32[18,16,256]{2,1,0:T(8,128)}, f32[18,16,256]{2,1,0:T(8,128)}, f32[10,24,256]{2,1,0:T(8,128)}, f32[10,24,256]{2,1,0:T(8,128)}) custom-call(f32[19,24,16,256]{3,2,1,0:T(8,128)} %pops.3, f32[4,24,16,256]{3,2,1,0:T(8,128)} %bitcast.2, s32[24,16,256]{2,1,0:T(8,128)} %pore.7, s32[24,16,256]{2,1,0:T(8,128)} %wall.5), custom_call_target="tpu_custom_call" | custom-call | tf_op jit(solution)/shard_map/edge_faces/pallas_call | solution.py:530
  4.2 2.5 %collective-permute-start = (f32[18,16,256]{2,1,0:T(8,128)}, f32[18,16,256]{2,1,0:T(8,128)S(1)}, u32[]{:S(2)}, u32[]{:S(2)}) collective-permute-start(f32[18,16,256]{2,1,0:T(8,128)} %get-tuple-element.18), channel_id=1, source_target_pairs={{0,16},{16,32},{32,48},{48,64},{64,80},{80,96},{96,112},{112,128},... | collective-permute-start | bytes 884744 | tf_op jit(solution)/shard_map/ppermute | solution.py:624
  6.8 5.0 %collective-permute-start.1 = (f32[18,16,256]{2,1,0:T(8,128)}, f32[18,16,256]{2,1,0:T(8,128)S(1)}, u32[]{:S(2)}, u32[]{:S(2)}) collective-permute-start(f32[18,16,256]{2,1,0:T(8,128)} %get-tuple-element.19), channel_id=1, source_target_pairs={{0,240},{16,0},{32,16},{48,32},{64,48},{80,64},{96,80},{112,96},{1... | collective-permute-start | bytes 884744 | tf_op jit(solution)/shard_map/ppermute | solution.py:624
  11.7 1.0 %collective-permute-start.2 = (f32[10,24,256]{2,1,0:T(8,128)}, f32[10,24,256]{2,1,0:T(8,128)S(1)}, u32[]{:S(2)}, u32[]{:S(2)}) collective-permute-start(f32[10,24,256]{2,1,0:T(8,128)} %get-tuple-element.20.near_m), channel_id=1, source_target_pairs={{0,1},{1,0},{2,3},{3,2},{4,5},{5,4},{6,7},{7,6},{8,9},{9,8},{10,11... | collective-permute-start | bytes 737288 | tf_op jit(solution)/shard_map/ppermute | solution.py:630
  12.7 2.3 %collective-permute-start.3 = (f32[10,24,256]{2,1,0:T(8,128)}, f32[10,24,256]{2,1,0:T(8,128)S(1)}, u32[]{:S(2)}, u32[]{:S(2)}) collective-permute-start(f32[10,24,256]{2,1,0:T(8,128)} %get-tuple-element.21.far_m), channel_id=1, source_target_pairs={{0,15},{1,2},{2,1},{3,4},{4,3},{5,6},{6,5},{7,8},{8,7},{9,10},{10,... | collective-permute-start | bytes 737288 | tf_op jit(solution)/shard_map/ppermute | solution.py:630
  15.0 0.0 copy-done.1
  15.0 0.0 copy-start.5
  15.0 0.0 copy-start
  15.0 0.0 copy-start.2
  15.0 5.1 %collide.1 = (f32[4,26,16,256]{3,2,1,0:T(8,128)S(1)}, f32[8,24,256]{2,1,0:T(8,128)S(1)}, f32[8,24,256]{2,1,0:T(8,128)S(1)}) custom-call(f32[19,24,16,256]{3,2,1,0:T(8,128)} %pops.3, s32[24,16,256]{2,1,0:T(8,128)S(1)} %copy-done.1), custom_call_target="tpu_custom_call" | custom-call | flops 20000000 | bytes 12000000 | tf_op jit(solution)/shard_map/collide/pallas_call | solution.py:551
  20.1 0.0 collective-permute-done.low
  20.2 0.0 collective-permute-done.1.high
  20.2 0.1 merge.1
  20.2 3.0 %collective-permute-start.4 = (f32[8,24,256]{2,1,0:T(8,128)S(1)}, f32[8,24,256]{2,1,0:T(8,128)S(1)}, u32[]{:S(2)}, u32[]{:S(2)}) collective-permute-start(f32[8,24,256]{2,1,0:T(8,128)S(1)} %get-tuple-element.24.near_w), channel_id=1, source_target_pairs={{0,1},{1,0},{2,3},{3,2},{4,5},{5,4},{6,7},{7,6},{8,9},{9,8},{10,11... | collective-permute-start | bytes 589832 | tf_op jit(solution)/shard_map/ppermute | solution.py:630
  23.3 0.0 collective-permute-start.5
  23.3 0.0 copy-done.5
  23.3 0.1 fusion.1
  23.4 0.1 slice.6
  23.5 0.0 collective-permute-done.2.got_near.got_near_m
  23.5 2.7 %collective-permute-done.3.got_far.got_far_m = f32[10,24,256]{2,1,0:T(8,128)S(1)} collective-permute-done((f32[10,24,256]{2,1,0:T(8,128)}, f32[10,24,256]{2,1,0:T(8,128)S(1)}, u32[]{:S(2)}, u32[]{:S(2)}) %collective-permute-start.3) | collective-permute-done | bytes 245792 | tf_op jit(solution)/shard_map/ppermute | solution.py:630
  26.2 0.0 copy-done
  26.2 0.0 copy-done.2
  26.2 0.0 copy-start.3
  26.2 0.0 copy-start.4
  26.2 3.1 %first_step.1 = (f32[4,24,16,256]{3,2,1,0:T(8,128)S(1)}, f32[3,24,16,256]{3,2,1,0:T(8,128)S(1)}) custom-call(f32[4,26]{1,0:T(4,128)S(1)} %pad_maximum_fusion.table, f32[4,24,16,256]{3,2,1,0:T(8,128)S(1)} %bitcast.3, s32[24,16,256]{2,1,0:T(8,128)S(1)} %copy-done.1, s32[24,16,256]{2,1,0:T(8,128)S(1)} %copy-done.2, ...), custom_call_target="tpu_custom_call" | custom-call | flops 20000000 | bytes 6000000 | tf_op jit(solution)/shard_map/first_step/pallas_call | solution.py:581
  29.3 0.0 collective-permute-done.4.got_near_w
  29.3 1.2 %collective-permute-done.5.got_far_w = f32[8,24,256]{2,1,0:T(8,128)S(1)} collective-permute-done((f32[8,24,256]{2,1,0:T(8,128)S(1)}, f32[8,24,256]{2,1,0:T(8,128)S(1)}, u32[]{:S(2)}, u32[]{:S(2)}) %collective-permute-start.5) | collective-permute-done | bytes 196640 | tf_op jit(solution)/shard_map/ppermute | solution.py:630
  30.4 0.1 broadcast_in_dim.6.wide
  30.5 0.0 copy-done.3
  30.5 0.0 copy-done.4
  30.5 4.8 %second_step.1 = (f32[3,24,16,256]{3,2,1,0:T(8,128)}, f32[4,24,16,256]{3,2,1,0:T(8,128)}, f32[8,128]{1,0:T(8,128)S(1)}) custom-call(f32[4,26]{1,0:T(4,128)S(1)} %pad_maximum_fusion.table, f32[4,24,128]{2,1,0:T(8,128)S(1)} %broadcast_in_dim.6.wide, f32[4,24,16,256]{3,2,1,0:T(8,128)S(1)} %bitcast.4, s32[24,16,256]{2,1,0:T(8,128)S(1)} %copy-done.1, ...), custom_call_target="tpu_custom_call" | custom-call | tf_op jit(solution)/shard_map/second_step/pallas_call | solution.py:600
  35.3 11.9 %all_to_all.10 = f32[16,8,128]{2,1,0:T(8,128)S(1)} all-to-all(f32[16,8,128]{2,1,0:T(8,128)S(1)} %broadcast_in_dim.7), channel_id=1, replica_groups=mesh['flow'=16,'trans'=16] {'flow'}, dimensions={0} | all-to-all | bytes 131072 | tf_op jit(solution)/shard_map/all_to_all | solution.py:644
  47.3 14.3 %all_to_all.11 = f32[16,8,128]{2,1,0:T(8,128)S(1)} all-to-all(f32[16,8,128]{2,1,0:T(8,128)S(1)} %broadcast_in_dim.8), channel_id=1, replica_groups=mesh['flow'=16,'trans'=16] {'trans'}, dimensions={0} | all-to-all | bytes 131072 | tf_op jit(solution)/shard_map/all_to_all | solution.py:644
  61.6 0.1 slice_reduce_fusion
  61.7 0.6 %div.14 = f32[2,2]{1,0:T(2,128)} reshape(f32[4]{0:T(128)S(1)} %broadcast_multiply_fusion) | data formatting | bytes 32 | tf_op jit(solution)/shard_map/div | solution.py:671
  (7 shorter events, 0.1 us)
Async XLA Ops:
  0.6 14.4 %copy-start.1 = (s32[24,16,256]{2,1,0:T(8,128)S(1)}, s32[24,16,256]{2,1,0:T(8,128)}, u32[]{:S(2)}) copy-start(s32[24,16,256]{2,1,0:T(8,128)} %pore.7) | copy-start | bytes 1179652
  4.2 15.9 %collective-permute-start = (f32[18,16,256]{2,1,0:T(8,128)}, f32[18,16,256]{2,1,0:T(8,128)S(1)}, u32[]{:S(2)}, u32[]{:S(2)}) collective-permute-start(f32[18,16,256]{2,1,0:T(8,128)} %get-tuple-element.18), channel_id=1, source_target_pairs={{0,16},{16,32},{32,48},{48,64},{64,80},{80,96},{96,112},{112,128},... | collective-permute-start | bytes 884744 | tf_op jit(solution)/shard_map/ppermute | solution.py:624
  6.8 13.4 %collective-permute-start.1 = (f32[18,16,256]{2,1,0:T(8,128)}, f32[18,16,256]{2,1,0:T(8,128)S(1)}, u32[]{:S(2)}, u32[]{:S(2)}) collective-permute-start(f32[18,16,256]{2,1,0:T(8,128)} %get-tuple-element.19), channel_id=1, source_target_pairs={{0,240},{16,0},{32,16},{48,32},{64,48},{80,64},{96,80},{112,96},{1... | collective-permute-start | bytes 884744 | tf_op jit(solution)/shard_map/ppermute | solution.py:624
  11.7 11.8 %collective-permute-start.2 = (f32[10,24,256]{2,1,0:T(8,128)}, f32[10,24,256]{2,1,0:T(8,128)S(1)}, u32[]{:S(2)}, u32[]{:S(2)}) collective-permute-start(f32[10,24,256]{2,1,0:T(8,128)} %get-tuple-element.20.near_m), channel_id=1, source_target_pairs={{0,1},{1,0},{2,3},{3,2},{4,5},{5,4},{6,7},{7,6},{8,9},{9,8},{10,11... | collective-permute-start | bytes 737288 | tf_op jit(solution)/shard_map/ppermute | solution.py:630
  12.7 13.5 %collective-permute-start.3 = (f32[10,24,256]{2,1,0:T(8,128)}, f32[10,24,256]{2,1,0:T(8,128)S(1)}, u32[]{:S(2)}, u32[]{:S(2)}) collective-permute-start(f32[10,24,256]{2,1,0:T(8,128)} %get-tuple-element.21.far_m), channel_id=1, source_target_pairs={{0,15},{1,2},{2,1},{3,4},{4,3},{5,6},{6,5},{7,8},{8,7},{9,10},{10,... | collective-permute-start | bytes 737288 | tf_op jit(solution)/shard_map/ppermute | solution.py:630
  15.0 8.3 %copy-start.5 = (f32[2]{0:T(128)S(1)}, f32[2]{0:T(128)}, u32[]{:S(2)}) copy-start(f32[2]{0:T(128)} %constant.38) | copy-start | bytes 28
  15.0 11.2 %copy-start = (f32[2,2,24,16,256]{4,3,2,1,0:T(8,128)S(1)}, f32[2,2,24,16,256]{4,3,2,1,0:T(8,128)}, u32[]{:S(2)}) copy-start(f32[2,2,24,16,256]{4,3,2,1,0:T(8,128)} %param.6) | copy-start | bytes 4718596
  15.0 11.2 %copy-start.2 = (s32[24,16,256]{2,1,0:T(8,128)S(1)}, s32[24,16,256]{2,1,0:T(8,128)}, u32[]{:S(2)}) copy-start(s32[24,16,256]{2,1,0:T(8,128)} %wall.5) | copy-start | bytes 1179652
  20.2 9.0 %collective-permute-start.4 = (f32[8,24,256]{2,1,0:T(8,128)S(1)}, f32[8,24,256]{2,1,0:T(8,128)S(1)}, u32[]{:S(2)}, u32[]{:S(2)}) collective-permute-start(f32[8,24,256]{2,1,0:T(8,128)S(1)} %get-tuple-element.24.near_w), channel_id=1, source_target_pairs={{0,1},{1,0},{2,3},{3,2},{4,5},{5,4},{6,7},{7,6},{8,9},{9,8},{10,11... | collective-permute-start | bytes 589832 | tf_op jit(solution)/shard_map/ppermute | solution.py:630
  23.3 7.1 %collective-permute-start.5 = (f32[8,24,256]{2,1,0:T(8,128)S(1)}, f32[8,24,256]{2,1,0:T(8,128)S(1)}, u32[]{:S(2)}, u32[]{:S(2)}) collective-permute-start(f32[8,24,256]{2,1,0:T(8,128)S(1)} %get-tuple-element.25.far_w), channel_id=1, source_target_pairs={{0,15},{1,2},{2,1},{3,4},{4,3},{5,6},{6,5},{7,8},{8,7},{9,10},{10,... | collective-permute-start | bytes 589832 | tf_op jit(solution)/shard_map/ppermute | solution.py:630
  26.2 4.3 %copy-start.3 = (f32[10,24,256]{2,1,0:T(8,128)S(1)}, f32[10,24,256]{2,1,0:T(8,128)}, u32[]{:S(2)}) copy-start(f32[10,24,256]{2,1,0:T(8,128)} %get-tuple-element.20.near_m) | copy-start | bytes 737284
  26.2 4.3 %copy-start.4 = (f32[10,24,256]{2,1,0:T(8,128)S(1)}, f32[10,24,256]{2,1,0:T(8,128)}, u32[]{:S(2)}) copy-start(f32[10,24,256]{2,1,0:T(8,128)} %get-tuple-element.21.far_m) | copy-start | bytes 737284

commit v3 on v2

--- a/solution.py
+++ b/solution.py
@@ -23,8 +23,8 @@
     return lax.broadcasted_iota(jnp.int32, shape, 0) == row
 
 
-def is_even():
-    return lax.rem(lax.axis_index("trans"), 2) == 0
+def is_even(axis):
+    return lax.rem(lax.axis_index(axis), 2) == 0
 
 
 def collide_layer(pop, pore):
@@ -99,19 +99,22 @@
     return above, here, below, edges
 
 
-def edge_kernel(pops, magnet, pore, wall, up, down, near, far, low_p, high_p, mag, por, wal, sems):
+def edge_kernel(
+    pops, magnet, pore, wall, z_near, z_far, y_near, y_far, low_p, high_p, mag, por, wal, up, down, left, right, sems
+):
     depth, width = por.shape[:2]
-    copies = [
-        pltpu.make_async_copy(pops.at[:, pl.ds(depth - 2, 2)], high_p, sems.at[0]),
-        pltpu.make_async_copy(pops.at[:, pl.ds(0, 2)], low_p, sems.at[1]),
-        pltpu.make_async_copy(pore, por, sems.at[2]),
-        pltpu.make_async_copy(wall, wal, sems.at[3]),
-        pltpu.make_async_copy(magnet, mag, sems.at[4]),
+    pairs = [
+        (pops.at[:, pl.ds(depth - 2, 2)], high_p),
+        (pore, por),
+        (pops.at[:, pl.ds(0, 2)], low_p),
+        (wall, wal),
+        (magnet, mag),
     ]
+    copies = [pltpu.make_async_copy(src, dst, sems.at[i]) for i, (src, dst) in enumerate(pairs)]
     for copy in copies:
         copy.start()
-    copies[2].wait()
-    for face, held, copy, border, behind in ((up, high_p, 0, 1, 0), (down, low_p, 1, 0, 1)):
+    copies[1].wait()
+    for face, held, copy, border, behind in ((up, high_p, 0, 1, 0), (down, low_p, 2, 0, 1)):
         copies[copy].wait()
         first = depth - 2 if face is up else 0
 
@@ -136,37 +139,52 @@
             face[17, at + 1 : at + 2, :] = edges[side][0] + edges_in[side][diag]
             face[17, at + 2 : at + 3, :] = sign * edges_in[side][diag]
             face[17, at + 3 : at + 4, :] = edges[side][1]
-    copies[3].wait()
-    copies[4].wait()
-    for face, border, behind in ((up, depth - 1, depth - 2), (down, 0, 1)):
-        face[7:11] = mag[:, border]
-        face[11:15] = mag[:, behind]
-        face[15] = por[border].astype(jnp.float32)
-        face[16] = wal[border].astype(jnp.float32)
-
-    def rows(face, border, behind):
-        def layer(z, carry):
-            at = pl.ds(z, 1)
+        if face is up:
+            copies[3].wait()
+            copies[4].wait()
+        at, back = (depth - 1, depth - 2) if face is up else (0, 1)
+        face[7:11] = mag[:, at]
+        face[11:15] = mag[:, back]
+        face[15] = por[at].astype(jnp.float32)
+        face[16] = wal[at].astype(jnp.float32)
+
+    def send(even, src, if_even, if_odd, sem):
+        to_even = pltpu.make_async_copy(src, if_even, sem)
+        to_odd = pltpu.make_async_copy(src, if_odd, sem)
+
+        @pl.when(even)
+        def _():
+            to_even.start()
+
+        @pl.when(jnp.logical_not(even))
+        def _():
+            to_odd.start()
+
+        return to_even
+
+    even_z, even_y = is_even("flow"), is_even("trans")
+    sent = [
+        send(even_z, up, z_near, z_far, sems.at[5]),
+        send(even_z, down, z_far, z_near, sems.at[6]),
+    ]
+
+    def rows(z, carry):
+        at = pl.ds(z, 1)
+        for face, border, behind in ((right, width - 1, width - 2), (left, 0, 1)):
             for k in range(4):
                 face[k, at, :] = mag[k, z, border : border + 1, :]
                 face[4 + k, at, :] = mag[k, z, behind : behind + 1, :]
             face[8, at, :] = por[z, border : border + 1, :].astype(jnp.float32)
             face[9, at, :] = wal[z, border : border + 1, :].astype(jnp.float32)
-            return carry
-
-        lax.fori_loop(0, depth, layer, 0, unroll=2)
-
-    even = is_even()
-
-    @pl.when(even)
-    def _():
-        rows(near, width - 1, width - 2)
-        rows(far, 0, 1)
-
-    @pl.when(jnp.logical_not(even))
-    def _():
-        rows(near, 0, 1)
-        rows(far, width - 1, width - 2)
+        return carry
+
+    lax.fori_loop(0, depth, rows, 0, unroll=2)
+    sent += [
+        send(even_y, right, y_near, y_far, sems.at[7]),
+        send(even_y, left, y_far, y_near, sems.at[8]),
+    ]
+    for copy in sent:
+        copy.wait()
 
 
 def collide_kernel(pops, pore, acc, up, down, held, por, rows, sems):
@@ -228,9 +246,12 @@
     lax.fori_loop(0, depth, border, 0, unroll=2)
 
 
-def merge_kernel(low, high, up, down, near, far):
+def merge_kernel(got_near, got_far, up, down, near, far, low, high):
     depth = up.shape[1]
     width = low.shape[1]
+    even_z = is_even("flow")
+    low[...] = jnp.where(even_z, got_far[...], got_near[...])
+    high[...] = jnp.where(even_z, got_near[...], got_far[...])
 
     def put(face, own, side, edge):
         face[...] = own[...]
@@ -252,7 +273,7 @@
             for k in range(4):
                 face[7, corner + k : corner + k + 1, :] = halo[7 + k, edge : edge + 1, :]
 
-    even = is_even()
+    even = is_even("trans")
 
     @pl.when(even)
     def _():
@@ -304,7 +325,9 @@
     return [table[0, z + 1], table[1, z + 1]], [table[2, z + 1], table[3, z + 1]]
 
 
-def first_kernel(table, magnet, pore, wall, acc, low, high, got_near, got_far, mid, vel, por, wal, mag, sems):
+def first_kernel(
+    table, magnet, pore, wall, acc, low, high, near_m, far_m, near_w, far_w, mid, vel, own, por, wal, mag, sems
+):
     depth, width, x_width = por.shape
     copies = [
         pltpu.make_async_copy(src, dst, sems.at[i])
@@ -312,9 +335,12 @@
     ]
     for copy in copies:
         copy.start()
+    even = is_even("trans")
+    for planes, near, far in ((slice(0, 10), near_m, far_m), (slice(10, 18), near_w, far_w)):
+        own[0, planes] = jnp.where(even, far[...], near[...])
+        own[1, planes] = jnp.where(even, near[...], far[...])
     for copy in copies:
         copy.wait()
-    even = is_even()
 
     def layer(z, extra, plus, minus):
         moments = [acc[k, z + 1] for k in range(4)]
@@ -336,9 +362,7 @@
         values = []
         for k in range(4):
             center = mag[k, z]
-            row_near = got_near[k, pl.ds(z, 1), :]
-            row_far = got_far[k, pl.ds(z, 1), :]
-            y_pair = beside(center, jnp.where(even, row_far, row_near), jnp.where(even, row_near, row_far))
+            y_pair = (pltpu.roll(center, width - 1, 0), pltpu.roll(center, 1, 0))
             values.append(stencil(coef, center, (plus(k), minus(k)), y_pair, x_width))
         for k, value in enumerate(rotate(values, cos, sin)):
             mid[k, z] = value
@@ -355,12 +379,12 @@
 
 def second_kernel(
     table, wide, magnet, pore, wall, acc, low, high,
-    near_m, far_m, near_w, far_w, got_near_m, got_far_m, got_near_w, got_far_w, mid_in, vel_in,
-    vel_out, mag_out, sums, por, wal, inside, mid, vel, new, rows, sides, own, sems,
+    own, got_near_m, got_far_m, got_near, got_far, mid_in, vel_in,
+    vel_out, mag_out, sums, por, wal, inside, mid, vel, new, rows, beside_m, beside_w, sems,
 ):
     depth, width, x_width = por.shape
     shape = (width, x_width)
-    chunks = 3
+    chunks = 6 if depth % 6 == 0 else 1
     size = depth // chunks
     loads = [
         pltpu.make_async_copy(pore, por, sems.at[0]),
@@ -370,15 +394,10 @@
     ]
     for copy in loads:
         copy.start()
-    even = is_even()
-    for planes, mine_near, mine_far, near, far in (
-        (slice(0, 10), near_m, far_m, got_near_m, got_far_m),
-        (slice(10, 18), near_w, far_w, got_near_w, got_far_w),
-    ):
-        sides[0, planes] = jnp.where(even, far[...], near[...])
-        sides[1, planes] = jnp.where(even, near[...], far[...])
-        own[0, planes] = jnp.where(even, mine_far[...], mine_near[...])
-        own[1, planes] = jnp.where(even, mine_near[...], mine_far[...])
+    even = is_even("trans")
+    for pair, near, far in ((beside_m, got_near_m, got_far_m), (beside_w, got_near, got_far)):
+        pair[0] = jnp.where(even, far[...], near[...])
+        pair[1] = jnp.where(even, near[...], far[...])
 
     first = row_mask((depth, x_width), 0)
     final = row_mask((depth, x_width), depth - 1)
@@ -404,22 +423,22 @@
         return speed, rotate(values, cos, sin)
 
     for side, edge in ((0, 0), (1, width - 1)):
-        face, mine = sides.at[side], own.at[side]
+        face, mine, late = beside_m.at[side], own.at[side], beside_w.at[side]
         sign = -1.0 if side == 0 else 1.0
         order = (lambda a, b: (a, b)) if side == 0 else (lambda a, b: (b, a))
         _, outer = column(
-            lambda j: face[13 + j],
+            lambda j: late[3 + j],
             lambda j: mine[10 + j],
             sign,
             face[8],
             face[9],
             lambda k: face[k],
-            lambda k: (face[17, 6 + k : 7 + k, :], face[17, 10 + k : 11 + k, :]),
+            lambda k: (late[7, 6 + k : 7 + k, :], late[7, 10 + k : 11 + k, :]),
             lambda k: order(mine[k], face[4 + k]),
         )
         speed, border = column(
             lambda j: mine[13 + j],
-            lambda j: face[10 + j],
+            lambda j: late[j],
             -sign,
             mine[8],
             mine[9],
@@ -439,8 +458,8 @@
     top = row_mask(shape, 0)
     bottom = row_mask(shape, width - 1)
     for halo, z, cross, base, corner, inner in ((low, -1, 0, 0, 6, 0), (high, depth, depth + 1, 3, 10, 1)):
-        d_l, z_l, x_l = [sides[0, 17, base + j : base + j + 1, :] for j in range(3)]
-        d_r, z_r, x_r = [sides[1, 17, base + j : base + j + 1, :] for j in range(3)]
+        d_l, z_l, x_l = [beside_w[0, 7, base + j : base + j + 1, :] for j in range(3)]
+        d_r, z_r, x_r = [beside_w[1, 7, base + j : base + j + 1, :] for j in range(3)]
         density = halo[3] + acc[0, cross] + jnp.where(top, d_l, jnp.where(bottom, d_r, 0.0))
         m_z = halo[4] + acc[1, cross] + jnp.where(top, z_l, jnp.where(bottom, z_r, 0.0))
         m_y = halo[5] + acc[2, cross] + jnp.where(top, d_l, jnp.where(bottom, -d_r, 0.0))
@@ -453,7 +472,7 @@
             z_pair = (inside[k, inner], halo[11 + k])
             z_pair = z_pair if z < 0 else z_pair[::-1]
             at = slice(corner + k, corner + k + 1)
-            y_pair = beside(center, sides[0, 17, at, :], sides[1, 17, at, :])
+            y_pair = beside(center, beside_w[0, 7, at, :], beside_w[1, 7, at, :])
             values.append(stencil(coef, center, z_pair, y_pair, x_width))
         for k, value in enumerate(rotate(values, *phases(table, z))):
             mid[k, z + 1] = value
@@ -496,10 +515,12 @@
         stores.append(pltpu.make_async_copy(vel.at[:, part], vel_out.at[:, part], sems.at[5 + 2 * c]))
         stores[-2].start()
         stores[-1].start()
-    sums[...] = jnp.zeros_like(sums)
+    lane = lax.broadcasted_iota(jnp.int32, sums.shape, 1)
+    row = jnp.zeros(sums.shape, jnp.float32)
     for k in range(4):
         line = jnp.sum(totals[k], axis=0, keepdims=True)
-        sums[k : k + 1, :] = line[:, :128] + line[:, 128:]
+        row = jnp.where(lane == k, jnp.sum(line, axis=1, keepdims=True), row)
+    sums[...] = row
     for copy in stores:
         copy.wait()
 
@@ -530,7 +551,7 @@
     return pl.pallas_call(
         edge_kernel,
         in_specs=[HBM] * 4,
-        out_specs=[VMEM] * 4,
+        out_specs=[HBM] * 4,
         out_shape=[struct(18, width, x_width)] * 2 + [struct(10, depth, x_width)] * 2,
         scratch_shapes=[
             floats(19, 2, width, x_width),
@@ -538,7 +559,11 @@
             floats(4, depth, width, x_width),
             ints(depth, width, x_width),
             ints(depth, width, x_width),
-            pltpu.SemaphoreType.DMA((5,)),
+            floats(18, width, x_width),
+            floats(18, width, x_width),
+            floats(10, depth, x_width),
+            floats(10, depth, x_width),
+            pltpu.SemaphoreType.DMA((9,)),
         ],
         compiler_params=params(60),
         name="edge_faces",
@@ -565,24 +590,28 @@
     )(pops, pore)
 
 
-def merge(low, high, up, down):
+def merge(got_near, got_far, up, down):
     return pl.pallas_call(
         merge_kernel,
         in_specs=[VMEM] * 4,
-        out_specs=[VMEM] * 2,
-        out_shape=[struct(*up.shape)] * 2,
+        out_specs=[VMEM] * 4,
+        out_shape=[struct(*up.shape)] * 2 + [struct(*got_near.shape)] * 2,
         compiler_params=params(8),
         name="merge",
-    )(low, high, up, down)
-
-
-def first_step(table, magnet, pore, wall, acc, low, high, got_near, got_far):
+    )(got_near, got_far, up, down)
+
+
+def first_step(table, magnet, pore, wall, acc, low, high, *faces):
     depth, width, x_width = pore.shape
     return pl.pallas_call(
         first_kernel,
-        in_specs=[SMEM] + [HBM] * 3 + [VMEM] * 5,
-        out_specs=[VMEM] * 2,
-        out_shape=[struct(4, depth, width, x_width), struct(3, depth, width, x_width)],
+        in_specs=[SMEM] + [HBM] * 3 + [VMEM] * (3 + len(faces)),
+        out_specs=[VMEM] * 3,
+        out_shape=[
+            struct(4, depth, width, x_width),
+            struct(3, depth, width, x_width),
+            struct(2, 18, depth, x_width),
+        ],
         scratch_shapes=[
             ints(depth, width, x_width),
             ints(depth, width, x_width),
@@ -592,7 +621,7 @@
         compiler_params=params(16),
         cost_estimate=pl.CostEstimate(flops=20_000_000, bytes_accessed=6_000_000, transcendentals=0),
         name="first_step",
-    )(table, magnet, pore, wall, acc, low, high, got_near, got_far)
+    )(table, magnet, pore, wall, acc, low, high, *faces)
 
 
 def second_step(table, wide, magnet, pore, wall, *rest):
@@ -601,7 +630,7 @@
         second_kernel,
         in_specs=[SMEM, VMEM] + [HBM] * 3 + [VMEM] * len(rest),
         out_specs=[HBM, HBM, VMEM],
-        out_shape=[struct(3, depth, width, x_width), struct(4, depth, width, x_width), struct(8, 128)],
+        out_shape=[struct(3, depth, width, x_width), struct(4, depth, width, x_width), struct(1, 128)],
         scratch_shapes=[
             ints(depth, width, x_width),
             ints(depth, width, x_width),
@@ -610,18 +639,13 @@
             floats(3, depth, width, x_width),
             floats(4, depth, width, x_width),
             floats(2, 11, depth, x_width),
-            floats(2, 18, depth, x_width),
-            floats(2, 18, depth, x_width),
-            pltpu.SemaphoreType.DMA((10,)),
+            floats(2, 10, depth, x_width),
+            floats(2, 8, depth, x_width),
+            pltpu.SemaphoreType.DMA((16,)),
         ],
         compiler_params=params(24),
         name="second_step",
     )(table, wide, magnet, pore, wall, *rest)
-
-
-def ring(value, axis, step):
-    count = lax.axis_size(axis)
-    return lax.ppermute(value, axis, [(i, (i + step) % count) for i in range(count)])
 
 
 def swap(value, axis, near):
@@ -638,10 +662,10 @@
     return jnp.concatenate([jnp.cos(angles), jnp.sin(angles)], axis=0)
 
 
-def sum_over(value, axis):
-    count = lax.axis_size(axis)
+def sum_over(value, axes):
+    count = math.prod(lax.axis_size(axis) for axis in axes)
     copies = jnp.broadcast_to(value[None], (count,) + value.shape)
-    return jnp.sum(lax.all_to_all(copies, axis, 0, 0), axis=0)
+    return jnp.sum(lax.all_to_all(copies, axes, 0, 0), axis=(0, 1))
 
 
 def local(populations, magnetization, pore, wall):
@@ -653,22 +677,22 @@
     table = phase_tables(lax.axis_index("flow") * depth, depth, extent)
     wide = jnp.broadcast_to(table[:, 1:-1, None], (4, depth, 128))
 
-    face_up, face_down, near_m, far_m = edge_faces(populations, magnet, pore, wall)
-    low = ring(face_up, "flow", 1)
-    high = ring(face_down, "flow", -1)
+    near_z, far_z, near_m, far_m = edge_faces(populations, magnet, pore, wall)
+    got_near_z = swap(near_z, "flow", True)
+    got_far_z = swap(far_z, "flow", False)
     got_near_m = swap(near_m, "trans", True)
     got_far_m = swap(far_m, "trans", False)
     acc, up, down = collide(populations, pore)
-    near_w, far_w = merge(low, high, up, down)
+    near_w, far_w, low, high = merge(got_near_z, got_far_z, up, down)
     got_near_w = swap(near_w, "trans", True)
     got_far_w = swap(far_w, "trans", False)
-    mid, vel = first_step(table, magnet, pore, wall, acc, low, high, got_near_m, got_far_m)
+    mid, vel, own = first_step(table, magnet, pore, wall, acc, low, high, near_m, far_m, near_w, far_w)
     velocity, magnet, sums = second_step(
         table, wide, magnet, pore, wall, acc, low, high,
-        near_m, far_m, near_w, far_w, got_near_m, got_far_m, got_near_w, got_far_w, mid, vel,
+        own, got_near_m, got_far_m, got_near_w, got_far_w, mid, vel,
     )
-    sums = sum_over(sum_over(sums, "flow"), "trans")
-    signal = jnp.sum(sums[:4], axis=1).reshape(2, 2) / math.sqrt(extent * width * trans_count * x_width)
+    totals = sum_over(sums, ("flow", "trans"))
+    signal = totals[:4].reshape(2, 2) / math.sqrt(extent * width * trans_count * x_width)
     return (velocity, magnet.reshape(magnetization.shape), signal)
 
 

time: 62.5 us -> 58.4 us (0.934)
  blocking collectives: 26.2 us -> 21.7 us
  starting transfers between devices: 13.8 us -> 14.8 us
    ppermute x4 -> x6, starting transfers between devices: 6.34 us -> 14.8 us  [swap(): lax.ppermute(value, axis, [(i, (i + (step if i % 2 == 0 else -step)) % co...]
    ppermute x2 -> x0, starting transfers between devices: 7.5 us -> none  [ring(): lax.ppermute(value, axis, [(i, (i + step) % count) for i in range(count)])]
    all_to_all x2 -> x1, blocking collectives: 26.2 us -> 21.7 us  [sum_over(): return jnp.sum(lax.all_to_all(copies, axes, 0, 0), axis=(0, 1))]
    ppermute x4 -> x6, waiting for transfers between devices: 3.83 us -> 3.61 us  [swap(): lax.ppermute(value, axis, [(i, (i + (step if i % 2 == 0 else -step)) % co...]
  transfers between devices with their start and end apart: 6 -> 6, of which waited for: 2 -> 1; matrix products, arithmetic and copies ran while one was open for 0% -> 0% of each run, Pallas kernels for 13% -> 14%
where the time goes in v3:
time: 58.4 us; the launch traced here: 58.3 us
  blocking collectives  21.7 us (37%)
  Pallas kernels  16.3 us (28%)
  starting transfers between devices  14.8 us (25%)
  waiting for transfers between devices  3.61 us (6%)
  local copies, waits for them, and re-layouts  0.88 us (2%)
  between operations  0.77 us (1%)
    all_to_all x1, blocking collectives, sum_over(): return jnp.sum(lax.all_to_all(copies, axes, 0, 0), axis=(0, 1))  21.7 us
    ppermute x6, starting transfers between devices, swap(): lax.ppermute(value, axis, [(i, (i + (step if i % 2 == 0 else -step)) % co...  14.8 us
    pallas_call x1, Pallas kernels, collide(): pl.pallas_call(collide_kernel, in_specs=[HBM] * 2, out_specs=[VMEM] * 3,...  5.11 us
    pallas_call x1, Pallas kernels, second_step(): pl.pallas_call(second_kernel, in_specs=[SMEM, VMEM] + [HBM] * 3 + [VMEM]...  4.53 us
    ppermute x6, waiting for transfers between devices, swap(): lax.ppermute(value, axis, [(i, (i + (step if i % 2 == 0 else -step)) % co...  3.61 us
    pallas_call x1, Pallas kernels, edge_faces(): pl.pallas_call(edge_kernel, in_specs=[HBM] * 4, out_specs=[HBM] * 4, out_...  3.49 us
    pallas_call x1, Pallas kernels, first_step(): pl.pallas_call(first_kernel, in_specs=[SMEM] + [HBM] * 3 + [VMEM] * (3 +...  3.03 us
  transfers between devices with their start and end apart: 6, of which 1 were waited for; matrix products, arithmetic and copies ran while one was open for 0% of the time, Pallas kernels for 14%

profile of v3, /device:TPU:1, one launch (start us, length us, event | category | flops | bytes accessed | tf_op | source)
XLA Modules:
  0.0 58.3 jit_solution(1078878432535990260)
XLA Ops:
  0.6 0.0 copy-start.1
  0.6 3.5 %edge_faces.1 = (f32[18,16,256]{2,1,0:T(8,128)}, f32[18,16,256]{2,1,0:T(8,128)}, f32[10,24,256]{2,1,0:T(8,128)}, f32[10,24,256]{2,1,0:T(8,128)}) custom-call(f32[19,24,16,256]{3,2,1,0:T(8,128)} %pops.3, f32[4,24,16,256]{3,2,1,0:T(8,128)} %bitcast.4, s32[24,16,256]{2,1,0:T(8,128)} %pore.7, s32[24,16,256]{2,1,0:T(8,128)} %wall.5), custom_call_target="tpu_custom_call" | custom-call | tf_op jit(solution)/shard_map/edge_faces/pallas_call | solution.py:551
  4.1 2.6 %collective-permute-start = (f32[18,16,256]{2,1,0:T(8,128)}, f32[18,16,256]{2,1,0:T(8,128)S(1)}, u32[]{:S(2)}, u32[]{:S(2)}) collective-permute-start(f32[18,16,256]{2,1,0:T(8,128)} %get-tuple-element.21), channel_id=1, source_target_pairs={{0,16},{16,0},{32,48},{48,32},{64,80},{80,64},{96,112},{112,96},{1... | collective-permute-start | bytes 884744 | tf_op jit(solution)/shard_map/ppermute | solution.py:654
  6.7 5.6 %collective-permute-start.1 = (f32[18,16,256]{2,1,0:T(8,128)}, f32[18,16,256]{2,1,0:T(8,128)S(1)}, u32[]{:S(2)}, u32[]{:S(2)}) collective-permute-start(f32[18,16,256]{2,1,0:T(8,128)} %get-tuple-element.22), channel_id=1, source_target_pairs={{0,240},{16,32},{32,16},{48,64},{64,48},{80,96},{96,80},{112,128},... | collective-permute-start | bytes 884744 | tf_op jit(solution)/shard_map/ppermute | solution.py:654
  12.3 1.2 %collective-permute-start.2 = (f32[10,24,256]{2,1,0:T(8,128)}, f32[10,24,256]{2,1,0:T(8,128)S(1)}, u32[]{:S(2)}, u32[]{:S(2)}) collective-permute-start(f32[10,24,256]{2,1,0:T(8,128)} %get-tuple-element.27.near_m), channel_id=1, source_target_pairs={{0,1},{1,0},{2,3},{3,2},{4,5},{5,4},{6,7},{7,6},{8,9},{9,8},{10,11... | collective-permute-start | bytes 737288 | tf_op jit(solution)/shard_map/ppermute | solution.py:654
  13.5 2.3 %collective-permute-start.3 = (f32[10,24,256]{2,1,0:T(8,128)}, f32[10,24,256]{2,1,0:T(8,128)S(1)}, u32[]{:S(2)}, u32[]{:S(2)}) collective-permute-start(f32[10,24,256]{2,1,0:T(8,128)} %get-tuple-element.28.far_m), channel_id=1, source_target_pairs={{0,15},{1,2},{2,1},{3,4},{4,3},{5,6},{6,5},{7,8},{8,7},{9,10},{10,... | collective-permute-start | bytes 737288 | tf_op jit(solution)/shard_map/ppermute | solution.py:654
  15.8 0.0 copy-done.1
  15.8 0.0 copy-start.5
  15.8 0.0 copy-start
  15.9 0.0 copy-start.2
  15.9 0.0 copy-start.3
  15.9 0.0 copy-start.4
  15.9 5.1 %collide.1 = (f32[4,26,16,256]{3,2,1,0:T(8,128)S(1)}, f32[8,24,256]{2,1,0:T(8,128)S(1)}, f32[8,24,256]{2,1,0:T(8,128)S(1)}) custom-call(f32[19,24,16,256]{3,2,1,0:T(8,128)} %pops.3, s32[24,16,256]{2,1,0:T(8,128)S(1)} %copy-done.1), custom_call_target="tpu_custom_call" | custom-call | flops 20000000 | bytes 12000000 | tf_op jit(solution)/shard_map/collide/pallas_call | solution.py:576
  21.0 0.0 collective-permute-done.got_near
  21.0 0.0 collective-permute-done.1.got_far
  21.0 0.1 merge.1
  21.2 3.0 %collective-permute-start.4 = (f32[8,24,256]{2,1,0:T(8,128)S(1)}, f32[8,24,256]{2,1,0:T(8,128)S(1)}, u32[]{:S(2)}, u32[]{:S(2)}) collective-permute-start(f32[8,24,256]{2,1,0:T(8,128)S(1)} %get-tuple-element.29.near_w), channel_id=1, source_target_pairs={{0,1},{1,0},{2,3},{3,2},{4,5},{5,4},{6,7},{7,6},{8,9},{9,8},{10,11... | collective-permute-start | bytes 589832 | tf_op jit(solution)/shard_map/ppermute | solution.py:654
  24.2 0.0 collective-permute-start.5
  24.2 0.0 copy-done.5
  24.2 0.1 fusion.1
  24.4 0.1 slice.14
  24.4 0.0 copy-done
  24.4 0.0 copy-done.2
  24.4 0.0 copy-done.3
  24.4 0.0 copy-done.4
  24.4 3.0 %first_step.1 = (f32[4,24,16,256]{3,2,1,0:T(8,128)S(1)}, f32[3,24,16,256]{3,2,1,0:T(8,128)S(1)}, f32[2,18,24,256]{3,2,1,0:T(8,128)S(1)}) custom-call(f32[4,26]{1,0:T(4,128)S(1)} %pad_maximum_fusion.table, f32[4,24,16,256]{3,2,1,0:T(8,128)S(1)} %bitcast.5, s32[24,16,256]{2,1,0:T(8,128)S(1)} %copy-done.1, s32[24,16,256]{2,1,0:T(8,128)S(1)} %copy-done.2, ...), custom_call_target="tpu_custom_call" | custom-call | flops 20000000 | bytes 6000000 | tf_op jit(solution)/shard_map/first_step/pallas_call | solution.py:606
  27.5 0.0 collective-permute-done.2.got_near_m
  27.5 0.0 collective-permute-done.3.got_far_m
  27.5 0.0 collective-permute-done.4.got_near
  27.5 3.6 %collective-permute-done.5.got_far = f32[8,24,256]{2,1,0:T(8,128)S(1)} collective-permute-done((f32[8,24,256]{2,1,0:T(8,128)S(1)}, f32[8,24,256]{2,1,0:T(8,128)S(1)}, u32[]{:S(2)}, u32[]{:S(2)}) %collective-permute-start.5) | collective-permute-done | bytes 196640 | tf_op jit(solution)/shard_map/ppermute | solution.py:654
  31.1 0.1 broadcast_in_dim.6.wide
  31.2 4.5 %second_step.1 = (f32[3,24,16,256]{3,2,1,0:T(8,128)}, f32[4,24,16,256]{3,2,1,0:T(8,128)}, f32[1,128]{1,0:T(1,128)S(1)}) custom-call(f32[4,26]{1,0:T(4,128)S(1)} %pad_maximum_fusion.table, f32[4,24,128]{2,1,0:T(8,128)S(1)} %broadcast_in_dim.6.wide, f32[4,24,16,256]{3,2,1,0:T(8,128)S(1)} %bitcast.6, s32[24,16,256]{2,1,0:T(8,128)S(1)} %copy-done.1, ...), custom_call_target="tpu_custom_call" | custom-call | tf_op jit(solution)/shard_map/second_step/pallas_call | solution.py:629
  35.7 0.1 broadcast_in_dim.8
  35.8 21.7 %all_to_all.5 = f32[256,1,128]{2,1,0:T(1,128)S(1)} all-to-all(f32[256,1,128]{2,1,0:T(1,128)S(1)} %broadcast_in_dim.8), channel_id=1, replica_groups=mesh['flow'=16,'trans'=16] {'flow','trans'}, dimensions={0} | all-to-all | bytes 262144 | tf_op jit(solution)/shard_map/all_to_all | solution.py:668
  57.6 0.6 %div.14 = f32[2,2]{1,0:T(2,128)} reshape(f32[4]{0:T(128)S(1)} %slice_multiply_fusion) | data formatting | bytes 32 | tf_op jit(solution)/shard_map/div | solution.py:695
  (4 shorter events, 0.1 us)
Async XLA Ops:
  0.6 15.2 %copy-start.1 = (s32[24,16,256]{2,1,0:T(8,128)S(1)}, s32[24,16,256]{2,1,0:T(8,128)}, u32[]{:S(2)}) copy-start(s32[24,16,256]{2,1,0:T(8,128)} %pore.7) | copy-start | bytes 1179652
  4.1 16.9 %collective-permute-start = (f32[18,16,256]{2,1,0:T(8,128)}, f32[18,16,256]{2,1,0:T(8,128)S(1)}, u32[]{:S(2)}, u32[]{:S(2)}) collective-permute-start(f32[18,16,256]{2,1,0:T(8,128)} %get-tuple-element.21), channel_id=1, source_target_pairs={{0,16},{16,0},{32,48},{48,32},{64,80},{80,64},{96,112},{112,96},{1... | collective-permute-start | bytes 884744 | tf_op jit(solution)/shard_map/ppermute | solution.py:654
  6.7 14.3 %collective-permute-start.1 = (f32[18,16,256]{2,1,0:T(8,128)}, f32[18,16,256]{2,1,0:T(8,128)S(1)}, u32[]{:S(2)}, u32[]{:S(2)}) collective-permute-start(f32[18,16,256]{2,1,0:T(8,128)} %get-tuple-element.22), channel_id=1, source_target_pairs={{0,240},{16,32},{32,16},{48,64},{64,48},{80,96},{96,80},{112,128},... | collective-permute-start | bytes 884744 | tf_op jit(solution)/shard_map/ppermute | solution.py:654
  12.3 15.2 %collective-permute-start.2 = (f32[10,24,256]{2,1,0:T(8,128)}, f32[10,24,256]{2,1,0:T(8,128)S(1)}, u32[]{:S(2)}, u32[]{:S(2)}) collective-permute-start(f32[10,24,256]{2,1,0:T(8,128)} %get-tuple-element.27.near_m), channel_id=1, source_target_pairs={{0,1},{1,0},{2,3},{3,2},{4,5},{5,4},{6,7},{7,6},{8,9},{9,8},{10,11... | collective-permute-start | bytes 737288 | tf_op jit(solution)/shard_map/ppermute | solution.py:654
  13.5 14.0 %collective-permute-start.3 = (f32[10,24,256]{2,1,0:T(8,128)}, f32[10,24,256]{2,1,0:T(8,128)S(1)}, u32[]{:S(2)}, u32[]{:S(2)}) collective-permute-start(f32[10,24,256]{2,1,0:T(8,128)} %get-tuple-element.28.far_m), channel_id=1, source_target_pairs={{0,15},{1,2},{2,1},{3,4},{4,3},{5,6},{6,5},{7,8},{8,7},{9,10},{10,... | collective-permute-start | bytes 737288 | tf_op jit(solution)/shard_map/ppermute | solution.py:654
  15.8 8.4 %copy-start.5 = (f32[2]{0:T(128)S(1)}, f32[2]{0:T(128)}, u32[]{:S(2)}) copy-start(f32[2]{0:T(128)} %constant.38) | copy-start | bytes 28
  15.8 8.6 %copy-start = (f32[2,2,24,16,256]{4,3,2,1,0:T(8,128)S(1)}, f32[2,2,24,16,256]{4,3,2,1,0:T(8,128)}, u32[]{:S(2)}) copy-start(f32[2,2,24,16,256]{4,3,2,1,0:T(8,128)} %param.6) | copy-start | bytes 4718596
  15.9 8.6 %copy-start.2 = (s32[24,16,256]{2,1,0:T(8,128)S(1)}, s32[24,16,256]{2,1,0:T(8,128)}, u32[]{:S(2)}) copy-start(s32[24,16,256]{2,1,0:T(8,128)} %wall.5) | copy-start | bytes 1179652
  15.9 8.6 %copy-start.3 = (f32[10,24,256]{2,1,0:T(8,128)S(1)}, f32[10,24,256]{2,1,0:T(8,128)}, u32[]{:S(2)}) copy-start(f32[10,24,256]{2,1,0:T(8,128)} %get-tuple-element.28.far_m) | copy-start | bytes 737284
  15.9 8.6 %copy-start.4 = (f32[10,24,256]{2,1,0:T(8,128)S(1)}, f32[10,24,256]{2,1,0:T(8,128)}, u32[]{:S(2)}) copy-start(f32[10,24,256]{2,1,0:T(8,128)} %get-tuple-element.27.near_m) | copy-start | bytes 737284
  21.2 6.3 %collective-permute-start.4 = (f32[8,24,256]{2,1,0:T(8,128)S(1)}, f32[8,24,256]{2,1,0:T(8,128)S(1)}, u32[]{:S(2)}, u32[]{:S(2)}) collective-permute-start(f32[8,24,256]{2,1,0:T(8,128)S(1)} %get-tuple-element.29.near_w), channel_id=1, source_target_pairs={{0,1},{1,0},{2,3},{3,2},{4,5},{5,4},{6,7},{7,6},{8,9},{9,8},{10,11... | collective-permute-start | bytes 589832 | tf_op jit(solution)/shard_map/ppermute | solution.py:654
  24.2 6.9 %collective-permute-start.5 = (f32[8,24,256]{2,1,0:T(8,128)S(1)}, f32[8,24,256]{2,1,0:T(8,128)S(1)}, u32[]{:S(2)}, u32[]{:S(2)}) collective-permute-start(f32[8,24,256]{2,1,0:T(8,128)S(1)} %get-tuple-element.30.far_w), channel_id=1, source_target_pairs={{0,15},{1,2},{2,1},{3,4},{4,3},{5,6},{6,5},{7,8},{8,7},{9,10},{10,... | collective-permute-start | bytes 589832 | tf_op jit(solution)/shard_map/ppermute | solution.py:654

commit v4 on v3

--- a/solution.py
+++ b/solution.py
@@ -325,8 +325,13 @@
     return [table[0, z + 1], table[1, z + 1]], [table[2, z + 1], table[3, z + 1]]
 
 
-def first_kernel(
-    table, magnet, pore, wall, acc, low, high, near_m, far_m, near_w, far_w, mid, vel, own, por, wal, mag, sems
+def turned_pair(center):
+    return pltpu.roll(center, center.shape[0] - 1, 0), pltpu.roll(center, 1, 0)
+
+
+def inner_kernel(
+    table, magnet, pore, wall, acc, low, high, near_m, far_m, near_w, far_w,
+    vel_out, new_out, own, inner, ends, part, por, wal, mag, mid, vel, new, sems,
 ):
     depth, width, x_width = por.shape
     copies = [
@@ -341,6 +346,17 @@
         own[1, planes] = jnp.where(even, near[...], far[...])
     for copy in copies:
         copy.wait()
+
+    def step(z, speed, pore_f, wall_f, center, plus, minus, put):
+        coef = coefficients(speed, pore_f, wall_f)
+        values = []
+        for k in range(4):
+            mid_k = center(k)
+            values.append(stencil(coef, mid_k, (plus(k), minus(k)), turned_pair(mid_k), x_width))
+        values = rotate(values, *phases(table, z))
+        for k in range(4):
+            put[k, z + 1 if put is mid else z] = values[k]
+        return values
 
     def layer(z, extra, plus, minus):
         moments = [acc[k, z + 1] for k in range(4)]
@@ -357,40 +373,79 @@
         speed = [m * scale for m in moments[1:]]
         for j in range(3):
             vel[j, z] = speed[j]
-        coef = coefficients(speed, pore_f, wal[z].astype(jnp.float32))
-        cos, sin = phases(table, z)
-        values = []
-        for k in range(4):
-            center = mag[k, z]
-            y_pair = (pltpu.roll(center, width - 1, 0), pltpu.roll(center, 1, 0))
-            values.append(stencil(coef, center, (plus(k), minus(k)), y_pair, x_width))
-        for k, value in enumerate(rotate(values, cos, sin)):
-            mid[k, z] = value
+        step(z, speed, pore_f, wal[z].astype(jnp.float32), lambda k: mag[k, z], plus, minus, mid)
+
+    for halo, z, cross, border in ((low, -1, 0, 0), (high, depth, depth + 1, depth - 1)):
+        scale = halo[15] / (halo[3] + acc[0, cross])
+        speed = [(halo[4 + j] + acc[1 + j, cross]) * scale for j in range(3)]
+        towards, behind = (lambda k: mag[k, border]), (lambda k: halo[11 + k])
+        pair = (towards, behind) if z < 0 else (behind, towards)
+        step(z, speed, halo[15], halo[16], lambda k: halo[7 + k], *pair, mid)
 
     layer(0, (low, 1.0), lambda k: mag[k, 1], lambda k: low[7 + k])
 
-    def inner(z, carry):
+    def middle(z, carry):
         layer(z, None, lambda k: mag[k, z + 1], lambda k: mag[k, z - 1])
         return carry
 
-    lax.fori_loop(1, depth - 1, inner, 0, unroll=2)
+    lax.fori_loop(1, depth - 1, middle, 0, unroll=2)
     layer(depth - 1, (high, -1.0), lambda k: high[7 + k], lambda k: mag[k, depth - 2])
 
-
-def second_kernel(
-    table, wide, magnet, pore, wall, acc, low, high,
-    own, got_near_m, got_far_m, got_near, got_far, mid_in, vel_in,
-    vel_out, mag_out, sums, por, wal, inside, mid, vel, new, rows, beside_m, beside_w, sems,
-):
-    depth, width, x_width = por.shape
-    shape = (width, x_width)
+    def second(z, totals):
+        speed = [vel[j, z] for j in range(3)]
+        pore_f, wall_f = por[z].astype(jnp.float32), wal[z].astype(jnp.float32)
+        values = step(
+            z, speed, pore_f, wall_f, lambda k: mid[k, z + 1], lambda k: mid[k, z + 2], lambda k: mid[k, z], new
+        )
+        return tuple(t + v for t, v in zip(totals, values))
+
     chunks = 6 if depth % 6 == 0 else 1
     size = depth // chunks
+    totals = (jnp.zeros((width, x_width), jnp.float32),) * 4
+    stores = [pltpu.make_async_copy(vel, vel_out, sems.at[3])]
+    stores[0].start()
+    for c in range(chunks):
+        totals = lax.fori_loop(c * size, (c + 1) * size, second, totals, unroll=2)
+        at = pl.ds(c * size, size)
+        stores.append(pltpu.make_async_copy(new.at[:, at], new_out.at[:, at], sems.at[4 + c]))
+        stores[-1].start()
+
+    def rows(z, carry):
+        at = pl.ds(z, 1)
+        for side, one, two in ((0, 1, 2), (1, width - 2, width - 3)):
+            for k in range(4):
+                inner[side, k, at, :] = mid[k, z + 1, one : one + 1, :]
+                inner[side, 4 + k, at, :] = mid[k, z + 1, two : two + 1, :]
+            for j in range(3):
+                inner[side, 8 + j, at, :] = vel[j, z, one : one + 1, :]
+            inner[side, 11, at, :] = por[z, one : one + 1, :].astype(jnp.float32)
+            inner[side, 12, at, :] = wal[z, one : one + 1, :].astype(jnp.float32)
+        return carry
+
+    lax.fori_loop(0, depth, rows, 0, unroll=2)
+    line = lax.broadcasted_iota(jnp.int32, (width, x_width), 0)
+    kept = jnp.logical_and(line >= 2, line < width - 2)
+    part[...] = jnp.zeros_like(part)
+    for k in range(4):
+        for side, one in ((0, 1), (1, width - 2)):
+            ends[side, k : k + 1, :] = mid[k, 0, one : one + 1, :]
+            ends[side, 4 + k : 5 + k, :] = mid[k, depth + 1, one : one + 1, :]
+        part[k : k + 1, :] = jnp.sum(jnp.where(kept, totals[k], 0.0), axis=0, keepdims=True)
+    for copy in stores:
+        copy.wait()
+
+
+def border_kernel(
+    table, wide, magnet, acc, low, high, own, inner, ends, part,
+    got_near_m, got_far_m, got_near, got_far, vel_in, new_in,
+    vel_out, mag_out, sums, inside, beside_m, beside_w, speeds, rows, corners, sems,
+):
+    depth, x_width = own.shape[2:]
+    width = low.shape[1]
+    shape = (width, x_width)
     loads = [
-        pltpu.make_async_copy(pore, por, sems.at[0]),
-        pltpu.make_async_copy(wall, wal, sems.at[1]),
-        pltpu.make_async_copy(magnet.at[:, pl.ds(0, 1)], inside.at[:, pl.ds(0, 1)], sems.at[2]),
-        pltpu.make_async_copy(magnet.at[:, pl.ds(depth - 1, 1)], inside.at[:, pl.ds(1, 1)], sems.at[3]),
+        pltpu.make_async_copy(magnet.at[:, pl.ds(0, 1)], inside.at[:, pl.ds(0, 1)], sems.at[0]),
+        pltpu.make_async_copy(magnet.at[:, pl.ds(depth - 1, 1)], inside.at[:, pl.ds(1, 1)], sems.at[1]),
     ]
     for copy in loads:
         copy.start()
@@ -404,42 +459,44 @@
     cos = [jnp.concatenate([wide[k], wide[k]], axis=1) for k in range(2)]
     sin = [jnp.concatenate([wide[2 + k], wide[2 + k]], axis=1) for k in range(2)]
 
-    def column(moments, cross, sign, pore_f, wall_f, center, ends, y_pair):
-        density = moments(0) + cross(0)
-        scale = pore_f / density
-        speed = [
+    def column(speed, pore_f, wall_f, center, end, y_pair):
+        coef = coefficients(speed, pore_f, wall_f)
+        values = []
+        for k in range(4):
+            low_end, high_end = end(k)
+            mid_k = center(k)
+            plus = jnp.where(final, high_end, pltpu.roll(mid_k, depth - 1, 0))
+            minus = jnp.where(first, low_end, pltpu.roll(mid_k, 1, 0))
+            values.append(stencil(coef, mid_k, (plus, minus), y_pair(k), x_width))
+        return rotate(values, cos, sin)
+
+    def flow(moments, cross, sign, pore_f):
+        scale = pore_f / (moments(0) + cross(0))
+        return [
             (moments(1) + cross(1)) * scale,
             (moments(2) + sign * cross(0)) * scale,
             (moments(3) + cross(2)) * scale,
         ]
-        coef = coefficients(speed, pore_f, wall_f)
-        values = []
-        for k in range(4):
-            low_end, high_end = ends(k)
-            mid_k = center(k)
-            plus = jnp.where(final, high_end, pltpu.roll(mid_k, depth - 1, 0))
-            minus = jnp.where(first, low_end, pltpu.roll(mid_k, 1, 0))
-            values.append(stencil(coef, mid_k, (plus, minus), y_pair(k), x_width))
-        return speed, rotate(values, cos, sin)
-
-    for side, edge in ((0, 0), (1, width - 1)):
+
+    edges = (0, width - 1)
+    orders = ((lambda a, b: (a, b)), (lambda a, b: (b, a)))
+    stores = []
+    for side, edge in enumerate(edges):
         face, mine, late = beside_m.at[side], own.at[side], beside_w.at[side]
         sign = -1.0 if side == 0 else 1.0
-        order = (lambda a, b: (a, b)) if side == 0 else (lambda a, b: (b, a))
-        _, outer = column(
-            lambda j: late[3 + j],
-            lambda j: mine[10 + j],
-            sign,
+        order = orders[side]
+        speed = flow(lambda j: late[3 + j], lambda j: mine[10 + j], sign, face[8])
+        outer = column(
+            speed,
             face[8],
             face[9],
             lambda k: face[k],
             lambda k: (late[7, 6 + k : 7 + k, :], late[7, 10 + k : 11 + k, :]),
             lambda k: order(mine[k], face[4 + k]),
         )
-        speed, border = column(
-            lambda j: mine[13 + j],
-            lambda j: late[j],
-            -sign,
+        speed = flow(lambda j: mine[13 + j], lambda j: late[j], -sign, mine[8])
+        border = column(
+            speed,
             mine[8],
             mine[9],
             lambda k: mine[k],
@@ -447,17 +504,18 @@
             lambda k: order(mine[4 + k], face[k]),
         )
         for k in range(4):
-            rows[side, k] = outer[k]
-        for k in range(4):
-            rows[side, 4 + k] = border[k]
+            rows[side, 0, k] = outer[k]
+            rows[side, 1, k] = border[k]
         for j in range(3):
-            rows[side, 8 + j] = speed[j]
+            speeds[side, j] = speed[j]
+        stores.append(pltpu.make_async_copy(speeds.at[side], vel_out.at[:, :, edge], sems.at[2 + side]))
+        stores[-1].start()
 
     for copy in loads:
         copy.wait()
     top = row_mask(shape, 0)
     bottom = row_mask(shape, width - 1)
-    for halo, z, cross, base, corner, inner in ((low, -1, 0, 0, 6, 0), (high, depth, depth + 1, 3, 10, 1)):
+    for halo, z, cross, base, corner, at_end in ((low, -1, 0, 0, 6, 0), (high, depth, depth + 1, 3, 10, 1)):
         d_l, z_l, x_l = [beside_w[0, 7, base + j : base + j + 1, :] for j in range(3)]
         d_r, z_r, x_r = [beside_w[1, 7, base + j : base + j + 1, :] for j in range(3)]
         density = halo[3] + acc[0, cross] + jnp.where(top, d_l, jnp.where(bottom, d_r, 0.0))
@@ -469,58 +527,52 @@
         values = []
         for k in range(4):
             center = halo[7 + k]
-            z_pair = (inside[k, inner], halo[11 + k])
+            z_pair = (inside[k, at_end], halo[11 + k])
             z_pair = z_pair if z < 0 else z_pair[::-1]
             at = slice(corner + k, corner + k + 1)
             y_pair = beside(center, beside_w[0, 7, at, :], beside_w[1, 7, at, :])
             values.append(stencil(coef, center, z_pair, y_pair, x_width))
         for k, value in enumerate(rotate(values, *phases(table, z))):
-            mid[k, z + 1] = value
-
-    def patched(layer, slot, at):
-        return jnp.where(top, rows[0, slot, at, :], jnp.where(bottom, rows[1, slot, at, :], layer))
-
-    def second(z, totals, final_layer=False):
-        at = pl.ds(z, 1)
-        speed = [patched(vel_in[j, z], 8 + j, at) for j in range(3)]
-        for j in range(3):
-            vel[j, z] = speed[j]
-        coef = coefficients(speed, por[z].astype(jnp.float32), wal[z].astype(jnp.float32))
-        values = []
-        for k in range(4):
-            center = mid[k, z + 1]
-            if final_layer:
-                plus = mid[k, z + 2]
-            else:
-                plus = patched(mid_in[k, z + 1], 4 + k, pl.ds(z + 1, 1))
-                mid[k, z + 2] = plus
-            y_pair = beside(center, rows[0, k, at, :], rows[1, k, at, :])
-            values.append(stencil(coef, center, (plus, mid[k, z]), y_pair, x_width))
-        values = rotate(values, *phases(table, z))
-        for k in range(4):
-            new[k, z] = values[k]
-        return tuple(t + v for t, v in zip(totals, values))
-
+            for side, edge in enumerate(edges):
+                at = 4 * at_end + k
+                corners[side, at : at + 1, :] = value[edge : edge + 1]
+
+    totals = [part[k : k + 1, :] for k in range(4)]
+    for side, edge in enumerate(edges):
+        mine, own_in, order = own.at[side], inner.at[side], orders[side]
+        for row, values in enumerate(
+            (
+                column(
+                    [speeds[side, j] for j in range(3)],
+                    mine[8],
+                    mine[9],
+                    lambda k: rows[side, 1, k],
+                    lambda k: (corners[side, k : k + 1, :], corners[side, 4 + k : 5 + k, :]),
+                    lambda k: order(own_in[k], rows[side, 0, k]),
+                ),
+                column(
+                    [own_in[8 + j] for j in range(3)],
+                    own_in[11],
+                    own_in[12],
+                    lambda k: own_in[k],
+                    lambda k: (ends[side, k : k + 1, :], ends[side, 4 + k : 5 + k, :]),
+                    lambda k: order(own_in[4 + k], rows[side, 1, k]),
+                ),
+            )
+        ):
+            for k in range(4):
+                rows[side, 2 + row, k] = values[k]
+                totals[k] = totals[k] + jnp.sum(values[k], axis=0, keepdims=True)
+            at = edge + (row if side == 0 else -row)
+            stores.append(
+                pltpu.make_async_copy(rows.at[side, 2 + row], mag_out.at[:, :, at], sems.at[4 + 2 * side + row])
+            )
+            stores[-1].start()
+    lane = lax.broadcasted_iota(jnp.int32, sums.shape, 1)
+    line = jnp.zeros(sums.shape, jnp.float32)
     for k in range(4):
-        mid[k, 1] = patched(mid_in[k, 0], 4 + k, pl.ds(0, 1))
-    totals = (jnp.zeros(shape, jnp.float32),) * 4
-    stores = []
-    for c in range(chunks):
-        ending = c == chunks - 1
-        totals = lax.fori_loop(c * size, (c + 1) * size - (1 if ending else 0), second, totals, unroll=2)
-        if ending:
-            totals = second(depth - 1, totals, True)
-        part = pl.ds(c * size, size)
-        stores.append(pltpu.make_async_copy(new.at[:, part], mag_out.at[:, part], sems.at[4 + 2 * c]))
-        stores.append(pltpu.make_async_copy(vel.at[:, part], vel_out.at[:, part], sems.at[5 + 2 * c]))
-        stores[-2].start()
-        stores[-1].start()
-    lane = lax.broadcasted_iota(jnp.int32, sums.shape, 1)
-    row = jnp.zeros(sums.shape, jnp.float32)
-    for k in range(4):
-        line = jnp.sum(totals[k], axis=0, keepdims=True)
-        row = jnp.where(lane == k, jnp.sum(line, axis=1, keepdims=True), row)
-    sums[...] = row
+        line = jnp.where(lane == k, jnp.sum(totals[k], axis=1, keepdims=True), line)
+    sums[...] = line
     for copy in stores:
         copy.wait()
 
@@ -601,51 +653,56 @@
     )(got_near, got_far, up, down)
 
 
-def first_step(table, magnet, pore, wall, acc, low, high, *faces):
+def inner_steps(table, magnet, pore, wall, acc, low, high, *faces):
     depth, width, x_width = pore.shape
     return pl.pallas_call(
-        first_kernel,
+        inner_kernel,
         in_specs=[SMEM] + [HBM] * 3 + [VMEM] * (3 + len(faces)),
-        out_specs=[VMEM] * 3,
+        out_specs=[HBM] * 2 + [VMEM] * 4,
         out_shape=[
+            struct(3, depth, width, x_width),
             struct(4, depth, width, x_width),
-            struct(3, depth, width, x_width),
             struct(2, 18, depth, x_width),
+            struct(2, 13, depth, x_width),
+            struct(2, 8, x_width),
+            struct(8, x_width),
         ],
         scratch_shapes=[
             ints(depth, width, x_width),
             ints(depth, width, x_width),
             floats(4, depth, width, x_width),
-            pltpu.SemaphoreType.DMA((3,)),
-        ],
-        compiler_params=params(16),
-        cost_estimate=pl.CostEstimate(flops=20_000_000, bytes_accessed=6_000_000, transcendentals=0),
-        name="first_step",
-    )(table, magnet, pore, wall, acc, low, high, *faces)
-
-
-def second_step(table, wide, magnet, pore, wall, *rest):
-    depth, width, x_width = pore.shape
-    return pl.pallas_call(
-        second_kernel,
-        in_specs=[SMEM, VMEM] + [HBM] * 3 + [VMEM] * len(rest),
-        out_specs=[HBM, HBM, VMEM],
-        out_shape=[struct(3, depth, width, x_width), struct(4, depth, width, x_width), struct(1, 128)],
-        scratch_shapes=[
-            ints(depth, width, x_width),
-            ints(depth, width, x_width),
-            floats(4, 2, width, x_width),
             floats(4, depth + 2, width, x_width),
             floats(3, depth, width, x_width),
             floats(4, depth, width, x_width),
-            floats(2, 11, depth, x_width),
+            pltpu.SemaphoreType.DMA((10,)),
+        ],
+        compiler_params=params(24),
+        cost_estimate=pl.CostEstimate(flops=40_000_000, bytes_accessed=9_000_000, transcendentals=0),
+        name="inner_steps",
+    )(table, magnet, pore, wall, acc, low, high, *faces)
+
+
+def border_rows(table, wide, magnet, *rest):
+    depth, width, x_width = magnet.shape[1:]
+    count = len(rest) - 2
+    return pl.pallas_call(
+        border_kernel,
+        in_specs=[SMEM, VMEM, HBM] + [VMEM] * count + [HBM] * 2,
+        out_specs=[HBM, HBM, VMEM],
+        out_shape=[struct(3, depth, width, x_width), struct(4, depth, width, x_width), struct(1, 128)],
+        input_output_aliases={3 + count: 0, 4 + count: 1},
+        scratch_shapes=[
+            floats(4, 2, width, x_width),
             floats(2, 10, depth, x_width),
             floats(2, 8, depth, x_width),
-            pltpu.SemaphoreType.DMA((16,)),
+            floats(2, 3, depth, x_width),
+            floats(2, 4, 4, depth, x_width),
+            floats(2, 8, x_width),
+            pltpu.SemaphoreType.DMA((8,)),
         ],
-        compiler_params=params(24),
-        name="second_step",
-    )(table, wide, magnet, pore, wall, *rest)
+        compiler_params=params(16),
+        name="border_rows",
+    )(table, wide, magnet, *rest)
 
 
 def swap(value, axis, near):
@@ -686,10 +743,12 @@
     near_w, far_w, low, high = merge(got_near_z, got_far_z, up, down)
     got_near_w = swap(near_w, "trans", True)
     got_far_w = swap(far_w, "trans", False)
-    mid, vel, own = first_step(table, magnet, pore, wall, acc, low, high, near_m, far_m, near_w, far_w)
-    velocity, magnet, sums = second_step(
-        table, wide, magnet, pore, wall, acc, low, high,
-        own, got_near_m, got_far_m, got_near_w, got_far_w, mid, vel,
+    velocity, magnet_out, own, inner, ends, part = inner_steps(
+        table, magnet, pore, wall, acc, low, high, near_m, far_m, near_w, far_w
+    )
+    velocity, magnet, sums = border_rows(
+        table, wide, magnet, acc, low, high, own, inner, ends, part,
+        got_near_m, got_far_m, got_near_w, got_far_w, velocity, magnet_out,
     )
     totals = sum_over(sums, ("flow", "trans"))
     signal = totals[:4].reshape(2, 2) / math.sqrt(extent * width * trans_count * x_width)

time: 58.4 us -> 56.3 us (0.964)
  waiting for transfers between devices: 3.61 us -> 0.88 us
  Pallas kernels: 16.3 us -> 17 us
    ppermute x6, waiting for transfers between devices: 3.61 us -> 0.88 us  [swap(): lax.ppermute(value, axis, [(i, (i + (step if i % 2 == 0 else -step)) % co...]
    pallas_call x2, Pallas kernels: 7.56 us -> 8.24 us  [the longest x1 5.77 us: inner_steps(): pl.pallas_call(inner_kernel, in_specs=[SMEM] + [HBM] * 3 + [VMEM] * (3 +...]
  transfers between devices with their start and end apart: 6 -> 6, of which waited for: 1 -> 1; matrix products, arithmetic and copies ran while one was open for 0% -> 0% of each run, Pallas kernels for 14% -> 20%
where the time goes in v4:
time: 56.3 us; the launch traced here: 56.2 us
  blocking collectives  21.7 us (39%)
  Pallas kernels  17 us (30%)
  starting transfers between devices  14.8 us (26%)
  local copies, waits for them, and re-layouts  0.88 us (2%)
  waiting for transfers between devices  0.88 us (2%)
  between operations  0.77 us (1%)
    all_to_all x1, blocking collectives, sum_over(): return jnp.sum(lax.all_to_all(copies, axes, 0, 0), axis=(0, 1))  21.7 us
    ppermute x6, starting transfers between devices, swap(): lax.ppermute(value, axis, [(i, (i + (step if i % 2 == 0 else -step)) % co...  14.8 us
    pallas_call x1, Pallas kernels, inner_steps(): pl.pallas_call(inner_kernel, in_specs=[SMEM] + [HBM] * 3 + [VMEM] * (3 +...  5.77 us
    pallas_call x1, Pallas kernels, collide(): pl.pallas_call(collide_kernel, in_specs=[HBM] * 2, out_specs=[VMEM] * 3,...  5.11 us
    pallas_call x1, Pallas kernels, edge_faces(): pl.pallas_call(edge_kernel, in_specs=[HBM] * 4, out_specs=[HBM] * 4, out_...  3.49 us
    pallas_call x1, Pallas kernels, border_rows(): pl.pallas_call(border_kernel, in_specs=[SMEM, VMEM, HBM] + [VMEM] * count...  2.47 us
  transfers between devices with their start and end apart: 6, of which 1 were waited for; matrix products, arithmetic and copies ran while one was open for 0% of the time, Pallas kernels for 20%

profile of v4, /device:TPU:1, one launch (start us, length us, event | category | flops | bytes accessed | tf_op | source)
XLA Modules:
  0.0 56.2 jit_solution(5184132032774865556)
XLA Ops:
  0.6 0.0 copy-start.1
  0.6 3.5 %edge_faces.1 = (f32[18,16,256]{2,1,0:T(8,128)}, f32[18,16,256]{2,1,0:T(8,128)}, f32[10,24,256]{2,1,0:T(8,128)}, f32[10,24,256]{2,1,0:T(8,128)}) custom-call(f32[19,24,16,256]{3,2,1,0:T(8,128)} %pops.3, f32[4,24,16,256]{3,2,1,0:T(8,128)} %bitcast.4, s32[24,16,256]{2,1,0:T(8,128)} %pore.5, s32[24,16,256]{2,1,0:T(8,128)} %wall.3), custom_call_target="tpu_custom_call" | custom-call | tf_op jit(solution)/shard_map/edge_faces/pallas_call | solution.py:603
  4.1 2.6 %collective-permute-start = (f32[18,16,256]{2,1,0:T(8,128)}, f32[18,16,256]{2,1,0:T(8,128)S(1)}, u32[]{:S(2)}, u32[]{:S(2)}) collective-permute-start(f32[18,16,256]{2,1,0:T(8,128)} %get-tuple-element.24), channel_id=1, source_target_pairs={{0,16},{16,0},{32,48},{48,32},{64,80},{80,64},{96,112},{112,96},{1... | collective-permute-start | bytes 884744 | tf_op jit(solution)/shard_map/ppermute | solution.py:711
  6.7 5.6 %collective-permute-start.1 = (f32[18,16,256]{2,1,0:T(8,128)}, f32[18,16,256]{2,1,0:T(8,128)S(1)}, u32[]{:S(2)}, u32[]{:S(2)}) collective-permute-start(f32[18,16,256]{2,1,0:T(8,128)} %get-tuple-element.25), channel_id=1, source_target_pairs={{0,240},{16,32},{32,16},{48,64},{64,48},{80,96},{96,80},{112,128},... | collective-permute-start | bytes 884744 | tf_op jit(solution)/shard_map/ppermute | solution.py:711
  12.3 1.2 %collective-permute-start.2 = (f32[10,24,256]{2,1,0:T(8,128)}, f32[10,24,256]{2,1,0:T(8,128)S(1)}, u32[]{:S(2)}, u32[]{:S(2)}) collective-permute-start(f32[10,24,256]{2,1,0:T(8,128)} %get-tuple-element.30.near_m), channel_id=1, source_target_pairs={{0,1},{1,0},{2,3},{3,2},{4,5},{5,4},{6,7},{7,6},{8,9},{9,8},{10,11... | collective-permute-start | bytes 737288 | tf_op jit(solution)/shard_map/ppermute | solution.py:711
  13.5 2.3 %collective-permute-start.3 = (f32[10,24,256]{2,1,0:T(8,128)}, f32[10,24,256]{2,1,0:T(8,128)S(1)}, u32[]{:S(2)}, u32[]{:S(2)}) collective-permute-start(f32[10,24,256]{2,1,0:T(8,128)} %get-tuple-element.31.far_m), channel_id=1, source_target_pairs={{0,15},{1,2},{2,1},{3,4},{4,3},{5,6},{6,5},{7,8},{8,7},{9,10},{10,... | collective-permute-start | bytes 737288 | tf_op jit(solution)/shard_map/ppermute | solution.py:711
  15.8 0.0 copy-done.1
  15.8 0.0 copy-start.5
  15.8 0.0 copy-start
  15.9 0.0 copy-start.2
  15.9 0.0 copy-start.3
  15.9 0.0 copy-start.4
  15.9 5.1 %collide.1 = (f32[4,26,16,256]{3,2,1,0:T(8,128)S(1)}, f32[8,24,256]{2,1,0:T(8,128)S(1)}, f32[8,24,256]{2,1,0:T(8,128)S(1)}) custom-call(f32[19,24,16,256]{3,2,1,0:T(8,128)} %pops.3, s32[24,16,256]{2,1,0:T(8,128)S(1)} %copy-done.1), custom_call_target="tpu_custom_call" | custom-call | flops 20000000 | bytes 12000000 | tf_op jit(solution)/shard_map/collide/pallas_call | solution.py:628
  21.0 0.0 collective-permute-done.got_near
  21.0 0.0 collective-permute-done.1.got_far
  21.0 0.1 merge.1
  21.2 3.0 %collective-permute-start.4 = (f32[8,24,256]{2,1,0:T(8,128)S(1)}, f32[8,24,256]{2,1,0:T(8,128)S(1)}, u32[]{:S(2)}, u32[]{:S(2)}) collective-permute-start(f32[8,24,256]{2,1,0:T(8,128)S(1)} %get-tuple-element.32.near_w), channel_id=1, source_target_pairs={{0,1},{1,0},{2,3},{3,2},{4,5},{5,4},{6,7},{7,6},{8,9},{9,8},{10,11... | collective-permute-start | bytes 589832 | tf_op jit(solution)/shard_map/ppermute | solution.py:711
  24.2 0.0 collective-permute-start.5
  24.2 0.0 copy-done.5
  24.2 0.1 fusion.1
  24.4 0.1 slice.14
  24.4 0.0 copy-done
  24.4 0.0 copy-done.2
  24.4 0.0 copy-done.3
  24.4 0.0 copy-done.4
  24.4 5.8 %inner_steps.1 = (f32[3,24,16,256]{3,2,1,0:T(8,128)}, f32[4,24,16,256]{3,2,1,0:T(8,128)}, f32[2,18,24,256]{3,2,1,0:T(8,128)S(1)}, f32[2,13,24,256]{3,2,1,0:T(8,1...) custom-call(f32[4,26]{1,0:T(4,128)S(1)} %pad_maximum_fusion.table, f32[4,24,16,256]{3,2,1,0:T(8,128)S(1)} %bitcast.5, ...), custom_call_target="tpu_custom_call" | custom-call | flops 40000000 | bytes 9000000 | tf_op jit(solution)/shard_map/inner_steps/pallas_call | solution.py:658
  30.2 0.0 collective-permute-done.2.got_near_m
  30.2 0.0 collective-permute-done.3.got_far_m
  30.2 0.0 collective-permute-done.4.got_near
  30.2 0.9 %collective-permute-done.5.got_far = f32[8,24,256]{2,1,0:T(8,128)S(1)} collective-permute-done((f32[8,24,256]{2,1,0:T(8,128)S(1)}, f32[8,24,256]{2,1,0:T(8,128)S(1)}, u32[]{:S(2)}, u32[]{:S(2)}) %collective-permute-start.5) | collective-permute-done | bytes 196640 | tf_op jit(solution)/shard_map/ppermute | solution.py:711
  31.1 0.1 broadcast_in_dim.6.wide
  31.2 2.5 %border_rows.1 = (f32[3,24,16,256]{3,2,1,0:T(8,128)}, f32[4,24,16,256]{3,2,1,0:T(8,128)}, f32[1,128]{1,0:T(1,128)S(1)}) custom-call(f32[4,26]{1,0:T(4,128)S(1)} %pad_maximum_fusion.table, f32[4,24,128]{2,1,0:T(8,128)S(1)} %broadcast_in_dim.6.wide, f32[4,24,16,256]{3,2,1,0:T(8,128)S(1)} %bitcast.6, ...), custom_call_target="tpu_custom_call", output_to_operand_aliasing={{0}: (14, {}), {1}: (15, {})} | custom-call | tf_op jit(solution)/shard_map/border_rows/pallas_call | solution.py:688
  33.7 0.1 broadcast_in_dim.8
  33.7 21.7 %all_to_all.5 = f32[256,1,128]{2,1,0:T(1,128)S(1)} all-to-all(f32[256,1,128]{2,1,0:T(1,128)S(1)} %broadcast_in_dim.8), channel_id=1, replica_groups=mesh['flow'=16,'trans'=16] {'flow','trans'}, dimensions={0} | all-to-all | bytes 262144 | tf_op jit(solution)/shard_map/all_to_all | solution.py:725
  55.5 0.6 %div.14 = f32[2,2]{1,0:T(2,128)} reshape(f32[4]{0:T(128)S(1)} %slice_multiply_fusion) | data formatting | bytes 32 | tf_op jit(solution)/shard_map/div | solution.py:754
  (4 shorter events, 0.1 us)
Async XLA Ops:
  0.6 15.2 %copy-start.1 = (s32[24,16,256]{2,1,0:T(8,128)S(1)}, s32[24,16,256]{2,1,0:T(8,128)}, u32[]{:S(2)}) copy-start(s32[24,16,256]{2,1,0:T(8,128)} %pore.5) | copy-start | bytes 1179652
  4.1 16.9 %collective-permute-start = (f32[18,16,256]{2,1,0:T(8,128)}, f32[18,16,256]{2,1,0:T(8,128)S(1)}, u32[]{:S(2)}, u32[]{:S(2)}) collective-permute-start(f32[18,16,256]{2,1,0:T(8,128)} %get-tuple-element.24), channel_id=1, source_target_pairs={{0,16},{16,0},{32,48},{48,32},{64,80},{80,64},{96,112},{112,96},{1... | collective-permute-start | bytes 884744 | tf_op jit(solution)/shard_map/ppermute | solution.py:711
  6.7 14.3 %collective-permute-start.1 = (f32[18,16,256]{2,1,0:T(8,128)}, f32[18,16,256]{2,1,0:T(8,128)S(1)}, u32[]{:S(2)}, u32[]{:S(2)}) collective-permute-start(f32[18,16,256]{2,1,0:T(8,128)} %get-tuple-element.25), channel_id=1, source_target_pairs={{0,240},{16,32},{32,16},{48,64},{64,48},{80,96},{96,80},{112,128},... | collective-permute-start | bytes 884744 | tf_op jit(solution)/shard_map/ppermute | solution.py:711
  12.3 17.9 %collective-permute-start.2 = (f32[10,24,256]{2,1,0:T(8,128)}, f32[10,24,256]{2,1,0:T(8,128)S(1)}, u32[]{:S(2)}, u32[]{:S(2)}) collective-permute-start(f32[10,24,256]{2,1,0:T(8,128)} %get-tuple-element.30.near_m), channel_id=1, source_target_pairs={{0,1},{1,0},{2,3},{3,2},{4,5},{5,4},{6,7},{7,6},{8,9},{9,8},{10,11... | collective-permute-start | bytes 737288 | tf_op jit(solution)/shard_map/ppermute | solution.py:711
  13.5 16.7 %collective-permute-start.3 = (f32[10,24,256]{2,1,0:T(8,128)}, f32[10,24,256]{2,1,0:T(8,128)S(1)}, u32[]{:S(2)}, u32[]{:S(2)}) collective-permute-start(f32[10,24,256]{2,1,0:T(8,128)} %get-tuple-element.31.far_m), channel_id=1, source_target_pairs={{0,15},{1,2},{2,1},{3,4},{4,3},{5,6},{6,5},{7,8},{8,7},{9,10},{10,... | collective-permute-start | bytes 737288 | tf_op jit(solution)/shard_map/ppermute | solution.py:711
  15.8 8.4 %copy-start.5 = (f32[2]{0:T(128)S(1)}, f32[2]{0:T(128)}, u32[]{:S(2)}) copy-start(f32[2]{0:T(128)} %constant.38) | copy-start | bytes 28
  15.8 8.6 %copy-start = (f32[2,2,24,16,256]{4,3,2,1,0:T(8,128)S(1)}, f32[2,2,24,16,256]{4,3,2,1,0:T(8,128)}, u32[]{:S(2)}) copy-start(f32[2,2,24,16,256]{4,3,2,1,0:T(8,128)} %param.6) | copy-start | bytes 4718596
  15.9 8.6 %copy-start.2 = (s32[24,16,256]{2,1,0:T(8,128)S(1)}, s32[24,16,256]{2,1,0:T(8,128)}, u32[]{:S(2)}) copy-start(s32[24,16,256]{2,1,0:T(8,128)} %wall.3) | copy-start | bytes 1179652
  15.9 8.6 %copy-start.3 = (f32[10,24,256]{2,1,0:T(8,128)S(1)}, f32[10,24,256]{2,1,0:T(8,128)}, u32[]{:S(2)}) copy-start(f32[10,24,256]{2,1,0:T(8,128)} %get-tuple-element.31.far_m) | copy-start | bytes 737284
  15.9 8.6 %copy-start.4 = (f32[10,24,256]{2,1,0:T(8,128)S(1)}, f32[10,24,256]{2,1,0:T(8,128)}, u32[]{:S(2)}) copy-start(f32[10,24,256]{2,1,0:T(8,128)} %get-tuple-element.30.near_m) | copy-start | bytes 737284
  21.2 9.1 %collective-permute-start.4 = (f32[8,24,256]{2,1,0:T(8,128)S(1)}, f32[8,24,256]{2,1,0:T(8,128)S(1)}, u32[]{:S(2)}, u32[]{:S(2)}) collective-permute-start(f32[8,24,256]{2,1,0:T(8,128)S(1)} %get-tuple-element.32.near_w), channel_id=1, source_target_pairs={{0,1},{1,0},{2,3},{3,2},{4,5},{5,4},{6,7},{7,6},{8,9},{9,8},{10,11... | collective-permute-start | bytes 589832 | tf_op jit(solution)/shard_map/ppermute | solution.py:711
  24.2 6.9 %collective-permute-start.5 = (f32[8,24,256]{2,1,0:T(8,128)S(1)}, f32[8,24,256]{2,1,0:T(8,128)S(1)}, u32[]{:S(2)}, u32[]{:S(2)}) collective-permute-start(f32[8,24,256]{2,1,0:T(8,128)S(1)} %get-tuple-element.33.far_w), channel_id=1, source_target_pairs={{0,15},{1,2},{2,1},{3,4},{4,3},{5,6},{6,5},{7,8},{8,7},{9,10},{10,... | collective-permute-start | bytes 589832 | tf_op jit(solution)/shard_map/ppermute | solution.py:711

commit v5 on v4

--- a/solution.py
+++ b/solution.py
@@ -178,7 +178,7 @@
             face[9, at, :] = wal[z, border : border + 1, :].astype(jnp.float32)
         return carry
 
-    lax.fori_loop(0, depth, rows, 0, unroll=2)
+    lax.fori_loop(0, depth, rows, 0, unroll=6)
     sent += [
         send(even_y, right, y_near, y_far, sems.at[7]),
         send(even_y, left, y_far, y_near, sems.at[8]),
@@ -624,7 +624,7 @@
 
 def collide(pops, pore):
     depth, width, x_width = pore.shape
-    chunks = 6 if depth % 12 == 0 else 1
+    chunks = 12 if depth % 24 == 0 else 1
     return pl.pallas_call(
         collide_kernel,
         in_specs=[HBM] * 2,
@@ -735,6 +735,7 @@
     wide = jnp.broadcast_to(table[:, 1:-1, None], (4, depth, 128))
 
     near_z, far_z, near_m, far_m = edge_faces(populations, magnet, pore, wall)
+    near_m, table, wide = lax.optimization_barrier((near_m, table, wide))
     got_near_z = swap(near_z, "flow", True)
     got_far_z = swap(far_z, "flow", False)
     got_near_m = swap(near_m, "trans", True)

time: 56.3 us -> 56.2 us (level)
  transfers between devices with their start and end apart: 6 -> 6, of which waited for: 1 -> 1; matrix products, arithmetic and copies ran while one was open for 0% -> 1% of each run, Pallas kernels for 20% -> 19%
where the time goes in v5:
time: 56.2 us; the launch traced here: 56.1 us
  blocking collectives  21.5 us (38%)
  Pallas kernels  16.7 us (30%)
  starting transfers between devices  14.8 us (26%)
  waiting for transfers between devices  1.17 us (2%)
  local copies, waits for them, and re-layouts  0.89 us (2%)
  between operations  0.77 us (1%)
    all_to_all x1, blocking collectives, sum_over(): return jnp.sum(lax.all_to_all(copies, axes, 0, 0), axis=(0, 1))  21.5 us
    ppermute x6, starting transfers between devices, swap(): lax.ppermute(value, axis, [(i, (i + (step if i % 2 == 0 else -step)) % co...  14.8 us
    pallas_call x1, Pallas kernels, inner_steps(): pl.pallas_call(inner_kernel, in_specs=[SMEM] + [HBM] * 3 + [VMEM] * (3 +...  5.77 us
    pallas_call x1, Pallas kernels, collide(): pl.pallas_call(collide_kernel, in_specs=[HBM] * 2, out_specs=[VMEM] * 3,...  4.94 us
    pallas_call x1, Pallas kernels, edge_faces(): pl.pallas_call(edge_kernel, in_specs=[HBM] * 4, out_specs=[HBM] * 4, out_...  3.44 us
    pallas_call x1, Pallas kernels, border_rows(): pl.pallas_call(border_kernel, in_specs=[SMEM, VMEM, HBM] + [VMEM] * count...  2.47 us
    ppermute x6, waiting for transfers between devices, swap(): lax.ppermute(value, axis, [(i, (i + (step if i % 2 == 0 else -step)) % co...  1.17 us
  transfers between devices with their start and end apart: 6, of which 1 were waited for; matrix products, arithmetic and copies ran while one was open for 1% of the time, Pallas kernels for 19%

profile of v5, /device:TPU:1, one launch (start us, length us, event | category | flops | bytes accessed | tf_op | source)
XLA Modules:
  0.0 56.1 jit_solution(6015536322565149977)
XLA Ops:
  0.6 0.0 copy-start.5
  0.6 0.0 copy-start.1
  0.7 3.4 %edge_faces.1 = (f32[18,16,256]{2,1,0:T(8,128)}, f32[18,16,256]{2,1,0:T(8,128)}, f32[10,24,256]{2,1,0:T(8,128)}, f32[10,24,256]{2,1,0:T(8,128)}) custom-call(f32[19,24,16,256]{3,2,1,0:T(8,128)} %pops.3, f32[4,24,16,256]{3,2,1,0:T(8,128)} %bitcast.4, s32[24,16,256]{2,1,0:T(8,128)} %pore.5, s32[24,16,256]{2,1,0:T(8,128)} %wall.3), custom_call_target="tpu_custom_call" | custom-call | tf_op jit(solution)/shard_map/edge_faces/pallas_call | solution.py:603
  4.1 2.6 %collective-permute-start = (f32[18,16,256]{2,1,0:T(8,128)}, f32[18,16,256]{2,1,0:T(8,128)S(1)}, u32[]{:S(2)}, u32[]{:S(2)}) collective-permute-start(f32[18,16,256]{2,1,0:T(8,128)} %get-tuple-element.30), channel_id=1, source_target_pairs={{0,16},{16,0},{32,48},{48,32},{64,80},{80,64},{96,112},{112,96},{1... | collective-permute-start | bytes 884744 | tf_op jit(solution)/shard_map/ppermute | solution.py:711
  6.6 5.6 %collective-permute-start.1 = (f32[18,16,256]{2,1,0:T(8,128)}, f32[18,16,256]{2,1,0:T(8,128)S(1)}, u32[]{:S(2)}, u32[]{:S(2)}) collective-permute-start(f32[18,16,256]{2,1,0:T(8,128)} %get-tuple-element.31), channel_id=1, source_target_pairs={{0,240},{16,32},{32,16},{48,64},{64,48},{80,96},{96,80},{112,128},... | collective-permute-start | bytes 884744 | tf_op jit(solution)/shard_map/ppermute | solution.py:711
  12.3 0.0 copy-done.5
  12.3 0.1 fusion.1
  12.4 0.1 slice.14
  12.5 0.1 broadcast_in_dim.6.wide
  12.5 1.3 %collective-permute-start.2 = (f32[10,24,256]{2,1,0:T(8,128)}, f32[10,24,256]{2,1,0:T(8,128)S(1)}, u32[]{:S(2)}, u32[]{:S(2)}) collective-permute-start(f32[10,24,256]{2,1,0:T(8,128)} %get-tuple-element.36.near_m), channel_id=1, source_target_pairs={{0,1},{1,0},{2,3},{3,2},{4,5},{5,4},{6,7},{7,6},{8,9},{9,8},{10,11... | collective-permute-start | bytes 737288 | tf_op jit(solution)/shard_map/ppermute | solution.py:711
  13.8 0.0 copy-start.2
  13.8 0.0 copy-start.3
  13.8 0.0 copy-start.4
  13.8 2.5 %collective-permute-start.3 = (f32[10,24,256]{2,1,0:T(8,128)}, f32[10,24,256]{2,1,0:T(8,128)S(1)}, u32[]{:S(2)}, u32[]{:S(2)}) collective-permute-start(f32[10,24,256]{2,1,0:T(8,128)} %get-tuple-element.37.far_m), channel_id=1, source_target_pairs={{0,15},{1,2},{2,1},{3,4},{4,3},{5,6},{6,5},{7,8},{8,7},{9,10},{10,... | collective-permute-start | bytes 737288 | tf_op jit(solution)/shard_map/ppermute | solution.py:711
  16.3 0.0 copy-done.1
  16.3 0.0 copy-start
  16.3 4.9 %collide.1 = (f32[4,26,16,256]{3,2,1,0:T(8,128)S(1)}, f32[8,24,256]{2,1,0:T(8,128)S(1)}, f32[8,24,256]{2,1,0:T(8,128)S(1)}) custom-call(f32[19,24,16,256]{3,2,1,0:T(8,128)} %pops.3, s32[24,16,256]{2,1,0:T(8,128)S(1)} %copy-done.1), custom_call_target="tpu_custom_call" | custom-call | flops 20000000 | bytes 12000000 | tf_op jit(solution)/shard_map/collide/pallas_call | solution.py:628
  21.2 0.0 collective-permute-done.got_near
  21.2 0.0 collective-permute-done.1.got_far
  21.2 0.1 merge.1
  21.4 2.9 %collective-permute-start.4 = (f32[8,24,256]{2,1,0:T(8,128)S(1)}, f32[8,24,256]{2,1,0:T(8,128)S(1)}, u32[]{:S(2)}, u32[]{:S(2)}) collective-permute-start(f32[8,24,256]{2,1,0:T(8,128)S(1)} %get-tuple-element.38.near_w), channel_id=1, source_target_pairs={{0,1},{1,0},{2,3},{3,2},{4,5},{5,4},{6,7},{7,6},{8,9},{9,8},{10,11... | collective-permute-start | bytes 589832 | tf_op jit(solution)/shard_map/ppermute | solution.py:711
  24.3 0.0 collective-permute-start.5
  24.3 0.0 copy-done.2
  24.3 0.0 copy-done.3
  24.3 0.0 copy-done.4
  24.3 0.0 copy-done
  24.3 5.8 %inner_steps.1 = (f32[3,24,16,256]{3,2,1,0:T(8,128)}, f32[4,24,16,256]{3,2,1,0:T(8,128)}, f32[2,18,24,256]{3,2,1,0:T(8,128)S(1)}, f32[2,13,24,256]{3,2,1,0:T(8,1...) custom-call(f32[4,26]{1,0:T(4,128)S(1)} %pad_maximum_fusion.table, f32[4,24,16,256]{3,2,1,0:T(8,128)S(1)} %bitcast.5, ...), custom_call_target="tpu_custom_call" | custom-call | flops 40000000 | bytes 9000000 | tf_op jit(solution)/shard_map/inner_steps/pallas_call | solution.py:658
  30.1 0.0 collective-permute-done.2.got_near_m
  30.1 0.0 collective-permute-done.3.got_far_m
  30.1 0.0 collective-permute-done.4.got_near
  30.1 1.2 %collective-permute-done.5.got_far = f32[8,24,256]{2,1,0:T(8,128)S(1)} collective-permute-done((f32[8,24,256]{2,1,0:T(8,128)S(1)}, f32[8,24,256]{2,1,0:T(8,128)S(1)}, u32[]{:S(2)}, u32[]{:S(2)}) %collective-permute-start.5) | collective-permute-done | bytes 196640 | tf_op jit(solution)/shard_map/ppermute | solution.py:711
  31.3 2.5 %border_rows.1 = (f32[3,24,16,256]{3,2,1,0:T(8,128)}, f32[4,24,16,256]{3,2,1,0:T(8,128)}, f32[1,128]{1,0:T(1,128)S(1)}) custom-call(f32[4,26]{1,0:T(4,128)S(1)} %pad_maximum_fusion.table, f32[4,24,128]{2,1,0:T(8,128)S(1)} %broadcast_in_dim.6.wide, f32[4,24,16,256]{3,2,1,0:T(8,128)S(1)} %bitcast.6, ...), custom_call_target="tpu_custom_call", output_to_operand_aliasing={{0}: (14, {}), {1}: (15, {})} | custom-call | tf_op jit(solution)/shard_map/border_rows/pallas_call | solution.py:688
  33.8 0.1 broadcast_in_dim.8
  33.9 21.5 %all_to_all.5 = f32[256,1,128]{2,1,0:T(1,128)S(1)} all-to-all(f32[256,1,128]{2,1,0:T(1,128)S(1)} %broadcast_in_dim.8), channel_id=1, replica_groups=mesh['flow'=16,'trans'=16] {'flow','trans'}, dimensions={0} | all-to-all | bytes 262144 | tf_op jit(solution)/shard_map/all_to_all | solution.py:725
  55.4 0.6 %div.14 = f32[2,2]{1,0:T(2,128)} reshape(f32[4]{0:T(128)S(1)} %slice_multiply_fusion) | data formatting | bytes 32 | tf_op jit(solution)/shard_map/div | solution.py:755
  (4 shorter events, 0.1 us)
Async XLA Ops:
  0.6 11.6 %copy-start.5 = (f32[2]{0:T(128)S(1)}, f32[2]{0:T(128)}, u32[]{:S(2)}) copy-start(f32[2]{0:T(128)} %constant.38) | copy-start | bytes 28
  0.6 15.6 %copy-start.1 = (s32[24,16,256]{2,1,0:T(8,128)S(1)}, s32[24,16,256]{2,1,0:T(8,128)}, u32[]{:S(2)}) copy-start(s32[24,16,256]{2,1,0:T(8,128)} %pore.5) | copy-start | bytes 1179652
  4.1 17.1 %collective-permute-start = (f32[18,16,256]{2,1,0:T(8,128)}, f32[18,16,256]{2,1,0:T(8,128)S(1)}, u32[]{:S(2)}, u32[]{:S(2)}) collective-permute-start(f32[18,16,256]{2,1,0:T(8,128)} %get-tuple-element.30), channel_id=1, source_target_pairs={{0,16},{16,0},{32,48},{48,32},{64,80},{80,64},{96,112},{112,96},{1... | collective-permute-start | bytes 884744 | tf_op jit(solution)/shard_map/ppermute | solution.py:711
  6.6 14.6 %collective-permute-start.1 = (f32[18,16,256]{2,1,0:T(8,128)}, f32[18,16,256]{2,1,0:T(8,128)S(1)}, u32[]{:S(2)}, u32[]{:S(2)}) collective-permute-start(f32[18,16,256]{2,1,0:T(8,128)} %get-tuple-element.31), channel_id=1, source_target_pairs={{0,240},{16,32},{32,16},{48,64},{64,48},{80,96},{96,80},{112,128},... | collective-permute-start | bytes 884744 | tf_op jit(solution)/shard_map/ppermute | solution.py:711
  12.5 17.6 %collective-permute-start.2 = (f32[10,24,256]{2,1,0:T(8,128)}, f32[10,24,256]{2,1,0:T(8,128)S(1)}, u32[]{:S(2)}, u32[]{:S(2)}) collective-permute-start(f32[10,24,256]{2,1,0:T(8,128)} %get-tuple-element.36.near_m), channel_id=1, source_target_pairs={{0,1},{1,0},{2,3},{3,2},{4,5},{5,4},{6,7},{7,6},{8,9},{9,8},{10,11... | collective-permute-start | bytes 737288 | tf_op jit(solution)/shard_map/ppermute | solution.py:711
  13.8 10.5 %copy-start.2 = (s32[24,16,256]{2,1,0:T(8,128)S(1)}, s32[24,16,256]{2,1,0:T(8,128)}, u32[]{:S(2)}) copy-start(s32[24,16,256]{2,1,0:T(8,128)} %wall.3) | copy-start | bytes 1179652
  13.8 10.5 %copy-start.3 = (f32[10,24,256]{2,1,0:T(8,128)S(1)}, f32[10,24,256]{2,1,0:T(8,128)}, u32[]{:S(2)}) copy-start(f32[10,24,256]{2,1,0:T(8,128)} %get-tuple-element.37.far_m) | copy-start | bytes 737284
  13.8 10.5 %copy-start.4 = (f32[10,24,256]{2,1,0:T(8,128)S(1)}, f32[10,24,256]{2,1,0:T(8,128)}, u32[]{:S(2)}) copy-start(f32[10,24,256]{2,1,0:T(8,128)} %get-tuple-element.36.near_m) | copy-start | bytes 737284
  13.8 16.3 %collective-permute-start.3 = (f32[10,24,256]{2,1,0:T(8,128)}, f32[10,24,256]{2,1,0:T(8,128)S(1)}, u32[]{:S(2)}, u32[]{:S(2)}) collective-permute-start(f32[10,24,256]{2,1,0:T(8,128)} %get-tuple-element.37.far_m), channel_id=1, source_target_pairs={{0,15},{1,2},{2,1},{3,4},{4,3},{5,6},{6,5},{7,8},{8,7},{9,10},{10,... | collective-permute-start | bytes 737288 | tf_op jit(solution)/shard_map/ppermute | solution.py:711
  16.3 8.1 %copy-start = (f32[2,2,24,16,256]{4,3,2,1,0:T(8,128)S(1)}, f32[2,2,24,16,256]{4,3,2,1,0:T(8,128)}, u32[]{:S(2)}) copy-start(f32[2,2,24,16,256]{4,3,2,1,0:T(8,128)} %param.6) | copy-start | bytes 4718596
  21.4 8.8 %collective-permute-start.4 = (f32[8,24,256]{2,1,0:T(8,128)S(1)}, f32[8,24,256]{2,1,0:T(8,128)S(1)}, u32[]{:S(2)}, u32[]{:S(2)}) collective-permute-start(f32[8,24,256]{2,1,0:T(8,128)S(1)} %get-tuple-element.38.near_w), channel_id=1, source_target_pairs={{0,1},{1,0},{2,3},{3,2},{4,5},{5,4},{6,7},{7,6},{8,9},{9,8},{10,11... | collective-permute-start | bytes 589832 | tf_op jit(solution)/shard_map/ppermute | solution.py:711
  24.3 7.0 %collective-permute-start.5 = (f32[8,24,256]{2,1,0:T(8,128)S(1)}, f32[8,24,256]{2,1,0:T(8,128)S(1)}, u32[]{:S(2)}, u32[]{:S(2)}) collective-permute-start(f32[8,24,256]{2,1,0:T(8,128)S(1)} %get-tuple-element.39.far_w), channel_id=1, source_target_pairs={{0,15},{1,2},{2,1},{3,4},{4,3},{5,6},{6,5},{7,8},{8,7},{9,10},{10,... | collective-permute-start | bytes 589832 | tf_op jit(solution)/shard_map/ppermute | solution.py:711

commit v6 on v5

--- a/solution.py
+++ b/solution.py
@@ -388,7 +388,7 @@
         layer(z, None, lambda k: mag[k, z + 1], lambda k: mag[k, z - 1])
         return carry
 
-    lax.fori_loop(1, depth - 1, middle, 0, unroll=2)
+    lax.fori_loop(1, depth - 1, middle, 0, unroll=4)
     layer(depth - 1, (high, -1.0), lambda k: high[7 + k], lambda k: mag[k, depth - 2])
 
     def second(z, totals):
@@ -405,7 +405,7 @@
     stores = [pltpu.make_async_copy(vel, vel_out, sems.at[3])]
     stores[0].start()
     for c in range(chunks):
-        totals = lax.fori_loop(c * size, (c + 1) * size, second, totals, unroll=2)
+        totals = lax.fori_loop(c * size, (c + 1) * size, second, totals, unroll=4)
         at = pl.ds(c * size, size)
         stores.append(pltpu.make_async_copy(new.at[:, at], new_out.at[:, at], sems.at[4 + c]))
         stores[-1].start()

time: 56.2 us -> 56.2 us (level)
  transfers between devices with their start and end apart: 6 -> 6, of which waited for: 1 -> 1; matrix products, arithmetic and copies ran while one was open for 1% -> 1% of each run, Pallas kernels for 19% -> 18%
where the time goes in v6:
time: 56.2 us; the launch traced here: 56.1 us
  blocking collectives  21.5 us (38%)
  Pallas kernels  16.3 us (29%)
  starting transfers between devices  14.8 us (26%)
  waiting for transfers between devices  1.64 us (3%)
  local copies, waits for them, and re-layouts  0.89 us (2%)
  between operations  0.77 us (1%)
    all_to_all x1, blocking collectives, sum_over(): return jnp.sum(lax.all_to_all(copies, axes, 0, 0), axis=(0, 1))  21.5 us
    ppermute x6, starting transfers between devices, swap(): lax.ppermute(value, axis, [(i, (i + (step if i % 2 == 0 else -step)) % co...  14.8 us
    pallas_call x1, Pallas kernels, inner_steps(): pl.pallas_call(inner_kernel, in_specs=[SMEM] + [HBM] * 3 + [VMEM] * (3 +...  5.3 us
    pallas_call x1, Pallas kernels, collide(): pl.pallas_call(collide_kernel, in_specs=[HBM] * 2, out_specs=[VMEM] * 3,...  4.94 us
    pallas_call x1, Pallas kernels, edge_faces(): pl.pallas_call(edge_kernel, in_specs=[HBM] * 4, out_specs=[HBM] * 4, out_...  3.44 us
    pallas_call x1, Pallas kernels, border_rows(): pl.pallas_call(border_kernel, in_specs=[SMEM, VMEM, HBM] + [VMEM] * count...  2.47 us
    ppermute x6, waiting for transfers between devices, swap(): lax.ppermute(value, axis, [(i, (i + (step if i % 2 == 0 else -step)) % co...  1.64 us
  transfers between devices with their start and end apart: 6, of which 1 were waited for; matrix products, arithmetic and copies ran while one was open for 1% of the time, Pallas kernels for 18%

profile of v6, /device:TPU:1, one launch (start us, length us, event | category | flops | bytes accessed | tf_op | source)
XLA Modules:
  0.0 56.1 jit_solution(11217506033260172459)
XLA Ops:
  0.6 0.0 copy-start.5
  0.6 0.0 copy-start.1
  0.7 3.4 %edge_faces.1 = (f32[18,16,256]{2,1,0:T(8,128)}, f32[18,16,256]{2,1,0:T(8,128)}, f32[10,24,256]{2,1,0:T(8,128)}, f32[10,24,256]{2,1,0:T(8,128)}) custom-call(f32[19,24,16,256]{3,2,1,0:T(8,128)} %pops.3, f32[4,24,16,256]{3,2,1,0:T(8,128)} %bitcast.4, s32[24,16,256]{2,1,0:T(8,128)} %pore.5, s32[24,16,256]{2,1,0:T(8,128)} %wall.3), custom_call_target="tpu_custom_call" | custom-call | tf_op jit(solution)/shard_map/edge_faces/pallas_call | solution.py:603
  4.1 2.6 %collective-permute-start = (f32[18,16,256]{2,1,0:T(8,128)}, f32[18,16,256]{2,1,0:T(8,128)S(1)}, u32[]{:S(2)}, u32[]{:S(2)}) collective-permute-start(f32[18,16,256]{2,1,0:T(8,128)} %get-tuple-element.30), channel_id=1, source_target_pairs={{0,16},{16,0},{32,48},{48,32},{64,80},{80,64},{96,112},{112,96},{1... | collective-permute-start | bytes 884744 | tf_op jit(solution)/shard_map/ppermute | solution.py:711
  6.6 5.6 %collective-permute-start.1 = (f32[18,16,256]{2,1,0:T(8,128)}, f32[18,16,256]{2,1,0:T(8,128)S(1)}, u32[]{:S(2)}, u32[]{:S(2)}) collective-permute-start(f32[18,16,256]{2,1,0:T(8,128)} %get-tuple-element.31), channel_id=1, source_target_pairs={{0,240},{16,32},{32,16},{48,64},{64,48},{80,96},{96,80},{112,128},... | collective-permute-start | bytes 884744 | tf_op jit(solution)/shard_map/ppermute | solution.py:711
  12.3 0.0 copy-done.5
  12.3 0.1 fusion.1
  12.4 0.1 slice.14
  12.5 0.1 broadcast_in_dim.6.wide
  12.5 1.3 %collective-permute-start.2 = (f32[10,24,256]{2,1,0:T(8,128)}, f32[10,24,256]{2,1,0:T(8,128)S(1)}, u32[]{:S(2)}, u32[]{:S(2)}) collective-permute-start(f32[10,24,256]{2,1,0:T(8,128)} %get-tuple-element.36.near_m), channel_id=1, source_target_pairs={{0,1},{1,0},{2,3},{3,2},{4,5},{5,4},{6,7},{7,6},{8,9},{9,8},{10,11... | collective-permute-start | bytes 737288 | tf_op jit(solution)/shard_map/ppermute | solution.py:711
  13.8 0.0 copy-start.2
  13.8 0.0 copy-start.3
  13.8 0.0 copy-start.4
  13.8 2.5 %collective-permute-start.3 = (f32[10,24,256]{2,1,0:T(8,128)}, f32[10,24,256]{2,1,0:T(8,128)S(1)}, u32[]{:S(2)}, u32[]{:S(2)}) collective-permute-start(f32[10,24,256]{2,1,0:T(8,128)} %get-tuple-element.37.far_m), channel_id=1, source_target_pairs={{0,15},{1,2},{2,1},{3,4},{4,3},{5,6},{6,5},{7,8},{8,7},{9,10},{10,... | collective-permute-start | bytes 737288 | tf_op jit(solution)/shard_map/ppermute | solution.py:711
  16.3 0.0 copy-done.1
  16.3 0.0 copy-start
  16.3 4.9 %collide.1 = (f32[4,26,16,256]{3,2,1,0:T(8,128)S(1)}, f32[8,24,256]{2,1,0:T(8,128)S(1)}, f32[8,24,256]{2,1,0:T(8,128)S(1)}) custom-call(f32[19,24,16,256]{3,2,1,0:T(8,128)} %pops.3, s32[24,16,256]{2,1,0:T(8,128)S(1)} %copy-done.1), custom_call_target="tpu_custom_call" | custom-call | flops 20000000 | bytes 12000000 | tf_op jit(solution)/shard_map/collide/pallas_call | solution.py:628
  21.2 0.0 collective-permute-done.got_near
  21.2 0.0 collective-permute-done.1.got_far
  21.2 0.1 merge.1
  21.4 2.9 %collective-permute-start.4 = (f32[8,24,256]{2,1,0:T(8,128)S(1)}, f32[8,24,256]{2,1,0:T(8,128)S(1)}, u32[]{:S(2)}, u32[]{:S(2)}) collective-permute-start(f32[8,24,256]{2,1,0:T(8,128)S(1)} %get-tuple-element.38.near_w), channel_id=1, source_target_pairs={{0,1},{1,0},{2,3},{3,2},{4,5},{5,4},{6,7},{7,6},{8,9},{9,8},{10,11... | collective-permute-start | bytes 589832 | tf_op jit(solution)/shard_map/ppermute | solution.py:711
  24.3 0.0 collective-permute-start.5
  24.3 0.0 copy-done.2
  24.3 0.0 copy-done.3
  24.3 0.0 copy-done.4
  24.3 0.0 copy-done
  24.3 5.3 %inner_steps.1 = (f32[3,24,16,256]{3,2,1,0:T(8,128)}, f32[4,24,16,256]{3,2,1,0:T(8,128)}, f32[2,18,24,256]{3,2,1,0:T(8,128)S(1)}, f32[2,13,24,256]{3,2,1,0:T(8,1...) custom-call(f32[4,26]{1,0:T(4,128)S(1)} %pad_maximum_fusion.table, f32[4,24,16,256]{3,2,1,0:T(8,128)S(1)} %bitcast.5, ...), custom_call_target="tpu_custom_call" | custom-call | flops 40000000 | bytes 9000000 | tf_op jit(solution)/shard_map/inner_steps/pallas_call | solution.py:658
  29.6 0.0 collective-permute-done.2.got_near_m
  29.7 0.0 collective-permute-done.3.got_far_m
  29.7 0.0 collective-permute-done.4.got_near
  29.7 1.6 %collective-permute-done.5.got_far = f32[8,24,256]{2,1,0:T(8,128)S(1)} collective-permute-done((f32[8,24,256]{2,1,0:T(8,128)S(1)}, f32[8,24,256]{2,1,0:T(8,128)S(1)}, u32[]{:S(2)}, u32[]{:S(2)}) %collective-permute-start.5) | collective-permute-done | bytes 196640 | tf_op jit(solution)/shard_map/ppermute | solution.py:711
  31.3 2.5 %border_rows.1 = (f32[3,24,16,256]{3,2,1,0:T(8,128)}, f32[4,24,16,256]{3,2,1,0:T(8,128)}, f32[1,128]{1,0:T(1,128)S(1)}) custom-call(f32[4,26]{1,0:T(4,128)S(1)} %pad_maximum_fusion.table, f32[4,24,128]{2,1,0:T(8,128)S(1)} %broadcast_in_dim.6.wide, f32[4,24,16,256]{3,2,1,0:T(8,128)S(1)} %bitcast.6, ...), custom_call_target="tpu_custom_call", output_to_operand_aliasing={{0}: (14, {}), {1}: (15, {})} | custom-call | tf_op jit(solution)/shard_map/border_rows/pallas_call | solution.py:688
  33.8 0.1 broadcast_in_dim.8
  33.9 21.5 %all_to_all.5 = f32[256,1,128]{2,1,0:T(1,128)S(1)} all-to-all(f32[256,1,128]{2,1,0:T(1,128)S(1)} %broadcast_in_dim.8), channel_id=1, replica_groups=mesh['flow'=16,'trans'=16] {'flow','trans'}, dimensions={0} | all-to-all | bytes 262144 | tf_op jit(solution)/shard_map/all_to_all | solution.py:725
  55.4 0.6 %div.14 = f32[2,2]{1,0:T(2,128)} reshape(f32[4]{0:T(128)S(1)} %slice_multiply_fusion) | data formatting | bytes 32 | tf_op jit(solution)/shard_map/div | solution.py:755
  (4 shorter events, 0.1 us)
Async XLA Ops:
  0.6 11.6 %copy-start.5 = (f32[2]{0:T(128)S(1)}, f32[2]{0:T(128)}, u32[]{:S(2)}) copy-start(f32[2]{0:T(128)} %constant.38) | copy-start | bytes 28
  0.6 15.6 %copy-start.1 = (s32[24,16,256]{2,1,0:T(8,128)S(1)}, s32[24,16,256]{2,1,0:T(8,128)}, u32[]{:S(2)}) copy-start(s32[24,16,256]{2,1,0:T(8,128)} %pore.5) | copy-start | bytes 1179652
  4.1 17.1 %collective-permute-start = (f32[18,16,256]{2,1,0:T(8,128)}, f32[18,16,256]{2,1,0:T(8,128)S(1)}, u32[]{:S(2)}, u32[]{:S(2)}) collective-permute-start(f32[18,16,256]{2,1,0:T(8,128)} %get-tuple-element.30), channel_id=1, source_target_pairs={{0,16},{16,0},{32,48},{48,32},{64,80},{80,64},{96,112},{112,96},{1... | collective-permute-start | bytes 884744 | tf_op jit(solution)/shard_map/ppermute | solution.py:711
  6.6 14.6 %collective-permute-start.1 = (f32[18,16,256]{2,1,0:T(8,128)}, f32[18,16,256]{2,1,0:T(8,128)S(1)}, u32[]{:S(2)}, u32[]{:S(2)}) collective-permute-start(f32[18,16,256]{2,1,0:T(8,128)} %get-tuple-element.31), channel_id=1, source_target_pairs={{0,240},{16,32},{32,16},{48,64},{64,48},{80,96},{96,80},{112,128},... | collective-permute-start | bytes 884744 | tf_op jit(solution)/shard_map/ppermute | solution.py:711
  12.5 17.1 %collective-permute-start.2 = (f32[10,24,256]{2,1,0:T(8,128)}, f32[10,24,256]{2,1,0:T(8,128)S(1)}, u32[]{:S(2)}, u32[]{:S(2)}) collective-permute-start(f32[10,24,256]{2,1,0:T(8,128)} %get-tuple-element.36.near_m), channel_id=1, source_target_pairs={{0,1},{1,0},{2,3},{3,2},{4,5},{5,4},{6,7},{7,6},{8,9},{9,8},{10,11... | collective-permute-start | bytes 737288 | tf_op jit(solution)/shard_map/ppermute | solution.py:711
  13.8 10.5 %copy-start.2 = (s32[24,16,256]{2,1,0:T(8,128)S(1)}, s32[24,16,256]{2,1,0:T(8,128)}, u32[]{:S(2)}) copy-start(s32[24,16,256]{2,1,0:T(8,128)} %wall.3) | copy-start | bytes 1179652
  13.8 10.5 %copy-start.3 = (f32[10,24,256]{2,1,0:T(8,128)S(1)}, f32[10,24,256]{2,1,0:T(8,128)}, u32[]{:S(2)}) copy-start(f32[10,24,256]{2,1,0:T(8,128)} %get-tuple-element.37.far_m) | copy-start | bytes 737284
  13.8 10.5 %copy-start.4 = (f32[10,24,256]{2,1,0:T(8,128)S(1)}, f32[10,24,256]{2,1,0:T(8,128)}, u32[]{:S(2)}) copy-start(f32[10,24,256]{2,1,0:T(8,128)} %get-tuple-element.36.near_m) | copy-start | bytes 737284
  13.8 15.9 %collective-permute-start.3 = (f32[10,24,256]{2,1,0:T(8,128)}, f32[10,24,256]{2,1,0:T(8,128)S(1)}, u32[]{:S(2)}, u32[]{:S(2)}) collective-permute-start(f32[10,24,256]{2,1,0:T(8,128)} %get-tuple-element.37.far_m), channel_id=1, source_target_pairs={{0,15},{1,2},{2,1},{3,4},{4,3},{5,6},{6,5},{7,8},{8,7},{9,10},{10,... | collective-permute-start | bytes 737288 | tf_op jit(solution)/shard_map/ppermute | solution.py:711
  16.3 8.1 %copy-start = (f32[2,2,24,16,256]{4,3,2,1,0:T(8,128)S(1)}, f32[2,2,24,16,256]{4,3,2,1,0:T(8,128)}, u32[]{:S(2)}) copy-start(f32[2,2,24,16,256]{4,3,2,1,0:T(8,128)} %param.6) | copy-start | bytes 4718596
  21.4 8.3 %collective-permute-start.4 = (f32[8,24,256]{2,1,0:T(8,128)S(1)}, f32[8,24,256]{2,1,0:T(8,128)S(1)}, u32[]{:S(2)}, u32[]{:S(2)}) collective-permute-start(f32[8,24,256]{2,1,0:T(8,128)S(1)} %get-tuple-element.38.near_w), channel_id=1, source_target_pairs={{0,1},{1,0},{2,3},{3,2},{4,5},{5,4},{6,7},{7,6},{8,9},{9,8},{10,11... | collective-permute-start | bytes 589832 | tf_op jit(solution)/shard_map/ppermute | solution.py:711
  24.3 7.0 %collective-permute-start.5 = (f32[8,24,256]{2,1,0:T(8,128)S(1)}, f32[8,24,256]{2,1,0:T(8,128)S(1)}, u32[]{:S(2)}, u32[]{:S(2)}) collective-permute-start(f32[8,24,256]{2,1,0:T(8,128)S(1)} %get-tuple-element.39.far_w), channel_id=1, source_target_pairs={{0,15},{1,2},{2,1},{3,4},{4,3},{5,6},{6,5},{7,8},{8,7},{9,10},{10,... | collective-permute-start | bytes 589832 | tf_op jit(solution)/shard_map/ppermute | solution.py:711
